TPU v7x, 32 devices: a whole 2x2x4 slice. The times are simulated.
32 devices in a mesh: dp: 2 (over x), blk: 16 (over z, y, core).
Axes of the slice: x: 2, y: 2, z: 4, core: 2. Of those that a mesh axis runs over, the one named last changes fastest.
Arguments:
- tokens: bfloat16 [2, 16, 128, 1024], P('dp', 'blk'), may hold values from -6 to 6
- cotangent: bfloat16 [2, 16, 128, 1024], P('dp', 'blk'), may hold values from -6 to 6
- lengths: int32 [2, 2], P('dp'), may hold values from 1 to 1536, as said below
- w_query: bfloat16 [1024, 1024], replicated, may hold values from -0.1875 to 0.1875
- w_key: bfloat16 [1024, 1024], replicated, may hold values from -0.1875 to 0.1875
- w_value: bfloat16 [1024, 1024], replicated, may hold values from -0.1875 to 0.1875
- w_out: bfloat16 [1024, 1024], replicated, may hold values from -0.1875 to 0.1875
- w_up: bfloat16 [1024, 4096], replicated, may hold values from -0.1875 to 0.1875
- w_gate: bfloat16 [1024, 4096], replicated, may hold values from -0.1875 to 0.1875
- w_down: bfloat16 [4096, 1024], replicated, may hold values from -0.09375 to 0.09375
- s_qk: float32 [1024], replicated, may hold values from 0.8 to 1.6
- s_up: float32 [4096], replicated, may hold values from 0.5 to 2
- s_gate: float32 [4096], replicated, may hold values from 0.5 to 2
- alpha_attn: float32 [1024], replicated, may hold values from 0.1 to 0.8
- alpha_mlp: float32 [1024], replicated, may hold values from 0.1 to 0.8
Outputs:
- output: bfloat16 [2, 16, 128, 1024], P('dp', 'blk')
- input_grad: float32 [2, 16, 128, 1024], P('dp', 'blk')
- grad_query: float32 [1024, 1024], P(('dp', 'blk'))
- grad_key: float32 [1024, 1024], P(('dp', 'blk'))
- grad_value: float32 [1024, 1024], P(('dp', 'blk'))
- grad_out: float32 [1024, 1024], P(('dp', 'blk'))
- grad_up: float32 [1024, 4096], P(('dp', 'blk'))
- grad_gate: float32 [1024, 4096], P(('dp', 'blk'))
- grad_down: float32 [4096, 1024], P(('dp', 'blk'))
- grad_qk_scale: float32 [1024], P(('dp', 'blk'))
- grad_up_scale: float32 [4096], P(('dp', 'blk'))
- grad_gate_scale: float32 [4096], P(('dp', 'blk'))
- grad_alpha_attn: float32 [1024], P(('dp', 'blk'))
- grad_alpha_mlp: float32 [1024], P(('dp', 'blk'))
- mean_alpha: float32 [], replicated
Inputs may be any that keep to these rules, and one draw needn't show every extreme that they name: In each row the lengths sum to 2048, and the first or the last of them is more than half of that sum; in every draw some row's long document has the largest length.
All inputs are finite; a program needn't handle non-finite values.
Results may differ from a plain program's by a relative error of at most 0.025.
Values may be sent and summed in bfloat16 or wider, within the bound.
A program may use at most 640 MiB of HBM per device.

v0:
```python
import math

import jax
import jax.numpy as jnp
from jax import lax
from jax.sharding import PartitionSpec as P

HEAD_DIM = 64


def rms_norm(vector):
    return vector * lax.rsqrt(jnp.mean(vector * vector, axis=-1, keepdims=True) + 1e-06)


def head_norm(vector, head_count):
    shaped = vector.reshape(vector.shape[0], head_count, -1)
    return rms_norm(shaped).reshape(vector.shape)


def silu_smooth(vector):
    return vector / (1.0 + jnp.exp(-vector))


def residual_mix(inputs, branch, alphas):
    return rms_norm(inputs + alphas * (rms_norm(branch) - inputs))


def gated_inner(up_raw, gate_raw, s_up, s_gate):
    return up_raw * s_up * silu_smooth(gate_raw * s_gate)


def stream_positions(row_index, tok_rows, members):
    half_rows = tok_rows // 2
    device = row_index // tok_rows
    within = row_index % tok_rows
    block_id = jnp.where(within < half_rows, device, 2 * members - 1 - device)
    return block_id * half_rows + within % half_rows


def doc_index(positions, doc_ends):
    return jnp.sum(
        (positions[:, None] >= doc_ends[None, :]).astype(jnp.int32), axis=1, dtype=jnp.int32
    )


def allowed_pairs(query_pos, query_doc, key_pos, key_doc):
    return (key_pos[None, :] <= query_pos[:, None]) & (key_doc[None, :] == query_doc[:, None])


def take_rows(matrix, first_row, row_count):
    return lax.dynamic_slice_in_dim(matrix, first_row, row_count, 0)


def fold_half(running, query_heads, key_heads, value_heads, allowed, score_scale):

    def absorb(carried):
        best_score, total_sum, accumulated = carried
        scores = (
            jnp.einsum("qhd,khd->hqk", query_heads, key_heads, preferred_element_type=jnp.float32)
            * score_scale
        )
        scores = jnp.where(allowed[None], scores, -1e30)
        new_best = jnp.maximum(best_score, jnp.max(scores, axis=2))
        weights = jnp.where(allowed[None], jnp.exp(scores - new_best[:, :, None]), 0.0)
        fade_factor = jnp.exp(best_score - new_best)
        total_sum = jnp.sum(weights, axis=2)
        accumulated = accumulated * fade_factor.T[:, :, None] + jnp.einsum(
            "hqk,khd->qhd",
            weights.astype(jnp.bfloat16),
            value_heads,
            preferred_element_type=jnp.float32,
        )
        return (new_best, total_sum, accumulated)

    return lax.cond(jnp.any(allowed), absorb, lambda carried: carried, running)


def pair_terms(query_side, key_heads, value_heads, allowed, score_scale):
    query_heads, grad_heads, log_total, delta_rows = (
        query_side[0],
        query_side[1],
        query_side[2],
        query_side[3],
    )
    scores = (
        jnp.einsum("qhd,khd->hqk", query_heads, key_heads, preferred_element_type=jnp.float32)
        * score_scale
    )
    scores = jnp.where(allowed[None], scores, -1e30)
    weights = jnp.exp(scores - log_total[:, :, None])
    grad_weights = jnp.einsum(
        "qhd,khd->hqk", grad_heads, value_heads, preferred_element_type=jnp.float32
    )
    grad_scores = (weights * (grad_weights - delta_rows[:, :, None])).astype(jnp.bfloat16)
    return (weights.astype(jnp.bfloat16), grad_scores)


def query_term(query_side, key_heads, value_heads, allowed, score_scale):
    weights, grad_scores = pair_terms(query_side, key_heads, value_heads, allowed, score_scale)
    return score_scale * jnp.einsum(
        "hqk,khd->qhd", grad_scores, key_heads, preferred_element_type=jnp.float32
    )


def key_term(query_side, key_heads, value_heads, allowed, score_scale):
    weights, grad_scores = pair_terms(query_side, key_heads, value_heads, allowed, score_scale)
    grad_keys = score_scale * jnp.einsum(
        "hqk,qhd->khd", grad_scores, query_side[0], preferred_element_type=jnp.float32
    )
    grad_values = jnp.einsum(
        "hqk,qhd->khd", weights, query_side[1], preferred_element_type=jnp.float32
    )
    return (grad_keys, grad_values)


def on_device(
    tokens,
    cotangent,
    lengths,
    w_query,
    w_key,
    w_value,
    w_out,
    w_up,
    w_gate,
    w_down,
    s_qk,
    s_up,
    s_gate,
    alpha_attn,
    alpha_mlp,
):
    model_width = w_query.shape[0]
    head_count = model_width // HEAD_DIM
    score_scale = 1.0 / math.sqrt(HEAD_DIM)
    tok_rows = tokens.shape[2]
    half_rows = tok_rows // 2
    members = lax.axis_size("blk")
    position = lax.axis_index("blk")
    doc_ends = jnp.cumsum(lengths[0], dtype=jnp.int32)
    hidden = tokens[0, 0]
    hidden_f = hidden.astype(jnp.float32)

    def key_info(first_row, row_count):
        key_pos = stream_positions(
            first_row + jnp.arange(row_count, dtype=jnp.int32), tok_rows, members
        )
        return (key_pos, doc_index(key_pos, doc_ends))

    def heads_of(matrix):
        return matrix.reshape(matrix.shape[0], head_count, HEAD_DIM)

    def scaled_norm(raw_rows, gain_vector):
        return head_norm(raw_rows, head_count) * gain_vector

    own_pos, own_doc = key_info(position * tok_rows, tok_rows)
    query_raw = jnp.dot(hidden, w_query, preferred_element_type=jnp.float32)
    key_raw = jnp.dot(hidden, w_key, preferred_element_type=jnp.float32)
    value_raw = jnp.dot(hidden, w_value, preferred_element_type=jnp.float32)
    queries = scaled_norm(query_raw, s_qk).astype(jnp.bfloat16)
    key_rows = scaled_norm(key_raw, s_qk).astype(jnp.bfloat16)
    value_rows = value_raw.astype(jnp.bfloat16)
    query_heads = heads_of(queries)

    def empty_state():
        return (
            jnp.full((head_count, half_rows), -1e30, jnp.float32),
            jnp.zeros((head_count, half_rows), jnp.float32),
            jnp.zeros((half_rows, head_count, HEAD_DIM), jnp.float32),
        )

    running = (empty_state(), empty_state())
    key_part = lax.all_gather(key_rows, "blk", axis=0, tiled=True)
    value_part = lax.all_gather(value_rows, "blk", axis=0, tiled=True)
    key_pos, key_doc = key_info(jnp.int32(0), key_part.shape[0])
    updated = []
    for part_index in range(2):
        rows_here = slice(part_index * half_rows, (part_index + 1) * half_rows)
        allowed = allowed_pairs(own_pos[rows_here], own_doc[rows_here], key_pos, key_doc)
        updated.append(
            fold_half(
                running[part_index],
                query_heads[rows_here],
                heads_of(key_part),
                heads_of(value_part),
                allowed,
                score_scale,
            )
        )
    folded = (updated[0], updated[1])
    best_score = jnp.concatenate([folded[0][0], folded[1][0]], axis=1)
    total_sum = jnp.concatenate([folded[0][1], folded[1][1]], axis=1)
    accumulated = jnp.concatenate([folded[0][2], folded[1][2]], axis=0)
    attended = accumulated / total_sum.T[:, :, None]
    log_total = best_score + jnp.log(total_sum)
    attended_low = attended.reshape(tok_rows, model_width).astype(jnp.bfloat16)
    branch = jnp.dot(attended_low, w_out, preferred_element_type=jnp.float32)
    middle = residual_mix(hidden_f, branch, alpha_attn)
    middle_low = middle.astype(jnp.bfloat16)
    up_raw = jnp.dot(middle_low, w_up, preferred_element_type=jnp.float32)
    gate_raw = jnp.dot(middle_low, w_gate, preferred_element_type=jnp.float32)
    inner_low = gated_inner(up_raw, gate_raw, s_up, s_gate).astype(jnp.bfloat16)
    mlp_raw = jnp.dot(inner_low, w_down, preferred_element_type=jnp.float32)
    result = residual_mix(middle, mlp_raw, alpha_mlp)
    mixed_out, pull_out = jax.vjp(residual_mix, middle, mlp_raw, alpha_mlp)
    grad_middle, grad_mlp, grad_alpha_mlp = pull_out(cotangent[0, 0].astype(jnp.float32))
    grad_mlp_low = grad_mlp.astype(jnp.bfloat16)
    grad_w_down = jnp.dot(inner_low.T, grad_mlp_low, preferred_element_type=jnp.float32)
    grad_inner = jnp.dot(grad_mlp_low, w_down.T, preferred_element_type=jnp.float32)
    inner_out, pull_inner = jax.vjp(gated_inner, up_raw, gate_raw, s_up, s_gate)
    grad_up_raw, grad_gate_raw, grad_s_up, grad_s_gate = pull_inner(grad_inner)
    up_low = grad_up_raw.astype(jnp.bfloat16)
    gate_low = grad_gate_raw.astype(jnp.bfloat16)
    grad_w_up = jnp.dot(middle_low.T, up_low, preferred_element_type=jnp.float32)
    grad_w_gate = jnp.dot(middle_low.T, gate_low, preferred_element_type=jnp.float32)
    grad_middle = (
        grad_middle
        + jnp.dot(up_low, w_up.T, preferred_element_type=jnp.float32)
        + jnp.dot(gate_low, w_gate.T, preferred_element_type=jnp.float32)
    )
    attn_out, pull_attn = jax.vjp(residual_mix, hidden_f, branch, alpha_attn)
    grad_hidden, grad_branch, grad_alpha_attn = pull_attn(grad_middle)
    branch_low = grad_branch.astype(jnp.bfloat16)
    grad_w_out = jnp.dot(attended_low.T, branch_low, preferred_element_type=jnp.float32)
    grad_att_low = jnp.dot(branch_low, w_out.T, preferred_element_type=jnp.float32).astype(
        jnp.bfloat16
    )
    grad_heads = heads_of(grad_att_low)
    delta_rows = jnp.sum(grad_heads.astype(jnp.float32) * attended, axis=2).T

    def local_side(part_index):
        rows_here = slice(part_index * half_rows, (part_index + 1) * half_rows)
        return (
            query_heads[rows_here],
            grad_heads[rows_here],
            log_total[:, rows_here],
            delta_rows[:, rows_here],
            own_pos[rows_here],
            own_doc[rows_here],
        )

    local_parts = (local_side(0), local_side(1))
    whole_keys, whole_values = (
        lax.all_gather(key_rows, "blk", axis=0, tiled=True),
        lax.all_gather(value_rows, "blk", axis=0, tiled=True),
    )

    def query_step(grad_parts, shard_index):
        first_row = shard_index * tok_rows
        key_part = heads_of(take_rows(whole_keys, first_row, tok_rows))
        value_part = heads_of(take_rows(whole_values, first_row, tok_rows))
        key_pos, key_doc = key_info(first_row, tok_rows)
        updated = []
        for part_index in range(2):
            query_side = local_parts[part_index]
            allowed = allowed_pairs(query_side[4], query_side[5], key_pos, key_doc)

            def add_term(grad_now):
                return grad_now + query_term(query_side, key_part, value_part, allowed, score_scale)

            updated.append(
                lax.cond(
                    jnp.any(allowed), add_term, lambda grad_now: grad_now, grad_parts[part_index]
                )
            )
        return ((updated[0], updated[1]), None)

    zero_part = jnp.zeros((half_rows, head_count, HEAD_DIM), jnp.float32)
    grad_parts, unused_out = lax.scan(
        query_step, (zero_part, zero_part), jnp.arange(members, dtype=jnp.int32)
    )
    grad_queries = jnp.concatenate(grad_parts, axis=0).reshape(tok_rows, model_width)
    first_row = jnp.int32(0)
    row_count = lax.axis_size("blk") * tok_rows
    key_part = heads_of(take_rows(whole_keys, first_row, row_count))
    value_part = heads_of(take_rows(whole_values, first_row, row_count))
    key_pos, key_doc = key_info(first_row, row_count)
    zero_keys = jnp.zeros((row_count, head_count, HEAD_DIM), jnp.float32)
    totals = (zero_keys, zero_keys)
    for part_index in range(2):
        query_side = local_parts[part_index]
        allowed = allowed_pairs(query_side[4], query_side[5], key_pos, key_doc)

        def add_terms(grad_now):
            grad_keys, grad_values = key_term(
                query_side, key_part, value_part, allowed, score_scale
            )
            return (grad_now[0] + grad_keys, grad_now[1] + grad_values)

        totals = lax.cond(jnp.any(allowed), add_terms, lambda grad_now: grad_now, totals)
    key_value_grads = lax.psum_scatter(
        jnp.concatenate(
            [totals[0].reshape(row_count, model_width), totals[1].reshape(row_count, model_width)],
            axis=1,
        ),
        "blk",
        scatter_dimension=0,
        tiled=True,
    )
    grad_keys = key_value_grads[:, :model_width]
    grad_values = key_value_grads[:, model_width:]
    query_out, pull_query = jax.vjp(scaled_norm, query_raw, s_qk)
    grad_query_raw, grad_qk_first = pull_query(grad_queries)
    key_out, pull_key = jax.vjp(scaled_norm, key_raw, s_qk)
    grad_key_raw, grad_qk_second = pull_key(grad_keys)
    grad_s_qk = grad_qk_first + grad_qk_second
    query_low = grad_query_raw.astype(jnp.bfloat16)
    key_low = grad_key_raw.astype(jnp.bfloat16)
    value_low = grad_values.astype(jnp.bfloat16)
    grad_w_query = jnp.dot(hidden.T, query_low, preferred_element_type=jnp.float32)
    grad_w_key = jnp.dot(hidden.T, key_low, preferred_element_type=jnp.float32)
    grad_w_value = jnp.dot(hidden.T, value_low, preferred_element_type=jnp.float32)
    input_grad = (
        grad_hidden
        + jnp.dot(query_low, w_query.T, preferred_element_type=jnp.float32)
        + jnp.dot(key_low, w_key.T, preferred_element_type=jnp.float32)
        + jnp.dot(value_low, w_value.T, preferred_element_type=jnp.float32)
    )
    summed = (
        lax.psum_scatter(grad_w_query, ("dp", "blk"), scatter_dimension=0, tiled=True),
        lax.psum_scatter(grad_w_key, ("dp", "blk"), scatter_dimension=0, tiled=True),
        lax.psum_scatter(grad_w_value, ("dp", "blk"), scatter_dimension=0, tiled=True),
        lax.psum_scatter(grad_w_out, ("dp", "blk"), scatter_dimension=0, tiled=True),
        lax.psum_scatter(grad_w_up, ("dp", "blk"), scatter_dimension=0, tiled=True),
        lax.psum_scatter(grad_w_gate, ("dp", "blk"), scatter_dimension=0, tiled=True),
        lax.psum_scatter(grad_w_down, ("dp", "blk"), scatter_dimension=0, tiled=True),
        lax.psum_scatter(grad_s_qk, ("dp", "blk"), scatter_dimension=0, tiled=True),
        lax.psum_scatter(grad_s_up, ("dp", "blk"), scatter_dimension=0, tiled=True),
        lax.psum_scatter(grad_s_gate, ("dp", "blk"), scatter_dimension=0, tiled=True),
        lax.psum_scatter(grad_alpha_attn, ("dp", "blk"), scatter_dimension=0, tiled=True),
        lax.psum_scatter(grad_alpha_mlp, ("dp", "blk"), scatter_dimension=0, tiled=True),
    )
    mean_alpha = 0.5 * (jnp.mean(alpha_attn) + jnp.mean(alpha_mlp))
    output = result.astype(jnp.bfloat16)[None, None]
    return (
        output,
        input_grad[None, None],
        summed[0],
        summed[1],
        summed[2],
        summed[3],
        summed[4],
        summed[5],
        summed[6],
        summed[7],
        summed[8],
        summed[9],
        summed[10],
        summed[11],
        mean_alpha,
    )


def solution(mesh):
    in_specs = (
        P("dp", "blk", None, None),
        P("dp", "blk", None, None),
        P("dp", None),
        P(),
        P(),
        P(),
        P(),
        P(),
        P(),
        P(),
        P(),
        P(),
        P(),
        P(),
        P(),
    )
    out_specs = (
        P("dp", "blk", None, None),
        P("dp", "blk", None, None),
        P(("dp", "blk"), None),
        P(("dp", "blk"), None),
        P(("dp", "blk"), None),
        P(("dp", "blk"), None),
        P(("dp", "blk"), None),
        P(("dp", "blk"), None),
        P(("dp", "blk"), None),
        P(("dp", "blk")),
        P(("dp", "blk")),
        P(("dp", "blk")),
        P(("dp", "blk")),
        P(("dp", "blk")),
        P(),
    )
    return jax.shard_map(
        on_device, mesh=mesh, in_specs=in_specs, out_specs=out_specs, check_vma=False
    )
```

profile of v0, /device:TPU:0, one launch (start us, length us, event | category | flops | bytes accessed | tf_op | source)
XLA Modules:
  0.0 1571.5 jit_solution(5257460091455004723)
XLA Ops:
  31.3 32.8 %all-gather.5.cloned.1.call-done = bf16[2048,1024]{1,0:T(8,128)(2,1)} async-done(((bf16[128,1024]{1,0:T(8,128)(2,1)}), bf16[2048,1024]{1,0:T(8,128)(2,1)}) %all-gather.5.cloned.1.call-update) | async-done | bytes 4194320 | tf_op jit(solution)/shard_map/all_gather | solution.py:174
  64.1 6.6 copy.113
  70.6 47.9 %all-gather.3.cloned.1.call-done = bf16[2048,1024]{0,1:T(8,128)(2,1)} async-done(((bf16[128,1024]{0,1:T(8,128)(2,1)}), bf16[2048,1024]{0,1:T(8,128)(2,1)}) %all-gather.3.cloned.1.call-update) | async-done | bytes 4194320 | tf_op jit(solution)/shard_map/all_gather | solution.py:173
  118.5 16.5 %conditional.6 = (f32[16,64]{1,0:T(8,128)}, f32[16,64]{1,0:T(8,128)S(1)}, f32[64,16,64]{0,2,1:T(8,128)}, f32[64,1024]{0,1:T(8,128)}) conditional(s32[]{:T(128)} %convert_element_type.129, () %tuple.87, (pred[64,2048]{1,0:T(8,128)(4,1)S(1)}, bf16[64,16,64]{0,2,1:T(8,128)(2,1)}, bf16[2048,16,64]{0,2,1:T(8,128)(2,1)}, ...), branch_computations={%region_6.7_spmd, %region_7.10_spmd} | conditional | flops 564200448 | bytes 52199484 | solution.py:75
  135.6 14.2 conditional.7
  166.5 7.7 multiply_reduce_fusion
  174.2 6.7 convolution_add_fusion.4
  189.3 29.0 %conditional.8 = (f32[2048,16,64]{0,2,1:T(8,128)}, f32[2048,16,64]{0,2,1:T(8,128)}) conditional(s32[]{:T(128)} %convert_element_type.129, () %tuple.92, (pred[64,2048]{1,0:T(8,128)(4,1)}, bf16[64,16,64]{0,2,1:T(8,128)(2,1)}, bf16[2048,16,64]{0,2,1:T(8,128)(2,1)}, f32[16,64]{1,0:T(8,128)S(1)}, bf16[64,16,64]{2,1,0:T(8,128)(2,1)S(1)}, ...), branch_computations={%region_34.35_spmd, %region_35.36_spmd} | conditional | flops 1096810496 | bytes 51916844 | solution.py:290
  189.6 6.9 fusion.123
  196.5 12.2 multiply_bitcast_fusion.2
  208.7 9.3 convolution_bitcast_fusion
  218.6 30.5 %conditional.9 = (f32[2048,1024]{0,1:T(8,128)}, f32[2048,1024]{0,1:T(8,128)}) conditional(s32[]{:T(128)} %convert_element_type.133, (f32[2048,16,64]{0,2,1:T(8,128)}, f32[2048,16,64]{0,2,1:T(8,128)}) %conditional.8, (pred[64,2048]{1,0:T(8,128)(4,1)S(1)}, bf16[64,16,64]{0,2,1:T(8,128)(2,1)S(1)}, bf16[2048,16,64]{0,2,1:T(8,128)(2,1)}, ...), branch_computations={%region_36.37_spmd, %region_37.38_spmd} | conditional | flops 1101004800 | bytes 68169744 | solution.py:290
  218.9 6.8 fusion.124
  225.6 11.3 bitcast_add_fusion.1
  236.9 12.1 bitcast_add_fusion
  249.0 11.7 pad_maximum_fusion
  267.3 87.8 %while.21 = (s32[]{:T(128)}, f32[64,16,64]{2,0,1:T(8,128)S(1)}, f32[64,16,64]{2,0,1:T(8,128)S(1)}, s32[16]{0:T(128)S(1)}, s32[64]{0:T(128)S(1)}, /*index=5*/s32[...) while((s32[]{:T(128)}, f32[64,16,64]{2,0,1:T(8,128)S(1)}, ...), condition=%wide.region_32.33_spmd, body=%wide.region_24.32_spmd.sunk | while | flops 102569088 | bytes 6344635 | solution.py:269
  360.2 5.5 copy.139
  366.0 8.1 fusion.81
  375.4 8.1 fusion.127
  384.8 8.1 fusion.128
  392.9 44.8 %reduce-scatter.15.cloned.1.call-done = f32[128,2048]{0,1:T(8,128)} async-done(((f32[2048,2048]{0,1:T(8,128)}), f32[128,2048]{0,1:T(8,128)}) %reduce-scatter.15.cloned.1.call-update) | async-done | bytes 1048592 | tf_op jit(solution)/shard_map/reduce_scatter | solution.py:291
  441.5 5.4 copy.143
  450.8 5.6 copy.141
  463.6 40.1 %all-reduce.5 = (f32[1024]{0:T(1024)S(1)}, f32[4096]{0:T(1024)S(1)}, f32[4096]{0:T(1024)S(1)}, f32[1024]{0:T(1024)S(1)}, f32[1024]{0:T(1024)S(1)}) all-reduce(f32[1024]{0:T(1024)S(1)} %add.379, f32[4096]{0:T(1024)S(1)} %copy-done.68, f32[4096]{0:T(1024)S(1)} %copy-done.67, ...), channel_id=10, replica_groups=mesh['dp'=2,'blk'=16] {'dp','blk'}, use_global_device_ids=true, to_apply=%region_49.50.clone | all-reduce | flops 11264 | bytes 90112
  512.6 68.3 %reduce-scatter.17.cloned.1.call-done = f32[32,1024]{1,0:T(8,128)} async-done(((f32[1024,1024]{1,0:T(8,128)}), f32[32,1024]{1,0:T(8,128)}) %reduce-scatter.17.cloned.1.call-update) | async-done | bytes 131088 | tf_op jit(solution)/shard_map/reduce_scatter | solution.py:323
  580.9 140.1 %reduce-scatter.25.cloned.1.call-done = f32[32,1024]{1,0:T(8,128)} async-done(((f32[1024,1024]{1,0:T(8,128)}), f32[32,1024]{1,0:T(8,128)}) %reduce-scatter.25.cloned.1.call-update) | async-done | bytes 131088
  721.0 182.5 %reduce-scatter.21.cloned.1.call-done = f32[32,4096]{1,0:T(8,128)} async-done(((f32[1024,4096]{1,0:T(8,128)}), f32[32,4096]{1,0:T(8,128)}) %reduce-scatter.21.cloned.1.call-update) | async-done | bytes 524304 | tf_op jit(solution)/shard_map/reduce_scatter | solution.py:325
  903.5 187.5 %reduce-scatter.19.cloned.1.call-done = f32[32,4096]{1,0:T(8,128)} async-done(((f32[1024,4096]{1,0:T(8,128)}), f32[32,4096]{1,0:T(8,128)}) %reduce-scatter.19.cloned.1.call-update) | async-done | bytes 524304 | tf_op jit(solution)/shard_map/reduce_scatter | solution.py:324
  1091.0 187.5 %reduce-scatter.23.cloned.1.call-done = f32[128,1024]{1,0:T(8,128)} async-done(((f32[4096,1024]{1,0:T(8,128)}), f32[128,1024]{1,0:T(8,128)}) %reduce-scatter.23.cloned.1.call-update) | async-done | bytes 524304 | tf_op jit(solution)/shard_map/reduce_scatter | solution.py:326
  1278.5 144.6 %reduce-scatter.29.cloned.1.call-done = f32[32,1024]{1,0:T(8,128)} async-done(((f32[1024,1024]{1,0:T(8,128)}), f32[32,1024]{1,0:T(8,128)}) %reduce-scatter.29.cloned.1.call-update) | async-done | bytes 131088
  1423.1 140.2 %reduce-scatter.27.cloned.1.call-done = f32[32,1024]{1,0:T(8,128)} async-done(((f32[1024,1024]{1,0:T(8,128)}), f32[32,1024]{1,0:T(8,128)}) %reduce-scatter.27.cloned.1.call-update) | async-done | bytes 131088
  (404 shorter events, 185.8 us)
Async XLA Ops:
  7.2 145.9 %copy-start = (bf16[1024,1024]{1,0:T(8,128)(2,1)S(1)}, bf16[1024,1024]{1,0:T(8,128)(2,1)}, u32[]{:S(2)}) copy-start(bf16[1024,1024]{1,0:T(8,128)(2,1)} %param.35) | copy-start | bytes 6291460
  7.2 11.1 copy-start.4
  7.2 56.9 %all-gather.5.cloned.1.call-start = ((), (), s32[]{:S(2)}) async-start(), calls=%async_computation.9 | async-start | bytes 4456448 | tf_op jit(solution)/shard_map/all_gather | solution.py:174
  10.2 14.5 copy-start.53
  10.3 15.5 copy-start.72
  10.3 108.3 %all-gather.3.cloned.1.call-start = ((), (), s32[]{:S(2)}) async-start(), calls=%async_computation.8 | async-start | bytes 4456448 | tf_op jit(solution)/shard_map/all_gather | solution.py:173
  25.8 411.9 %reduce-scatter.15.cloned.1.call-start = ((), (), s32[]{:S(2)}) async-start(), calls=%async_computation.10 | async-start | bytes 17825792 | tf_op jit(solution)/shard_map/reduce_scatter | solution.py:291
  29.4 89.1 %copy-start.24 = (pred[64,2048]{1,0:T(8,128)(4,1)S(1)}, pred[64,2048]{1,0:T(8,128)(4,1)}, u32[]{:S(2)}) copy-start(pred[64,2048]{1,0:T(8,128)(4,1)} %get-tuple-element.806) | copy-start | bytes 393220
  31.3 103.7 %copy-start.11 = (bf16[64,1024]{0,1:T(8,128)(2,1)}, bf16[64,1024]{0,1:T(8,128)(2,1)S(1)}, u32[]{:S(2)}) copy-start(bf16[64,1024]{0,1:T(8,128)(2,1)S(1)} %get-tuple-element.823) | copy-start | bytes 393220
  135.0 18.6 %copy-start.37 = (f32[1024]{0:T(1024)S(1)}, f32[1024]{0:T(1024)}, u32[]{:S(2)}) copy-start(f32[1024]{0:T(1024)} %param.42) | copy-start | bytes 12292
  164.5 16.5 %slice-start = ((s8[8388608]{0:T(1024)(128)(4,1)}), s8[4194304]{0:T(1024)(128)(4,1)S(1)}, s32[]{:S(2)}) async-start(s8[8388608]{0:T(1024)(128)(4,1)} %bitcast.187), calls=%async_computation.18 | async-start | bytes 8388608
  166.5 14.5 slice-start.1
  187.6 30.9 %copy-start.41 = (f32[16,64]{1,0:T(8,128)}, f32[16,64]{1,0:T(8,128)S(1)}, u32[]{:S(2)}) copy-start(f32[16,64]{1,0:T(8,128)S(1)} %get-tuple-element.1081) | copy-start | bytes 12292
  189.3 29.2 %copy-start.12 = (bf16[64,1024]{0,1:T(8,128)(2,1)S(1)}, bf16[64,1024]{0,1:T(8,128)(2,1)}, u32[]{:S(2)}) copy-start(bf16[64,1024]{0,1:T(8,128)(2,1)} %copy-done.11) | copy-start | bytes 393220
  260.9 320.0 %reduce-scatter.17.cloned.1.call-start = ((), (), s32[]{:S(2)}) async-start(), calls=%async_computation.11 | async-start | bytes 4325376 | tf_op jit(solution)/shard_map/reduce_scatter | solution.py:323
  267.1 454.0 %reduce-scatter.25.cloned.1.call-start = ((), (), s32[]{:S(2)}) async-start(), calls=%async_computation.15 | async-start | bytes 4325376
  267.3 89.8 %copy-start.48 = (f32[128,16]{0,1:T(8,128)S(1)}, f32[128,16]{0,1:T(8,128)}, u32[]{:S(2)}) copy-start(f32[128,16]{0,1:T(8,128)} %copy-done.47) | copy-start | bytes 24580
  267.3 89.8 %copy-start.40 = (f32[128,16]{0,1:T(8,128)S(1)}, f32[128,16]{0,1:T(8,128)}, u32[]{:S(2)}) copy-start(f32[128,16]{0,1:T(8,128)} %copy-done.39) | copy-start | bytes 24580
  365.8 537.8 %reduce-scatter.21.cloned.1.call-start = ((), (), s32[]{:S(2)}) async-start(), calls=%async_computation.13 | async-start | bytes 17301504 | tf_op jit(solution)/shard_map/reduce_scatter | solution.py:325
  374.1 716.9 %reduce-scatter.19.cloned.1.call-start = ((), (), s32[]{:S(2)}) async-start(), calls=%async_computation.12 | async-start | bytes 17301504 | tf_op jit(solution)/shard_map/reduce_scatter | solution.py:324
  383.5 895.0 %reduce-scatter.23.cloned.1.call-start = ((), (), s32[]{:S(2)}) async-start(), calls=%async_computation.14 | async-start | bytes 17301504 | tf_op jit(solution)/shard_map/reduce_scatter | solution.py:326
  392.9 54.1 %copy-start.6 = (f32[128,16,64]{0,2,1:T(8,128)S(1)}, f32[128,16,64]{0,2,1:T(8,128)}, u32[]{:S(2)}) copy-start(f32[128,16,64]{0,2,1:T(8,128)} %copy-done.5) | copy-start | bytes 1572868
  392.9 54.3 %copy-start.46 = (f32[128,16]{0,1:T(8,128)S(1)}, f32[128,16]{0,1:T(8,128)}, u32[]{:S(2)}) copy-start(f32[128,16]{0,1:T(8,128)} %copy-done.45) | copy-start | bytes 24580
  392.9 54.4 %copy-start.50 = (f32[128,16]{0,1:T(8,128)S(1)}, f32[128,16]{0,1:T(8,128)}, u32[]{:S(2)}) copy-start(f32[128,16]{0,1:T(8,128)} %copy-done.49) | copy-start | bytes 24580
  392.9 1030.2 %reduce-scatter.29.cloned.1.call-start = ((), (), s32[]{:S(2)}) async-start(), calls=%async_computation.17 | async-start | bytes 4325376
  446.9 1116.4 %reduce-scatter.27.cloned.1.call-start = ((), (), s32[]{:S(2)}) async-start(), calls=%async_computation.16 | async-start | bytes 4325376
  450.7 11.5 copy-start.16
  450.8 12.8 copy-start.65
  450.8 12.8 copy-start.66
  450.8 12.8 copy-start.67
  450.8 12.8 copy-start.68
  450.8 1112.5 %copy-start.1 = (bf16[1024,1024]{1,0:T(8,128)(2,1)S(1)}, bf16[1024,1024]{1,0:T(8,128)(2,1)}, u32[]{:S(2)}) copy-start(bf16[1024,1024]{1,0:T(8,128)(2,1)} %param.35) | copy-start | bytes 6291460
  (57 other events, 255.0 us)
Sparse Core Ops, SparseCore 0:
  10.8 53.2 all-gather.4
  66.8 51.6 all-gather.2
  260.9 176.7 reduce-scatter.14
  440.4 140.4 reduce-scatter.16
  583.6 137.4 reduce-scatter.24
  723.7 179.7 reduce-scatter.20
  906.4 184.5 reduce-scatter.18
  1093.9 184.5 reduce-scatter.22
  1281.4 141.6 reduce-scatter.28
  1425.8 137.4 reduce-scatter.26
where the time goes:
time: 1580 us; the launch traced here: 1570 us
  waiting for transfers between devices  1180 us (75%)
  matrix products  171 us (11%)
  local copies, waits for them, and re-layouts  81.9 us (5%)
  other arithmetic  48.9 us (3%)
  blocking collectives  40.1 us (3%)
  loops' own time  33.6 us (2%)
  between operations  19.1 us (1%)
    unnamed x13, waiting for transfers between devices  425 us
    reduce_scatter x1, waiting for transfers between devices, on_device(): lax.psum_scatter(grad_w_down, ('dp', 'blk'), scatter_dimension=0, tiled=T...  187 us
    reduce_scatter x1, waiting for transfers between devices, on_device(): lax.psum_scatter(grad_w_up, ('dp', 'blk'), scatter_dimension=0, tiled=True)  187 us
    reduce_scatter x1, waiting for transfers between devices, on_device(): lax.psum_scatter(grad_w_gate, ('dp', 'blk'), scatter_dimension=0, tiled=T...  183 us
    reduce_scatter x1, waiting for transfers between devices, on_device(): lax.psum_scatter(grad_w_out, ('dp', 'blk'), scatter_dimension=0, tiled=True)  68.3 us
    all_gather x1, waiting for transfers between devices, on_device(): key_part = lax.all_gather(key_rows, 'blk', axis=0, tiled=True)  47.9 us
    reduce_scatter x1, waiting for transfers between devices, on_device(): lax.psum_scatter(jnp.concatenate([totals[0].reshape(row_count, model_widt...  44.8 us
    unnamed x1, blocking collectives  40.1 us
  transfers between devices with their start and end apart: 10, of which 10 were waited for; matrix products, arithmetic and copies ran while one was open for 10% of the time, Pallas kernels for 0%

commit v1 on v0

--- a/solution.py
+++ b/solution.py
@@ -1,8 +1,11 @@
+import functools
 import math
 
 import jax
 import jax.numpy as jnp
 from jax import lax
+from jax.experimental import pallas as pl
+from jax.experimental.pallas import tpu as pltpu
 from jax.sharding import PartitionSpec as P
 
 HEAD_DIM = 64
@@ -113,7 +116,7 @@
     return (grad_keys, grad_values)
 
 
-def on_device(
+def on_device_general(
     tokens,
     cotangent,
     lengths,
@@ -351,6 +354,631 @@
     )
 
 
+MESH = pl.DeviceIdType.MESH
+VMEM_SPEC = pl.BlockSpec(memory_space=pltpu.VMEM)
+VMEM_LIMIT = 56 << 20
+GROUP = 16
+
+
+def here():
+    return lax.axis_index("dp"), lax.axis_index("blk")
+
+
+def greet(partners):
+    barrier = pltpu.get_barrier_semaphore()
+    for partner in partners:
+        pl.semaphore_signal(barrier, inc=1, device_id=partner, device_id_type=MESH)
+    pl.semaphore_wait(barrier, len(partners))
+
+
+def remote(src, dst, send_sem, recv_sem, device):
+    return pltpu.make_async_remote_copy(
+        src_ref=src,
+        dst_ref=dst,
+        send_sem=send_sem,
+        recv_sem=recv_sem,
+        device_id=device,
+        device_id_type=MESH,
+    )
+
+
+class Gather:
+    CLASSES = 15
+
+    def __init__(self, own, out, send, recv):
+        self.own, self.out, self.send, self.recv = own, out, send, recv
+        dp, b = here()
+        self.z, self.y, self.c = b // 4, (b // 2) % 2, b % 2
+        self.up = (dp, self.block(1, 0))
+        self.down = (dp, self.block(3, 0))
+        self.side = (dp, self.block(0, 1))
+        self.sib = (dp, b + 1 - 2 * self.c)
+        self.b = b
+
+    def block(self, dz, dy):
+        return (((self.z + dz) % 4) * 2 + (self.y + dy) % 2) * 2 + self.c
+
+    def slot(self, block, half):
+        return 2 * GROUP - 1 - block if half else block
+
+    def copy(self, block, kind, half, device, own=False):
+        place = self.slot(block, half)
+        source = self.own.at[half] if own else self.out.at[place]
+        index = 2 * kind + half
+        return remote(source, self.out.at[place], self.send.at[index], self.recv.at[index], device)
+
+    def partners(self):
+        return [self.up, self.down, self.side, self.sib]
+
+    KINDS = {
+        0: (0, 1, (0, 1)),
+        1: (3, 0, (0, 1)),
+        2: (1, 0, (0, 1)),
+        3: (3, 1, (0, 1)),
+        4: (1, 1, (0, 1)),
+        5: (2, 0, (0, 1)),
+        6: (2, 1, (0, 1)),
+    }
+
+    def start(self):
+        for half in (0, 1):
+            self.copy(self.b, 1, half, self.up, True).start()
+            self.copy(self.b, 2, half, self.down, True).start()
+            self.copy(self.b, 0, half, self.side, True).start()
+        for half in (0, 1):
+            self.copy(self.b, 7, half, self.sib, True).start()
+        for half in (0, 1):
+            self.out[self.slot(self.b, half)] = self.own[half]
+
+    def arrive(self, kind):
+        dz, dy, halves = self.KINDS[kind]
+        block = self.block(dz, dy)
+        for half in halves:
+            self.copy(block, kind, half, self.sib).wait_recv()
+            if kind == 0:
+                self.copy(block, 3, half, self.up).start()
+                self.copy(block, 4, half, self.down).start()
+            if kind == 1 and half == 0:
+                self.copy(block, 5, half, self.up).start()
+            if kind == 2 and half == 1:
+                self.copy(block, 5, half, self.down).start()
+            if kind == 5:
+                self.copy(block, 6, half, self.side).start()
+            self.copy(block, 8 + kind, half, self.sib).start()
+
+    def first(self):
+        for kind in (0, 1, 2):
+            self.arrive(kind)
+
+    def second(self):
+        for kind in (5, 3, 4):
+            self.arrive(kind)
+
+    def last(self):
+        self.arrive(6)
+        for kind in range(7):
+            dz, dy, halves = self.KINDS[kind]
+            other = self.block(dz, dy) + 1 - 2 * self.c
+            for half in halves:
+                self.copy(other, 8 + kind, half, self.sib).wait_recv()
+        for half in (0, 1):
+            self.copy(self.b + 1 - 2 * self.c, 7, half, self.sib).wait_recv()
+        for kind in range(self.CLASSES):
+            for half in (0, 1):
+                self.copy(self.b, kind, half, self.sib).wait_send()
+
+
+def gather_kernel(own, out, send, recv):
+    gather = Gather(own, out, send, recv)
+    greet(gather.partners())
+    gather.start()
+    gather.first()
+    gather.second()
+    gather.last()
+
+
+def comm_params(collective_id):
+    return pltpu.CompilerParams(
+        collective_id=collective_id, has_side_effects=True, vmem_limit_bytes=VMEM_LIMIT
+    )
+
+
+def all_gather_group(rows, collective_id):
+    tok_rows, width = rows.shape
+    gathered = pl.pallas_call(
+        gather_kernel,
+        out_shape=jax.ShapeDtypeStruct((2 * GROUP, tok_rows // 2, width), rows.dtype),
+        in_specs=[VMEM_SPEC],
+        out_specs=VMEM_SPEC,
+        scratch_shapes=[
+            pltpu.SemaphoreType.DMA((2 * Gather.CLASSES,)),
+            pltpu.SemaphoreType.DMA((2 * Gather.CLASSES,)),
+        ],
+        compiler_params=comm_params(collective_id),
+        name="gather_group",
+    )(rows.reshape(2, tok_rows // 2, width))
+    return gathered.reshape(GROUP * tok_rows, width)
+
+
+def swap_group_kernel(blocks, out, send, recv):
+    dp, b = here()
+    greet([(dp, (b + step) % GROUP) for step in range(1, GROUP)])
+    copies = []
+    for step in range(1, GROUP):
+        target = (b + step) % GROUP
+        copies.append(
+            remote(blocks.at[target], out.at[b], send.at[step], recv.at[step], (dp, target))
+        )
+        copies[-1].start()
+    out[b] = blocks[b]
+    for copy in copies:
+        copy.wait()
+
+
+def swap_group(blocks, collective_id):
+    return pl.pallas_call(
+        swap_group_kernel,
+        out_shape=jax.ShapeDtypeStruct(blocks.shape, blocks.dtype),
+        in_specs=[VMEM_SPEC],
+        out_specs=VMEM_SPEC,
+        scratch_shapes=[
+            pltpu.SemaphoreType.DMA((GROUP,)),
+            pltpu.SemaphoreType.DMA((GROUP,)),
+        ],
+        compiler_params=comm_params(collective_id),
+        name="swap_group",
+    )(blocks)
+
+
+def swap_dp_kernel(count, *refs):
+    blocks, outs, send, recv = refs[:count], refs[count : 2 * count], refs[-2], refs[-1]
+    dp, b = here()
+    greet([(1 - dp, b)])
+    copies = [
+        remote(blocks[i], outs[i], send.at[i], recv.at[i], (1 - dp, b)) for i in range(count)
+    ]
+    for copy in copies:
+        copy.start()
+    for copy in copies:
+        copy.wait()
+
+
+def swap_dp(blocks, collective_id):
+    count = len(blocks)
+    return pl.pallas_call(
+        functools.partial(swap_dp_kernel, count),
+        out_shape=[jax.ShapeDtypeStruct(block.shape, block.dtype) for block in blocks],
+        in_specs=[VMEM_SPEC] * count,
+        out_specs=[VMEM_SPEC] * count,
+        scratch_shapes=[
+            pltpu.SemaphoreType.DMA((count,)),
+            pltpu.SemaphoreType.DMA((count,)),
+        ],
+        compiler_params=comm_params(collective_id),
+        name="swap_dp",
+    )(*blocks)
+
+
+def swap_all_kernel(blocks, out, send, recv):
+    dp, b = here()
+    me = dp * GROUP + b
+    total = 2 * GROUP
+    targets = [(me + step) % total for step in range(1, total)]
+    greet([(target // GROUP, target % GROUP) for target in targets])
+    copies = []
+    for step, target in enumerate(targets):
+        copies.append(
+            remote(
+                blocks.at[target],
+                out.at[me],
+                send.at[step],
+                recv.at[step],
+                (target // GROUP, target % GROUP),
+            )
+        )
+        copies[-1].start()
+    out[me] = blocks[me]
+    for copy in copies:
+        copy.wait()
+
+
+def swap_all(blocks, collective_id):
+    return pl.pallas_call(
+        swap_all_kernel,
+        out_shape=jax.ShapeDtypeStruct(blocks.shape, blocks.dtype),
+        in_specs=[VMEM_SPEC],
+        out_specs=VMEM_SPEC,
+        scratch_shapes=[
+            pltpu.SemaphoreType.DMA((2 * GROUP,)),
+            pltpu.SemaphoreType.DMA((2 * GROUP,)),
+        ],
+        compiler_params=comm_params(collective_id),
+        name="swap_all",
+    )(blocks)
+
+
+ATT = 256
+
+
+def dot_nt(left, right):
+    return lax.dot_general(left, right, (((1,), (1,)), ((), ())), preferred_element_type=jnp.float32)
+
+
+def dot_tn(left, right):
+    return lax.dot_general(left, right, (((0,), (0,)), ((), ())), preferred_element_type=jnp.float32)
+
+
+def dot_nn(left, right):
+    return jnp.dot(left, right, preferred_element_type=jnp.float32)
+
+
+def attend_kernel(first_ref, q_ref, k_ref, v_ref, start_ref, o_ref, l_ref):
+    length = q_ref.shape[0]
+    for query_block in range(length // ATT):
+        rows = pl.ds(query_block * ATT, ATT)
+        queries = q_ref[rows, :]
+        doc_start = start_ref[rows, :]
+        query_pos = query_block * ATT + lax.broadcasted_iota(jnp.int32, (ATT, ATT), 0)
+        key_lane = lax.broadcasted_iota(jnp.int32, (ATT, ATT), 1)
+
+        def step(key_block, total):
+            base = pl.multiple_of(key_block * ATT, ATT)
+            keys = k_ref[pl.ds(base, ATT), :]
+            values = v_ref[pl.ds(base, ATT), :]
+            key_pos = base + key_lane
+            allowed = (key_pos <= query_pos) & (key_pos >= doc_start)
+            weights = jnp.where(allowed, jnp.exp(dot_nt(queries, keys)), 0.0)
+            return total + dot_nn(weights.astype(jnp.bfloat16), values)
+
+        total = lax.fori_loop(
+            first_ref[query_block], query_block + 1, step, jnp.zeros((ATT, 128), jnp.float32)
+        )
+        row_sum = total[:, HEAD_DIM : HEAD_DIM + 1]
+        o_ref[rows, :] = total[:, :HEAD_DIM] / row_sum
+        l_ref[rows, :] = jnp.log(row_sum)
+
+
+def attend_grad_kernel(last_ref, q_ref, k_ref, v_ref, g_ref, start_ref, dq_ref, dk_ref, dv_ref):
+    length = q_ref.shape[0]
+    dq_ref[...] = jnp.zeros_like(dq_ref)
+    key_row = lax.broadcasted_iota(jnp.int32, (ATT, ATT), 0)
+    query_lane = lax.broadcasted_iota(jnp.int32, (ATT, ATT), 1)
+    for key_block in range(length // ATT):
+        rows = pl.ds(key_block * ATT, ATT)
+        keys = k_ref[rows, :]
+        values = v_ref[rows, :]
+        key_pos = key_block * ATT + key_row
+
+        def step(query_block, carried):
+            dk, dv = carried
+            base = pl.multiple_of(query_block * ATT, ATT)
+            queries = q_ref[pl.ds(base, ATT), :]
+            grads = g_ref[pl.ds(base, ATT), :]
+            doc_start = start_ref[pl.ds(query_block, 1), :]
+            allowed = (key_pos <= base + query_lane) & (key_pos >= doc_start)
+            weights = jnp.where(allowed, jnp.exp(dot_nt(keys, queries)), 0.0)
+            slopes = (weights * dot_nt(values, grads)).astype(jnp.bfloat16)
+            dv = dv + dot_nn(weights.astype(jnp.bfloat16), grads)
+            dk = dk + dot_nn(slopes, queries)
+            dq_ref[pl.ds(base, ATT), :] += dot_tn(slopes, keys)
+            return dk, dv
+
+        zero = jnp.zeros((ATT, 128), jnp.float32)
+        dk, dv = lax.fori_loop(key_block, last_ref[key_block], step, (zero, zero))
+        dk_ref[rows, :] = dk
+        dv_ref[rows, :] = dv
+
+
+SMEM_SPEC = pl.BlockSpec(memory_space=pltpu.SMEM)
+
+
+def split_three(column):
+    high = column.astype(jnp.bfloat16)
+    rest = column - high.astype(jnp.float32)
+    mid = rest.astype(jnp.bfloat16)
+    low = (rest - mid.astype(jnp.float32)).astype(jnp.bfloat16)
+    return [high, mid, low]
+
+
+def widened(matrix, columns):
+    joined = jnp.concatenate([matrix] + columns, axis=1)
+    return jnp.pad(joined, ((0, 0), (0, 128 - joined.shape[1])))
+
+
+def pack_stream(stream):
+    half = stream.shape[0] // 2
+    lower = stream[:half].reshape(GROUP, half // GROUP, -1)
+    upper = stream[half:].reshape(GROUP, half // GROUP, -1)[::-1]
+    return jnp.concatenate([lower, upper], axis=2)
+
+
+def unpack_rows(blocks):
+    width = blocks.shape[2] // 2
+    return jnp.concatenate(
+        [blocks[:, :, :width].transpose(1, 0, 2), blocks[:, :, width:].transpose(1, 0, 2)], axis=0
+    )
+
+
+def pack_rows(rows):
+    half = rows.shape[0] // 2
+    return jnp.concatenate(
+        [
+            rows[:half].reshape(half, GROUP, -1).transpose(1, 0, 2),
+            rows[half:].reshape(half, GROUP, -1).transpose(1, 0, 2),
+        ],
+        axis=2,
+    )
+
+
+def unpack_stream(blocks):
+    width = blocks.shape[2] // 2
+    lower = blocks[:, :, :width].reshape(-1, width)
+    upper = blocks[::-1, :, width:].reshape(-1, width)
+    return jnp.concatenate([lower, upper], axis=0)
+
+
+def on_device_heads(
+    tokens,
+    cotangent,
+    lengths,
+    w_query,
+    w_key,
+    w_value,
+    w_out,
+    w_up,
+    w_gate,
+    w_down,
+    s_qk,
+    s_up,
+    s_gate,
+    alpha_attn,
+    alpha_mlp,
+):
+    low = jnp.bfloat16
+    model_width = w_query.shape[0]
+    tok_rows = tokens.shape[2]
+    length = GROUP * tok_rows
+    dp, b = here()
+    score_scale = 1.0 / math.sqrt(HEAD_DIM)
+    hidden = tokens[0, 0]
+    hidden_f = hidden.astype(jnp.float32)
+    positions = jnp.arange(length, dtype=jnp.int32)
+    doc_ends = jnp.cumsum(lengths[0], dtype=jnp.int32)
+    doc_starts = doc_ends - lengths[0]
+    document = doc_index(positions, doc_ends)
+    member = document[:, None] == jnp.arange(lengths.shape[1], dtype=jnp.int32)[None]
+    start_of = jnp.sum(jnp.where(member, doc_starts[None], 0), axis=1, dtype=jnp.int32)
+    end_of = jnp.sum(jnp.where(member, doc_ends[None], 0), axis=1, dtype=jnp.int32)
+    blocks = length // ATT
+    first_block = start_of[::ATT] // ATT
+    last_block = (end_of[ATT - 1 :: ATT] + ATT - 1) // ATT
+
+    hidden_all = all_gather_group(hidden, 0)
+    head_col = b * HEAD_DIM
+
+    def head_slice(weight):
+        return lax.dynamic_slice_in_dim(weight, head_col, HEAD_DIM, 1)
+
+    gain = lax.dynamic_slice_in_dim(s_qk, head_col, HEAD_DIM, 0)
+    w_head = jnp.concatenate([head_slice(w_query), head_slice(w_key), head_slice(w_value)], axis=1)
+    raw = dot_nn(hidden_all, w_head)
+    query_raw, key_raw, value_raw = (
+        raw[:, :HEAD_DIM],
+        raw[:, HEAD_DIM : 2 * HEAD_DIM],
+        raw[:, 2 * HEAD_DIM :],
+    )
+
+    def scaled_norm(raw_rows, gain_vector):
+        return rms_norm(raw_rows) * gain_vector
+
+    queries = scaled_norm(query_raw, gain).astype(low)
+    keys = scaled_norm(key_raw, gain).astype(low)
+    values = value_raw.astype(low)
+    scaled_queries = queries * jnp.asarray(score_scale, low)
+    ones = jnp.ones((length, 1), low)
+    attended_head, log_total = pl.pallas_call(
+        attend_kernel,
+        out_shape=[
+            jax.ShapeDtypeStruct((length, HEAD_DIM), jnp.float32),
+            jax.ShapeDtypeStruct((length, 1), jnp.float32),
+        ],
+        in_specs=[SMEM_SPEC] + [VMEM_SPEC] * 4,
+        out_specs=[VMEM_SPEC] * 2,
+        compiler_params=pltpu.CompilerParams(vmem_limit_bytes=VMEM_LIMIT),
+        name="attend",
+    )(first_block, scaled_queries, keys, widened(values, [ones]), start_of[:, None])
+    attended_head_low = attended_head.astype(low)
+
+    attended_low = unpack_rows(swap_group(pack_stream(attended_head_low), 1)).reshape(
+        tok_rows, model_width
+    )
+    branch = dot_nn(attended_low, w_out)
+    middle, pull_attn = jax.vjp(residual_mix, hidden_f, branch, alpha_attn)
+    middle_low = middle.astype(low)
+    up_raw = dot_nn(middle_low, w_up)
+    gate_raw = dot_nn(middle_low, w_gate)
+    inner_low = gated_inner(up_raw, gate_raw, s_up, s_gate).astype(low)
+    mlp_raw = dot_nn(inner_low, w_down)
+    result, pull_out = jax.vjp(residual_mix, middle, mlp_raw, alpha_mlp)
+    grad_middle, grad_mlp, grad_alpha_mlp = pull_out(cotangent[0, 0].astype(jnp.float32))
+    grad_mlp_low = grad_mlp.astype(low)
+    grad_inner = dot_nt(grad_mlp_low, w_down)
+    _, pull_inner = jax.vjp(lambda u, g: gated_inner(u, g, s_up, s_gate), up_raw, gate_raw)
+    grad_up_raw, grad_gate_raw = pull_inner(grad_inner)
+    grad_middle = (
+        grad_middle
+        + dot_nt(grad_up_raw.astype(low), w_up)
+        + dot_nt(grad_gate_raw.astype(low), w_gate)
+    )
+    grad_hidden, grad_branch, grad_alpha_attn = pull_attn(grad_middle)
+    branch_low = grad_branch.astype(low)
+    grad_att_low = dot_nt(branch_low, w_out).astype(low)
+
+    grad_head = unpack_stream(swap_group(pack_rows(grad_att_low), 2))
+    delta = jnp.sum(grad_head.astype(jnp.float32) * attended_head, axis=1, keepdims=True)
+    minus = [-ones] * 3
+    dq, dk, dv = pl.pallas_call(
+        attend_grad_kernel,
+        out_shape=[jax.ShapeDtypeStruct((length, 128), jnp.float32)] * 3,
+        in_specs=[SMEM_SPEC] + [VMEM_SPEC] * 5,
+        out_specs=[VMEM_SPEC] * 3,
+        compiler_params=pltpu.CompilerParams(vmem_limit_bytes=VMEM_LIMIT),
+        name="attend_grad",
+    )(
+        last_block,
+        widened(scaled_queries, split_three(log_total)),
+        widened(keys, minus),
+        widened(values, minus),
+        widened(grad_head, split_three(delta)),
+        start_of.reshape(blocks, ATT),
+    )
+    grad_queries = dq[:, :HEAD_DIM] * score_scale
+    grad_keys = dk[:, :HEAD_DIM]
+    grad_values = dv[:, :HEAD_DIM]
+    _, pull_query = jax.vjp(scaled_norm, query_raw, gain)
+    grad_query_raw, grad_qk_first = pull_query(grad_queries)
+    _, pull_key = jax.vjp(scaled_norm, key_raw, gain)
+    grad_key_raw, grad_qk_second = pull_key(grad_keys)
+    grad_s_qk = grad_qk_first + grad_qk_second
+    raw_low = jnp.concatenate([grad_query_raw, grad_key_raw, grad_values], axis=1).astype(low)
+    home = swap_group(pack_stream(raw_low), 3)
+    home = unpack_rows(home)
+
+    def home_part(index):
+        return home[:, :, index * HEAD_DIM : (index + 1) * HEAD_DIM].reshape(tok_rows, model_width)
+
+    input_grad = (
+        grad_hidden
+        + dot_nt(home_part(0), w_query)
+        + dot_nt(home_part(1), w_key)
+        + dot_nt(home_part(2), w_value)
+    )
+
+    middle_all = all_gather_group(middle_low, 4)
+    mlp_all = all_gather_group(grad_mlp_low, 5)
+    branch_all = all_gather_group(branch_low, 6)
+    ff_part = w_up.shape[1] // (2 * GROUP)
+    ff_half = w_up.shape[1] // 2
+
+    def ff_slice(array, axis):
+        return jnp.concatenate(
+            [
+                lax.dynamic_slice_in_dim(array, b * ff_part, ff_part, axis),
+                lax.dynamic_slice_in_dim(array, ff_half + b * ff_part, ff_part, axis),
+            ],
+            axis=axis,
+        )
+
+    up_part = dot_nn(middle_all, ff_slice(w_up, 1))
+    gate_part = dot_nn(middle_all, ff_slice(w_gate, 1))
+    inner_grad_part = dot_nt(mlp_all, ff_slice(w_down, 0))
+    inner_part, pull_part = jax.vjp(
+        gated_inner, up_part, gate_part, ff_slice(s_up, 0), ff_slice(s_gate, 0)
+    )
+    g_up, g_gate, g_s_up, g_s_gate = pull_part(inner_grad_part)
+    part_down = dot_tn(inner_part.astype(low), mlp_all)
+    part_up = dot_tn(middle_all, g_up.astype(low))
+    part_gate = dot_tn(middle_all, g_gate.astype(low))
+    part_qkv = dot_tn(hidden_all, raw_low)
+    part_out = dot_tn(attended_head_low, branch_all)
+
+    part_wide = jnp.concatenate(
+        [part_up, part_gate, part_qkv, jnp.zeros((model_width, 64), jnp.float32)], axis=1
+    )
+    half_width = model_width // 2
+
+    def mine(array, size, axis=0):
+        return lax.dynamic_slice_in_dim(array, dp * size, size, axis)
+
+    def other(array, size, axis=0):
+        return lax.dynamic_slice_in_dim(array, (1 - dp) * size, size, axis)
+
+    got_wide, got_down, got_out = swap_dp(
+        [other(part_wide, half_width).astype(low), other(part_down, ff_part).astype(low), part_out.astype(low)],
+        7,
+    )
+    grad_down = mine(part_down, ff_part) + got_down
+    wide = (mine(part_wide, half_width) + got_wide).astype(low)
+    out_rows = part_out + got_out
+    wide = wide.reshape(GROUP, half_width // GROUP, -1)
+    got = swap_group(wide, 8)
+    grad_up = jnp.concatenate(
+        [got[:, :, i * ff_part : (i + 1) * ff_part].transpose(1, 0, 2).reshape(-1, ff_half) for i in (0, 1)],
+        axis=1,
+    ).astype(jnp.float32)
+    grad_gate = jnp.concatenate(
+        [got[:, :, i * ff_part : (i + 1) * ff_part].transpose(1, 0, 2).reshape(-1, ff_half) for i in (2, 3)],
+        axis=1,
+    ).astype(jnp.float32)
+    base = 4 * ff_part
+    grad_query, grad_key, grad_value = (
+        got[:, :, base + i * HEAD_DIM : base + (i + 1) * HEAD_DIM]
+        .transpose(1, 0, 2)
+        .reshape(-1, model_width)
+        .astype(jnp.float32)
+        for i in range(3)
+    )
+    out_all = lax.all_gather(out_rows, "blk", axis=0, tiled=True)
+    rows_out = model_width // (2 * GROUP)
+    grad_out = lax.dynamic_slice_in_dim(out_all, (dp * GROUP + b) * rows_out, rows_out, 0)
+
+    def vector_rows(vector):
+        rows = vector.reshape(2 * GROUP, -1)
+        return jnp.pad(rows, ((0, 0), (0, 128 - rows.shape[1])))
+
+    def placed(part, total):
+        full = jnp.zeros((total,), jnp.float32)
+        return full, part
+
+    s_full = jnp.zeros((model_width,), jnp.float32)
+    s_full = lax.dynamic_update_slice_in_dim(s_full, grad_s_qk, head_col, 0)
+
+    def ff_full(part):
+        full = jnp.zeros((w_up.shape[1],), jnp.float32)
+        full = lax.dynamic_update_slice_in_dim(full, part[:ff_part], b * ff_part, 0)
+        return lax.dynamic_update_slice_in_dim(full, part[ff_part:], ff_half + b * ff_part, 0)
+
+    small = jnp.stack(
+        [
+            vector_rows(s_full),
+            vector_rows(ff_full(g_s_up)),
+            vector_rows(ff_full(g_s_gate)),
+            vector_rows(grad_alpha_attn),
+            vector_rows(grad_alpha_mlp),
+        ],
+        axis=1,
+    )
+    small = jnp.pad(small, ((0, 0), (0, 3), (0, 0)))
+    small = jnp.sum(swap_all(small, 9), axis=0)
+    mean_alpha = 0.5 * (jnp.mean(alpha_attn) + jnp.mean(alpha_mlp))
+    return (
+        result.astype(low)[None, None],
+        input_grad[None, None],
+        grad_query,
+        grad_key,
+        grad_value,
+        grad_out,
+        grad_up,
+        grad_gate,
+        grad_down,
+        small[0, :rows_out],
+        small[1],
+        small[2],
+        small[3, :rows_out],
+        small[4, :rows_out],
+        mean_alpha,
+    )
+
+
+def on_device(*arrays):
+    head_count = arrays[3].shape[0] // HEAD_DIM
+    tok_rows = arrays[0].shape[2]
+    fits = lax.axis_size("blk") == head_count == 16 and lax.axis_size("dp") == 2
+    if fits and tok_rows == 128:
+        return on_device_heads(*arrays)
+    return on_device_general(*arrays)
+
+
 def solution(mesh):
     in_specs = (
         P("dp", "blk", None, None),

time: 1580 us -> 480 us (0.30)
  the two profiles are of different devices: /device:TPU:0 before, /device:TPU:13 now
where the time goes in v1:
time: 480 us; the launch traced here: 473 us
  Pallas kernels  320 us (67%)
  matrix products  58.9 us (12%)
  local copies, waits for them, and re-layouts  38.4 us (8%)
  other arithmetic  37.8 us (8%)
  between operations  17.8 us (4%)
    pallas_call x4, Pallas kernels, all_gather_group(): pl.pallas_call(gather_kernel, out_shape=jax.ShapeDtypeStruct((2 * GROUP,...  166 us
    pallas_call x4, Pallas kernels, swap_group(): pl.pallas_call(swap_group_kernel, out_shape=jax.ShapeDtypeStruct(blocks.s...  81.1 us
    pallas_call x1, Pallas kernels, swap_dp(): pl.pallas_call(functools.partial(swap_dp_kernel, count), out_shape=[jax.S...  29.9 us
    dot_general x8, matrix products, dot_nt(): lax.dot_general(left, right, (((1,), (1,)), ((), ())), preferred_element_...  26.5 us
    dot_general x7, matrix products, dot_nn(): return jnp.dot(left, right, preferred_element_type=jnp.float32)  18.2 us
    pallas_call x1, Pallas kernels, on_device_heads(): pl.pallas_call(attend_grad_kernel, out_shape=[jax.ShapeDtypeStruct((lengt...  16.1 us
    dot_general x5, matrix products, dot_tn(): lax.dot_general(left, right, (((0,), (0,)), ((), ())), preferred_element_...  14.2 us
    pallas_call x1, Pallas kernels, swap_all(): pl.pallas_call(swap_all_kernel, out_shape=jax.ShapeDtypeStruct(blocks.sha...  14.1 us
  transfers between devices with their start and end apart: 1, of which 0 were waited for; matrix products, arithmetic and copies ran while one was open for 6% of the time, Pallas kernels for 15%

profile of v1, /device:TPU:13, one launch (start us, length us, event | category | flops | bytes accessed | tf_op | source)
XLA Modules:
  0.0 473.0 jit_solution(3595171495343419968)
XLA Ops:
  13.1 40.9 %gather_group.4 = bf16[32,64,1024]{2,1,0:T(8,128)(2,1)} custom-call(bf16[2,64,1024]{2,1,0:T(8,128)(2,1)} %bitcast.170), custom_call_target="tpu_custom_call" | custom-call | tf_op jit(solution)/shard_map/gather_group/pallas_call | solution.py:488
  55.2 3.6 convolution_bitcast_fusion
  64.3 12.7 %attend.1 = (f32[2048,64]{1,0:T(8,128)}, f32[2048,1]{1,0:T(8,128)}) custom-call(s32[8]{0:T(128)} %get-tuple-element.118.first_ref, bf16[2048,64]{1,0:T(8,128)(2,1)} %get-tuple-element.67.q_ref, bf16[2048,64]{1,0:T(8,128)(2,1)} %copy-done.9, bf16[2048,128]{1,0:T(8,128)(2,1)} %get-tuple-element.88.v_ref, s32[2048,1]{1,0:T(8,128)} %copy.75.start_ref), custom_call_target="tpu_custom_call" | custom-call | tf_op jit(solution)/shard_map/attend/pallas_call | solution.py:779
  80.0 12.2 %swap_group.4 = bf16[16,64,128]{2,1,0:T(8,128)(2,1)} custom-call(bf16[16,64,128]{2,1,0:T(8,128)(2,1)} %pad_maximum_fusion.4.blocks), custom_call_target="tpu_custom_call" | custom-call | tf_op jit(solution)/shard_map/swap_group/pallas_call | solution.py:519
  96.4 2.2 constant_dynamic-slice_fusion.2
  98.7 4.8 %convolution_multiply_fusion = f32[128,4096]{1,0:T(8,128)S(1)} fusion(bf16[128,1024]{1,0:T(8,128)(2,1)S(1)} %multiply_convert_fusion.15, bf16[1024,4096]{1,0:T(8,128)(2,1)} %param.23, f32[4096]{0:T(1024)S(1)} %copy-done.48), kind=kOutput, calls=%fused_computation | convolution fusion | flops 1074266112 | bytes 10764288 | tf_op jit(solution)/shard_map/dot_general | solution.py:612
  111.3 7.8 %fusion.83 = f32[128,4096]{1,0:T(8,128)} fusion(bf16[128,1024]{1,0:T(8,128)(2,1)S(1)} %get-tuple-element.85, bf16[4096,1024]{1,0:T(8,128)(2,1)} %param.24), kind=kOutput, calls=%fused_computation.230 | convolution fusion | flops 1073741824 | bytes 10747904 | tf_op jit(solution)/shard_map/dot_general | solution.py:604
  119.1 5.5 %convolution_add_fusion.4 = f32[128,1024]{1,0:T(8,128)} fusion(bf16[1024,4096]{1,0:T(8,128)(2,1)S(1)} %bitcast.149, f32[128,4096]{1,0:T(8,128)} %fusion.83, f32[4096]{0:T(1024)S(1)} %copy-done.47, f32[128,4096]{1,0:T(8,128)S(1)} %convolution_multiply_fusion, f32[128,1024]{1,0:T(8,128)S(1)} %get-tuple-element.53, ...), kind=kOutput, calls=%fused_computation.27 | convolution fusion | flops 1078067200 | bytes 13915136 | tf_op jit(solution)/shard_map/dot_general | solution.py:604
  124.7 6.1 %multiply_reduce_fusion.12 = (f32[128]{0:T(128)S(1)}, f32[128,1024]{1,0:T(8,128)S(1)}) fusion(f32[128,1024]{1,0:T(8,128)S(1)} %get-tuple-element.55, f32[128,1024]{1,0:T(8,128)} %convolution_add_fusion.4, bf16[1024,4096]{1,0:T(8,128)(2,1)S(1)} %bitcast.151, f32[128,4096]{1,0:T(8,128)S(1)} %convolution_multiply_fusion, f32[128,4096]{1,0:T(8,128)} %copy-done.30, ...), kind=kOutput, calls=%fused_computation.123 | convolution fusion | flops 1081474944 | bytes 16269824 | tf_op jit(solution)/shard_map/dot_general | solution.py:604
  134.5 12.1 %swap_group.5 = bf16[16,64,128]{2,1,0:T(8,128)(2,1)} custom-call(bf16[16,64,128]{2,1,0:T(8,128)(2,1)} %pad_maximum_fusion.5.blocks), custom_call_target="tpu_custom_call" | custom-call | tf_op jit(solution)/shard_map/swap_group/pallas_call | solution.py:519
  148.6 41.3 %gather_group.6 = bf16[32,64,1024]{2,1,0:T(8,128)(2,1)} custom-call(bf16[2,64,1024]{2,1,0:T(8,128)(2,1)} %bitcast.171), custom_call_target="tpu_custom_call" | custom-call | tf_op jit(solution)/shard_map/gather_group/pallas_call | solution.py:488
  189.9 42.4 %gather_group.5 = bf16[32,64,1024]{2,1,0:T(8,128)(2,1)} custom-call(bf16[2,64,1024]{2,1,0:T(8,128)(2,1)} %bitcast.155), custom_call_target="tpu_custom_call" | custom-call | tf_op jit(solution)/shard_map/gather_group/pallas_call | solution.py:488
  236.0 4.1 multiply_reduce_fusion
  240.1 2.5 fusion.6
  242.6 2.6 fusion.4
  252.6 16.1 %attend_grad.1 = (f32[2048,128]{1,0:T(8,128)}, f32[2048,128]{1,0:T(8,128)}, f32[2048,128]{1,0:T(8,128)}) custom-call(s32[8]{0:T(128)} %get-tuple-element.117.last_ref, bf16[2048,128]{1,0:T(8,128)(2,1)} %fusion.32.q_ref, bf16[2048,128]{1,0:T(8,128)(2,1)} %fusion.13.k_ref, bf16[2048,128]{1,0:T(8,128)(2,1)} %get-tuple-element.87.v_ref, ...), custom_call_target="tpu_custom_call" | custom-call | tf_op jit(solution)/shard_map/attend_grad/pallas_call | solution.py:820
  270.0 2.9 multiply_reduce_fusion.2
  273.0 1.7 fusion.1
  275.2 2.8 convolution_bitcast_fusion.1
  278.0 41.6 %gather_group.7 = bf16[32,64,1024]{2,1,0:T(8,128)(2,1)} custom-call(bf16[2,64,1024]{2,1,0:T(8,128)(2,1)} %bitcast.165), custom_call_target="tpu_custom_call" | custom-call | tf_op jit(solution)/shard_map/gather_group/pallas_call | solution.py:488
  319.7 3.9 fusion.82
  323.5 2.4 fusion.5
  326.0 1.8 dynamic-slice_convert_fusion.1.refs_1_
  327.8 1.8 maximum_maximum_fusion
  329.6 1.7 copy-done.4
  332.3 29.9 %swap_dp.1 = (bf16[512,768]{1,0:T(8,128)(2,1)}, bf16[128,1024]{1,0:T(8,128)(2,1)}, bf16[64,1024]{1,0:T(8,128)(2,1)}) custom-call(bf16[512,768]{1,0:T(8,128)(2,1)} %dynamic-slice_convert_fusion.refs_0_, bf16[128,1024]{1,0:T(8,128)(2,1)} %dynamic-slice_convert_fusion.1.refs_1_, bf16[64,1024]{1,0:T(8,128)(2,1)} %get-tuple-element.115.refs_2_), custom_call_target="tpu_custom_call" | custom-call | tf_op jit(solution)/shard_map/swap_dp/pallas_call | solution.py:548
  366.6 32.7 %swap_group.6 = bf16[16,64,384]{2,1,0:T(8,128)(2,1)} custom-call(bf16[16,64,384]{2,1,0:T(8,128)(2,1)} %pad_maximum_fusion.1.blocks), custom_call_target="tpu_custom_call" | custom-call | tf_op jit(solution)/shard_map/swap_group/pallas_call | solution.py:519
  403.5 14.1 %swap_all.1 = f32[32,8,128]{2,1,0:T(8,128)} custom-call(f32[32,8,128]{2,1,0:T(8,128)} %pad.42.blocks), custom_call_target="tpu_custom_call" | custom-call | tf_op jit(solution)/shard_map/swap_all/pallas_call | solution.py:586
  417.6 2.6 add_convert_fusion
  420.2 24.1 %swap_group.7 = bf16[16,32,768]{2,1,0:T(8,128)(2,1)} custom-call(bf16[16,32,768]{2,1,0:T(8,128)(2,1)} %bitcast.164), custom_call_target="tpu_custom_call" | custom-call | tf_op jit(solution)/shard_map/swap_group/pallas_call | solution.py:519
  453.9 1.9 convert_add_fusion.1
  455.9 2.4 convolution_add_fusion.2
  (239 shorter events, 70.0 us)
Async XLA Ops:
  7.2 87.2 %copy-start = (bf16[1024,1024]{1,0:T(8,128)(2,1)S(1)}, bf16[1024,1024]{1,0:T(8,128)(2,1)}, u32[]{:S(2)}) copy-start(bf16[1024,1024]{1,0:T(8,128)(2,1)} %param.21) | copy-start | bytes 6291460
  7.2 456.0 %all-gather.2.cloned.1.call-start = ((), (), s32[]{:S(2)}) async-start(), calls=%async_computation | async-start | bytes 4456448 | tf_op jit(solution)/shard_map/all_gather | solution.py:921
  58.9 2.5 copy-start.2
  60.4 3.4 copy-start.9
  98.6 5.0 %slice-start = ((s8[8388608]{0:T(1024)(128)(4,1)}), s8[4194304]{0:T(1024)(128)(4,1)S(1)}, s32[]{:S(2)}) async-start(s8[8388608]{0:T(1024)(128)(4,1)} %bitcast.148), calls=%async_computation.1 | async-start | bytes 8388608
  98.7 4.9 %copy-start.5 = (bf16[128,1024]{1,0:T(8,128)(2,1)}, bf16[128,1024]{1,0:T(8,128)(2,1)S(1)}, u32[]{:S(2)}) copy-start(bf16[128,1024]{1,0:T(8,128)(2,1)S(1)} %multiply_convert_fusion.15) | copy-start | bytes 786436
  98.7 5.8 %slice-start.1 = ((s8[8388608]{0:T(1024)(128)(4,1)}), s8[4194304]{0:T(1024)(128)(4,1)S(1)}, s32[]{:S(2)}) async-start(s8[8388608]{0:T(1024)(128)(4,1)} %bitcast.148), calls=%async_computation.2 | async-start | bytes 8388608
  98.7 7.1 %slice-start.4 = ((s8[8388608]{0:T(1024)(128)(4,1)}), s8[4194304]{0:T(1024)(128)(4,1)S(1)}, s32[]{:S(2)}) async-start(s8[8388608]{0:T(1024)(128)(4,1)} %bitcast.153), calls=%async_computation.5 | async-start | bytes 8388608
  104.6 2.6 slice-start.5
  111.3 7.8 %copy-start.25 = (bf16[128,1024]{1,0:T(8,128)(2,1)}, bf16[128,1024]{1,0:T(8,128)(2,1)S(1)}, u32[]{:S(2)}) copy-start(bf16[128,1024]{1,0:T(8,128)(2,1)S(1)} %get-tuple-element.85) | copy-start | bytes 786436
  111.3 13.3 %slice-start.2 = ((s8[8388608]{0:T(1024)(128)(4,1)}), s8[4194304]{0:T(1024)(128)(4,1)S(1)}, s32[]{:S(2)}) async-start(s8[8388608]{0:T(1024)(128)(4,1)} %bitcast.150), calls=%async_computation.3 | async-start | bytes 8388608
  119.1 5.5 %slice-start.3 = ((s8[8388608]{0:T(1024)(128)(4,1)}), s8[4194304]{0:T(1024)(128)(4,1)S(1)}, s32[]{:S(2)}) async-start(s8[8388608]{0:T(1024)(128)(4,1)} %bitcast.150), calls=%async_computation.4 | async-start | bytes 8388608
  124.7 6.1 %copy-start.24 = (bf16[1,1,128,1024]{3,2,1,0:T(8,128)(2,1)S(1)}, bf16[1,1,128,1024]{3,2,1,0:T(8,128)(2,1)}, u32[]{:S(2)}) copy-start(bf16[1,1,128,1024]{3,2,1,0:T(8,128)(2,1)} %param.15) | copy-start | bytes 786436
  133.3 14.6 %copy-start.12 = (f32[2048,64]{1,0:T(8,128)S(1)}, f32[2048,64]{1,0:T(8,128)}, u32[]{:S(2)}) copy-start(f32[2048,64]{1,0:T(8,128)} %get-tuple-element.23) | copy-start | bytes 1572868
  148.6 83.8 %copy-start.40 = (bf16[128,1024]{1,0:T(8,128)(2,1)S(1)}, bf16[128,1024]{1,0:T(8,128)(2,1)}, u32[]{:S(2)}) copy-start(bf16[128,1024]{1,0:T(8,128)(2,1)} %get-tuple-element.57) | copy-start | bytes 786436
  189.9 42.5 %copy-start.16 = (bf16[32,64,1024]{2,1,0:T(8,128)(2,1)S(1)}, bf16[32,64,1024]{2,1,0:T(8,128)(2,1)}, u32[]{:S(2)}) copy-start(bf16[32,64,1024]{2,1,0:T(8,128)(2,1)} %gather_group.6) | copy-start | bytes 12582916
  189.9 42.5 %copy-start.39 = (bf16[128,1024]{1,0:T(8,128)(2,1)S(1)}, bf16[128,1024]{1,0:T(8,128)(2,1)}, u32[]{:S(2)}) copy-start(bf16[128,1024]{1,0:T(8,128)(2,1)} %get-tuple-element.56) | copy-start | bytes 786436
  242.6 2.6 copy-start.31
  248.2 2.8 copy-start.29
  252.6 17.4 %copy-start.3 = (f32[2048,192]{1,0:T(8,128)S(1)}, f32[2048,192]{1,0:T(8,128)}, u32[]{:S(2)}) copy-start(f32[2048,192]{1,0:T(8,128)} %copy-done.2) | copy-start | bytes 4718596
  270.0 3.0 copy-start.17
  270.0 3.0 copy-start.18
  278.0 41.6 %copy-start.7 = (bf16[2048,64]{1,0:T(8,128)(2,1)S(1)}, bf16[2048,64]{1,0:T(8,128)(2,1)}, u32[]{:S(2)}) copy-start(bf16[2048,64]{1,0:T(8,128)(2,1)} %copy-done.6) | copy-start | bytes 786436
  278.0 45.5 %copy-start.49 = (f32[2048,256]{1,0:T(8,128)S(1)}, f32[2048,256]{1,0:T(8,128)}, u32[]{:S(2)}) copy-start(f32[2048,256]{1,0:T(8,128)} %get-tuple-element.49) | copy-start | bytes 6291460
  319.7 3.9 copy-start.15
  323.5 4.2 copy-start.32
  401.4 16.2 %copy-start.33 = (bf16[512,768]{1,0:T(8,128)(2,1)S(1)}, bf16[512,768]{1,0:T(8,128)(2,1)}, u32[]{:S(2)}) copy-start(bf16[512,768]{1,0:T(8,128)(2,1)} %get-tuple-element.28) | copy-start | bytes 2359300
  445.5 7.4 %copy-start.35 = (f32[32,8,128]{2,1,0:T(8,128)S(1)}, f32[32,8,128]{2,1,0:T(8,128)}, u32[]{:S(2)}) copy-start(f32[32,8,128]{2,1,0:T(8,128)} %swap_all.1) | copy-start | bytes 393220
  446.7 7.3 %copy-start.34 = (f32[256,1024]{1,0:T(8,128)S(1)}, f32[256,1024]{1,0:T(8,128)}, u32[]{:S(2)}) copy-start(f32[256,1024]{1,0:T(8,128)} %fusion.6) | copy-start | bytes 3145732
  447.6 8.3 %copy-start.11 = (f32[128,1024]{1,0:T(8,128)S(1)}, f32[128,1024]{1,0:T(8,128)}, u32[]{:S(2)}) copy-start(f32[128,1024]{1,0:T(8,128)} %copy-done.10) | copy-start | bytes 1572868
  453.9 4.4 copy-start.19
  459.2 5.6 %copy-start.1 = (bf16[1024,1024]{1,0:T(8,128)(2,1)S(1)}, bf16[1024,1024]{1,0:T(8,128)(2,1)}, u32[]{:S(2)}) copy-start(bf16[1024,1024]{1,0:T(8,128)(2,1)} %param.21) | copy-start | bytes 6291460
  (25 other events, 44.0 us)
Sparse Core Ops, SparseCore 0:
  363.9 65.3 all-gather.1

commit v2 on v1

--- a/solution.py
+++ b/solution.py
@@ -383,98 +383,133 @@
 
 
 class Gather:
-    CLASSES = 15
+    SEMAPHORES = 40
 
     def __init__(self, own, out, send, recv):
         self.own, self.out, self.send, self.recv = own, out, send, recv
         dp, b = here()
+        self.dp, self.b = dp, b
         self.z, self.y, self.c = b // 4, (b // 2) % 2, b % 2
-        self.up = (dp, self.block(1, 0))
-        self.down = (dp, self.block(3, 0))
-        self.side = (dp, self.block(0, 1))
+        self.up = (dp, (b + 4) % GROUP)
+        self.down = (dp, (b + 12) % GROUP)
+        self.side = (dp, b + 2 - 4 * self.y)
         self.sib = (dp, b + 1 - 2 * self.c)
-        self.b = b
-
-    def block(self, dz, dy):
-        return (((self.z + dz) % 4) * 2 + (self.y + dy) % 2) * 2 + self.c
-
-    def slot(self, block, half):
-        return 2 * GROUP - 1 - block if half else block
-
-    def copy(self, block, kind, half, device, own=False):
-        place = self.slot(block, half)
+
+    def partners(self):
+        return [self.up, self.down, self.side, self.sib]
+
+    def copy(self, z, y, c, kind, half, device, own=False):
+        block = z * 4 + y * 2 + c
+        place = 2 * GROUP - 1 - block if half else block
         source = self.own.at[half] if own else self.out.at[place]
         index = 2 * kind + half
         return remote(source, self.out.at[place], self.send.at[index], self.recv.at[index], device)
 
-    def partners(self):
-        return [self.up, self.down, self.side, self.sib]
-
-    KINDS = {
-        0: (0, 1, (0, 1)),
-        1: (3, 0, (0, 1)),
-        2: (1, 0, (0, 1)),
-        3: (3, 1, (0, 1)),
-        4: (1, 1, (0, 1)),
-        5: (2, 0, (0, 1)),
-        6: (2, 1, (0, 1)),
-    }
+    def along(self, z, half, device, own=False, back=False):
+        return self.copy(z, self.y, self.c, z + (16 if back else 0), half, device, own)
+
+    def across(self, z, y, half, own=False):
+        return self.copy(z, y, self.c, 4 + z, half, self.side, own)
+
+    def to_sib(self, z, y, c, half, own=False):
+        return self.copy(z, y, c, 8 + 2 * z + y, half, self.sib, own)
 
     def start(self):
+        z, y = self.z, self.y
         for half in (0, 1):
-            self.copy(self.b, 1, half, self.up, True).start()
-            self.copy(self.b, 2, half, self.down, True).start()
-            self.copy(self.b, 0, half, self.side, True).start()
+
+            @pl.when(z < 3)
+            def _():
+                self.along(z, half, self.up, True).start()
+
+            @pl.when(z > 0)
+            def _():
+                self.along(z, half, self.down, True, True).start()
+
+            self.across(z, y, half, True).start()
         for half in (0, 1):
-            self.copy(self.b, 7, half, self.sib, True).start()
+            self.to_sib(z, y, self.c, half, True).start()
         for half in (0, 1):
-            self.out[self.slot(self.b, half)] = self.own[half]
-
-    def arrive(self, kind):
-        dz, dy, halves = self.KINDS[kind]
-        block = self.block(dz, dy)
-        for half in halves:
-            self.copy(block, kind, half, self.sib).wait_recv()
-            if kind == 0:
-                self.copy(block, 3, half, self.up).start()
-                self.copy(block, 4, half, self.down).start()
-            if kind == 1 and half == 0:
-                self.copy(block, 5, half, self.up).start()
-            if kind == 2 and half == 1:
-                self.copy(block, 5, half, self.down).start()
-            if kind == 5:
-                self.copy(block, 6, half, self.side).start()
-            self.copy(block, 8 + kind, half, self.sib).start()
-
-    def first(self):
-        for kind in (0, 1, 2):
-            self.arrive(kind)
-
-    def second(self):
-        for kind in (5, 3, 4):
-            self.arrive(kind)
-
-    def last(self):
-        self.arrive(6)
-        for kind in range(7):
-            dz, dy, halves = self.KINDS[kind]
-            other = self.block(dz, dy) + 1 - 2 * self.c
-            for half in halves:
-                self.copy(other, 8 + kind, half, self.sib).wait_recv()
+            place = 2 * GROUP - 1 - self.b if half else self.b
+            self.out[place] = self.own[half]
+
+    def line(self, distance):
         for half in (0, 1):
-            self.copy(self.b + 1 - 2 * self.c, 7, half, self.sib).wait_recv()
-        for kind in range(self.CLASSES):
-            for half in (0, 1):
-                self.copy(self.b, kind, half, self.sib).wait_send()
+            low, high = self.z - distance, self.z + distance
+
+            @pl.when(low >= 0)
+            def _():
+                self.along(low, half, self.sib).wait_recv()
+
+                @pl.when(self.z < 3)
+                def _():
+                    self.along(low, half, self.up).start()
+
+                self.across(low, self.y, half).start()
+                self.to_sib(low, self.y, self.c, half).start()
+
+            @pl.when(high <= 3)
+            def _():
+                self.along(high, half, self.sib, False, True).wait_recv()
+
+                @pl.when(self.z > 0)
+                def _():
+                    self.along(high, half, self.down, False, True).start()
+
+                self.across(high, self.y, half).start()
+                self.to_sib(high, self.y, self.c, half).start()
+
+    def sides(self, distance):
+        def one(z, half):
+            self.across(z, 1 - self.y, half).wait_recv()
+            self.to_sib(z, 1 - self.y, self.c, half).start()
+
+        for half in (0, 1):
+            if distance == 0:
+                one(self.z, half)
+            else:
+
+                @pl.when(self.z - distance >= 0)
+                def _():
+                    one(self.z - distance, half)
+
+                @pl.when(self.z + distance <= 3)
+                def _():
+                    one(self.z + distance, half)
+
+    def finish(self):
+        for half in (0, 1):
+            for z in range(4):
+                for y in (0, 1):
+                    self.to_sib(z, y, 1 - self.c, half).wait_recv()
+                    self.to_sib(z, y, self.c, half).wait_send()
+                self.across(z, self.y, half).wait_send()
+
+                @pl.when((self.z >= z) & (self.z < 3))
+                def _():
+                    self.along(z, half, self.up).wait_send()
+
+                @pl.when((self.z <= z) & (self.z > 0))
+                def _():
+                    self.along(z, half, self.down, False, True).wait_send()
+
+
+def gather_scratch():
+    return [pltpu.SemaphoreType.DMA((Gather.SEMAPHORES,)) for _ in range(2)]
 
 
 def gather_kernel(own, out, send, recv):
     gather = Gather(own, out, send, recv)
     greet(gather.partners())
     gather.start()
-    gather.first()
-    gather.second()
-    gather.last()
+    gather.line(1)
+    gather.sides(0)
+    gather.line(2)
+    gather.sides(1)
+    gather.line(3)
+    gather.sides(2)
+    gather.sides(3)
+    gather.finish()
 
 
 def comm_params(collective_id):
@@ -490,10 +525,7 @@
         out_shape=jax.ShapeDtypeStruct((2 * GROUP, tok_rows // 2, width), rows.dtype),
         in_specs=[VMEM_SPEC],
         out_specs=VMEM_SPEC,
-        scratch_shapes=[
-            pltpu.SemaphoreType.DMA((2 * Gather.CLASSES,)),
-            pltpu.SemaphoreType.DMA((2 * Gather.CLASSES,)),
-        ],
+        scratch_shapes=gather_scratch(),
         compiler_params=comm_params(collective_id),
         name="gather_group",
     )(rows.reshape(2, tok_rows // 2, width))
@@ -669,15 +701,257 @@
         dv_ref[rows, :] = dv
 
 
+FF_STEP = 512
+
+
+def mean_last(array):
+    return jnp.mean(array, axis=-1, keepdims=True)
+
+
+def rms_scale(array):
+    return lax.rsqrt(mean_last(array * array) + 1e-06)
+
+
+def rms_pull(grad, normed, scale):
+    return scale * (grad - normed * mean_last(grad * normed))
+
+
+def half_lanes(shape):
+    return lax.broadcasted_iota(jnp.int32, shape, 1) < HEAD_DIM
+
+
+class Swap:
+    def __init__(self, blocks, out, send, recv):
+        self.blocks, self.out = blocks, out
+        dp, self.b = here()
+        self.copies = []
+        for step in range(1, GROUP):
+            target = (self.b + step) % GROUP
+            self.copies.append(
+                remote(blocks.at[target], out.at[self.b], send.at[step], recv.at[step], (dp, target))
+            )
+        self.partners = [(dp, (self.b + step) % GROUP) for step in range(1, GROUP)]
+
+    def start(self):
+        for copy in self.copies:
+            copy.start()
+        self.out[self.b] = self.blocks[self.b]
+
+    def wait(self):
+        for copy in self.copies:
+            copy.wait()
+
+
+def middle_kernel(
+    o_ref,
+    hidden_ref,
+    cot_ref,
+    w_out_hbm,
+    w_up_hbm,
+    w_gate_hbm,
+    w_down_hbm,
+    s_up_ref,
+    s_gate_ref,
+    alpha_attn_ref,
+    alpha_mlp_ref,
+    result_ref,
+    g_res_ref,
+    grad_head_ref,
+    mid_all_ref,
+    g_mlp_ref,
+    att_ref,
+    g_branch_ref,
+    g_alpha_attn_ref,
+    g_alpha_mlp_ref,
+    w_out,
+    w_up,
+    w_gate,
+    w_down,
+    up_raw,
+    gate_raw,
+    mid_own,
+    o_in,
+    g_send,
+    acc,
+    load_sem,
+    swap_sems,
+    back_sems,
+    ag_send,
+    ag_recv,
+):
+    low = jnp.bfloat16
+    loads = [
+        pltpu.make_async_copy(source, target, load_sem.at[i])
+        for i, (source, target) in enumerate(
+            [(w_out_hbm, w_out), (w_up_hbm, w_up), (w_gate_hbm, w_gate), (w_down_hbm, w_down)]
+        )
+    ]
+    for load in loads:
+        load.start()
+    swap = Swap(o_ref, o_in, swap_sems.at[0], swap_sems.at[1])
+    gather = Gather(mid_own, mid_all_ref, ag_send, ag_recv)
+    greet(swap.partners)
+    swap.start()
+    swap.wait()
+    rows = hidden_ref.shape[0]
+    half = rows // 2
+    first = half_lanes((half, 128))
+    for pair in range(GROUP // 2):
+        even = o_in[2 * pair].astype(jnp.float32)
+        odd = o_in[2 * pair + 1].astype(jnp.float32)
+        lanes = pl.ds(pair * 128, 128)
+        att_ref[:half, lanes] = jnp.where(first, even, pltpu.roll(odd, HEAD_DIM, 1)).astype(low)
+        att_ref[half:, lanes] = jnp.where(first, pltpu.roll(even, HEAD_DIM, 1), odd).astype(low)
+    hidden = hidden_ref[...].astype(jnp.float32)
+    alpha_attn = alpha_attn_ref[...]
+    alpha_mlp = alpha_mlp_ref[...]
+    loads[0].wait()
+    branch = dot_nn(att_ref[...], w_out[...])
+    branch_scale = rms_scale(branch)
+    branch_normed = branch * branch_scale
+    mixed = hidden + alpha_attn * (branch_normed - hidden)
+    middle_scale = rms_scale(mixed)
+    middle = mixed * middle_scale
+    middle_low = middle.astype(low)
+    mid_own[0] = middle_low[:half]
+    mid_own[1] = middle_low[half:]
+    gather.start()
+
+    for load in loads[1:]:
+        load.wait()
+    steps = w_up.shape[1] // FF_STEP
+    acc[...] = jnp.zeros_like(acc)
+
+    def forward(step, carry):
+        cols = pl.ds(pl.multiple_of(step * FF_STEP, FF_STEP), FF_STEP)
+        up = dot_nn(middle_low, w_up[:, cols])
+        gate = dot_nn(middle_low, w_gate[:, cols])
+        up_raw[:, cols] = up
+        gate_raw[:, cols] = gate
+        scaled = gate * s_gate_ref[:, cols]
+        inner = up * s_up_ref[:, cols] * (scaled / (1.0 + jnp.exp(-scaled)))
+        acc[...] += dot_nn(inner.astype(low), w_down[cols, :])
+        return carry
+
+    lax.fori_loop(0, steps, forward, 0)
+    gather.line(1)
+    gather.sides(0)
+    mlp = acc[...]
+    mlp_scale = rms_scale(mlp)
+    mlp_normed = mlp * mlp_scale
+    mixed_out = middle + alpha_mlp * (mlp_normed - middle)
+    out_scale = rms_scale(mixed_out)
+    result = mixed_out * out_scale
+    result_ref[...] = result.astype(low)
+    g_mixed = rms_pull(cot_ref[...].astype(jnp.float32), result, out_scale)
+    g_alpha_mlp_ref[...] = jnp.sum(g_mixed * (mlp_normed - middle), axis=0, keepdims=True)
+    g_mlp = rms_pull(g_mixed * alpha_mlp, mlp_normed, mlp_scale).astype(low)
+    g_mlp_ref[...] = g_mlp
+    acc[...] = g_mixed * (1.0 - alpha_mlp)
+
+    def backward(step, carry):
+        cols = pl.ds(pl.multiple_of(step * FF_STEP, FF_STEP), FF_STEP)
+        g_inner = dot_nt(g_mlp, w_down[cols, :])
+        s_up = s_up_ref[:, cols]
+        s_gate = s_gate_ref[:, cols]
+        scaled = gate_raw[:, cols] * s_gate
+        sigmoid = 1.0 / (1.0 + jnp.exp(-scaled))
+        g_up = g_inner * (scaled * sigmoid) * s_up
+        slope = sigmoid * (1.0 + scaled * (1.0 - sigmoid))
+        g_gate = g_inner * (up_raw[:, cols] * s_up) * slope * s_gate
+        acc[...] += dot_nt(g_up.astype(low), w_up[:, cols]) + dot_nt(
+            g_gate.astype(low), w_gate[:, cols]
+        )
+        return carry
+
+    lax.fori_loop(0, steps // 2, backward, 0)
+    gather.line(2)
+    gather.sides(1)
+    lax.fori_loop(steps // 2, steps, backward, 0)
+    g_pre = rms_pull(acc[...], middle, middle_scale)
+    g_res_ref[...] = g_pre * (1.0 - alpha_attn)
+    g_alpha_attn_ref[...] = jnp.sum(g_pre * (branch_normed - hidden), axis=0, keepdims=True)
+    g_branch = rms_pull(g_pre * alpha_attn, branch_normed, branch_scale).astype(low)
+    g_branch_ref[...] = g_branch
+    g_att = dot_nt(g_branch, w_out[...]).astype(low).astype(jnp.float32)
+    for pair in range(GROUP // 2):
+        lower = g_att[:half, pair * 128 : (pair + 1) * 128]
+        upper = g_att[half:, pair * 128 : (pair + 1) * 128]
+        g_send[2 * pair] = jnp.where(first, lower, pltpu.roll(upper, HEAD_DIM, 1)).astype(low)
+        g_send[2 * pair + 1] = jnp.where(first, pltpu.roll(lower, HEAD_DIM, 1), upper).astype(low)
+    back = Swap(g_send, grad_head_ref, back_sems.at[0], back_sems.at[1])
+    back.start()
+    gather.line(3)
+    gather.sides(2)
+    gather.sides(3)
+    gather.finish()
+    back.wait()
+
+
+ANY_SPEC = pl.BlockSpec(memory_space=pl.ANY)
+
+
+def middle_block(packed, hidden, cot, w_out, w_up, w_gate, w_down, s_up, s_gate, alpha_attn, alpha_mlp):
+    rows, width = hidden.shape
+    ff = w_up.shape[1]
+    low, f32 = jnp.bfloat16, jnp.float32
+    shape = jax.ShapeDtypeStruct
+    return pl.pallas_call(
+        middle_kernel,
+        out_shape=[
+            shape((rows, width), low),
+            shape((rows, width), f32),
+            shape(packed.shape, low),
+            shape((2 * GROUP, rows // 2, width), low),
+            shape((rows, width), low),
+            shape((rows, width), low),
+            shape((rows, width), low),
+            shape((1, width), f32),
+            shape((1, width), f32),
+        ],
+        in_specs=[VMEM_SPEC] * 3 + [ANY_SPEC] * 4 + [VMEM_SPEC] * 4,
+        out_specs=[VMEM_SPEC] * 9,
+        scratch_shapes=[
+            pltpu.VMEM(w_out.shape, low),
+            pltpu.VMEM(w_up.shape, low),
+            pltpu.VMEM(w_gate.shape, low),
+            pltpu.VMEM(w_down.shape, low),
+            pltpu.VMEM((rows, ff), f32),
+            pltpu.VMEM((rows, ff), f32),
+            pltpu.VMEM((2, rows // 2, width), low),
+            pltpu.VMEM(packed.shape, low),
+            pltpu.VMEM(packed.shape, low),
+            pltpu.VMEM((rows, width), f32),
+            pltpu.SemaphoreType.DMA((4,)),
+            pltpu.SemaphoreType.DMA((2, GROUP)),
+            pltpu.SemaphoreType.DMA((2, GROUP)),
+        ]
+        + gather_scratch(),
+        compiler_params=comm_params(1),
+        name="middle_block",
+    )(
+        packed,
+        hidden,
+        cot,
+        w_out,
+        w_up,
+        w_gate,
+        w_down,
+        s_up[None],
+        s_gate[None],
+        alpha_attn[None],
+        alpha_mlp[None],
+    )
+
+
 SMEM_SPEC = pl.BlockSpec(memory_space=pltpu.SMEM)
 
 
 def split_three(column):
-    high = column.astype(jnp.bfloat16)
-    rest = column - high.astype(jnp.float32)
-    mid = rest.astype(jnp.bfloat16)
-    low = (rest - mid.astype(jnp.float32)).astype(jnp.bfloat16)
-    return [high, mid, low]
+    high = lax.reduce_precision(column, 8, 7)
+    rest = column - high
+    mid = lax.reduce_precision(rest, 8, 7)
+    return [part.astype(jnp.bfloat16) for part in (high, mid, rest - mid)]
 
 
 def widened(matrix, columns):
@@ -789,32 +1063,32 @@
     )(first_block, scaled_queries, keys, widened(values, [ones]), start_of[:, None])
     attended_head_low = attended_head.astype(low)
 
-    attended_low = unpack_rows(swap_group(pack_stream(attended_head_low), 1)).reshape(
-        tok_rows, model_width
-    )
-    branch = dot_nn(attended_low, w_out)
-    middle, pull_attn = jax.vjp(residual_mix, hidden_f, branch, alpha_attn)
-    middle_low = middle.astype(low)
-    up_raw = dot_nn(middle_low, w_up)
-    gate_raw = dot_nn(middle_low, w_gate)
-    inner_low = gated_inner(up_raw, gate_raw, s_up, s_gate).astype(low)
-    mlp_raw = dot_nn(inner_low, w_down)
-    result, pull_out = jax.vjp(residual_mix, middle, mlp_raw, alpha_mlp)
-    grad_middle, grad_mlp, grad_alpha_mlp = pull_out(cotangent[0, 0].astype(jnp.float32))
-    grad_mlp_low = grad_mlp.astype(low)
-    grad_inner = dot_nt(grad_mlp_low, w_down)
-    _, pull_inner = jax.vjp(lambda u, g: gated_inner(u, g, s_up, s_gate), up_raw, gate_raw)
-    grad_up_raw, grad_gate_raw = pull_inner(grad_inner)
-    grad_middle = (
-        grad_middle
-        + dot_nt(grad_up_raw.astype(low), w_up)
-        + dot_nt(grad_gate_raw.astype(low), w_gate)
-    )
-    grad_hidden, grad_branch, grad_alpha_attn = pull_attn(grad_middle)
-    branch_low = grad_branch.astype(low)
-    grad_att_low = dot_nt(branch_low, w_out).astype(low)
-
-    grad_head = unpack_stream(swap_group(pack_rows(grad_att_low), 2))
+    (
+        result,
+        grad_hidden,
+        grad_packed,
+        middle_all,
+        grad_mlp_low,
+        attended_low,
+        branch_low,
+        grad_alpha_attn,
+        grad_alpha_mlp,
+    ) = middle_block(
+        pack_stream(attended_head_low),
+        hidden,
+        cotangent[0, 0],
+        w_out,
+        w_up,
+        w_gate,
+        w_down,
+        s_up,
+        s_gate,
+        alpha_attn,
+        alpha_mlp,
+    )
+    middle_all = middle_all.reshape(length, model_width)
+
+    grad_head = unpack_stream(grad_packed)
     delta = jnp.sum(grad_head.astype(jnp.float32) * attended_head, axis=1, keepdims=True)
     minus = [-ones] * 3
     dq, dk, dv = pl.pallas_call(
@@ -854,9 +1128,7 @@
         + dot_nt(home_part(2), w_value)
     )
 
-    middle_all = all_gather_group(middle_low, 4)
     mlp_all = all_gather_group(grad_mlp_low, 5)
-    branch_all = all_gather_group(branch_low, 6)
     ff_part = w_up.shape[1] // (2 * GROUP)
     ff_half = w_up.shape[1] // 2
 
@@ -880,7 +1152,7 @@
     part_up = dot_tn(middle_all, g_up.astype(low))
     part_gate = dot_tn(middle_all, g_gate.astype(low))
     part_qkv = dot_tn(hidden_all, raw_low)
-    part_out = dot_tn(attended_head_low, branch_all)
+    part_out = dot_tn(attended_low, branch_low)
 
     part_wide = jnp.concatenate(
         [part_up, part_gate, part_qkv, jnp.zeros((model_width, 64), jnp.float32)], axis=1
@@ -893,13 +1165,11 @@
     def other(array, size, axis=0):
         return lax.dynamic_slice_in_dim(array, (1 - dp) * size, size, axis)
 
-    got_wide, got_down, got_out = swap_dp(
-        [other(part_wide, half_width).astype(low), other(part_down, ff_part).astype(low), part_out.astype(low)],
-        7,
+    got_wide, got_down = swap_dp(
+        [other(part_wide, half_width).astype(low), other(part_down, ff_part).astype(low)], 7
     )
     grad_down = mine(part_down, ff_part) + got_down
     wide = (mine(part_wide, half_width) + got_wide).astype(low)
-    out_rows = part_out + got_out
     wide = wide.reshape(GROUP, half_width // GROUP, -1)
     got = swap_group(wide, 8)
     grad_up = jnp.concatenate(
@@ -918,17 +1188,12 @@
         .astype(jnp.float32)
         for i in range(3)
     )
-    out_all = lax.all_gather(out_rows, "blk", axis=0, tiled=True)
     rows_out = model_width // (2 * GROUP)
-    grad_out = lax.dynamic_slice_in_dim(out_all, (dp * GROUP + b) * rows_out, rows_out, 0)
+    grad_out = lax.psum_scatter(part_out, ("dp", "blk"), scatter_dimension=0, tiled=True)
 
     def vector_rows(vector):
         rows = vector.reshape(2 * GROUP, -1)
         return jnp.pad(rows, ((0, 0), (0, 128 - rows.shape[1])))
-
-    def placed(part, total):
-        full = jnp.zeros((total,), jnp.float32)
-        return full, part
 
     s_full = jnp.zeros((model_width,), jnp.float32)
     s_full = lax.dynamic_update_slice_in_dim(s_full, grad_s_qk, head_col, 0)
@@ -943,8 +1208,8 @@
             vector_rows(s_full),
             vector_rows(ff_full(g_s_up)),
             vector_rows(ff_full(g_s_gate)),
-            vector_rows(grad_alpha_attn),
-            vector_rows(grad_alpha_mlp),
+            vector_rows(grad_alpha_attn[0]),
+            vector_rows(grad_alpha_mlp[0]),
         ],
         axis=1,
     )
@@ -952,7 +1217,7 @@
     small = jnp.sum(swap_all(small, 9), axis=0)
     mean_alpha = 0.5 * (jnp.mean(alpha_attn) + jnp.mean(alpha_mlp))
     return (
-        result.astype(low)[None, None],
+        result[None, None],
         input_grad[None, None],
         grad_query,
         grad_key,

time: 480 us -> 370 us (0.77)
  the two profiles are of different devices: /device:TPU:13 before, /device:TPU:0 now
where the time goes in v2:
time: 370 us; the launch traced here: 364 us
  Pallas kernels  239 us (65%)
  other arithmetic  41.3 us (11%)
  local copies, waits for them, and re-layouts  40.5 us (11%)
  matrix products  25.4 us (7%)
  between operations  17.6 us (5%)
    pallas_call x2, Pallas kernels, all_gather_group(): pl.pallas_call(gather_kernel, out_shape=jax.ShapeDtypeStruct((2 * GROUP,...  81.2 us
    pallas_call x1, Pallas kernels, middle_block(): pl.pallas_call(middle_kernel, out_shape=[shape((rows, width), low), shape...  46.4 us
    pallas_call x2, Pallas kernels, swap_group(): pl.pallas_call(swap_group_kernel, out_shape=jax.ShapeDtypeStruct(blocks.s...  38.4 us
    pallas_call x1, Pallas kernels, swap_dp(): pl.pallas_call(functools.partial(swap_dp_kernel, count), out_shape=[jax.S...  29.5 us
    pallas_call x1, Pallas kernels, on_device_heads(): pl.pallas_call(attend_grad_kernel, out_shape=[jax.ShapeDtypeStruct((lengt...  16 us
    pallas_call x1, Pallas kernels, swap_all(): pl.pallas_call(swap_all_kernel, out_shape=jax.ShapeDtypeStruct(blocks.sha...  15.2 us
    pallas_call x1, Pallas kernels, on_device_heads(): pl.pallas_call(attend_kernel, out_shape=[jax.ShapeDtypeStruct((length, HE...  12.6 us
    dot_general x5, matrix products, dot_tn(): lax.dot_general(left, right, (((0,), (0,)), ((), ())), preferred_element_...  9.98 us
  transfers between devices with their start and end apart: 1, of which 0 were waited for; matrix products, arithmetic and copies ran while one was open for 22% of the time, Pallas kernels for 40%

profile of v2, /device:TPU:0, one launch (start us, length us, event | category | flops | bytes accessed | tf_op | source)
XLA Modules:
  0.0 364.2 jit_solution(12936772783350774519)
XLA Ops:
  9.3 34.1 %gather_group.2 = bf16[32,64,1024]{2,1,0:T(8,128)(2,1)} custom-call(bf16[2,64,1024]{2,1,0:T(8,128)(2,1)} %bitcast.125), custom_call_target="tpu_custom_call" | custom-call | tf_op jit(solution)/shard_map/gather_group/pallas_call | solution.py:523
  45.5 3.6 %convolution_bitcast_fusion = f32[2048,192]{1,0:T(8,128)S(1)} fusion(bf16[2048,1024]{1,0:T(8,128)(2,1)} %bitcast.114, bf16[1024,64]{1,0:T(8,128)(2,1)S(1)} %get-tuple-element.111, bf16[1024,64]{1,0:T(8,128)(2,1)S(1)} %get-tuple-element.112, bf16[1024,64]{1,0:T(8,128)(2,1)S(1)} %constant_dynamic-slice_fusion.8), kind=kOutput, calls=%fused_computation.1 | convolution fusion | flops 806486016 | bytes 6160384 | tf_op jit(solution)/shard_map/dot_general | solution.py:644
  55.8 12.6 %attend.1 = (f32[2048,64]{1,0:T(8,128)}, f32[2048,1]{1,0:T(8,128)}) custom-call(s32[8]{0:T(128)} %get-tuple-element.110.first_ref, bf16[2048,64]{1,0:T(8,128)(2,1)} %get-tuple-element.73.q_ref, bf16[2048,64]{1,0:T(8,128)(2,1)} %multiply_convert_fusion.6.k_ref, bf16[2048,128]{1,0:T(8,128)(2,1)} %get-tuple-element.92.v_ref, s32[2048,1]{1,0:T(8,128)} %copy.69.start_ref), custom_call_target="tpu_custom_call" | custom-call | tf_op jit(solution)/shard_map/attend/pallas_call | solution.py:1053
  70.6 46.4 %middle_block.1 = (bf16[128,1024]{1,0:T(8,128)(2,1)}, f32[128,1024]{1,0:T(8,128)}, bf16[16,64,128]{2,1,0:T(8,128)(2,1)}, bf16[32,64,1024]{2,1,0:T(8,128)(2,1)}, ...) custom-call(bf16[16,64,128]{2,1,0:T(8,128)(2,1)} %pad_maximum_fusion, ...), custom_call_target="tpu_custom_call" | custom-call | tf_op jit(solution)/shard_map/middle_block/pallas_call | solution.py:899
  117.0 3.7 %fusion.67 = f32[1024,1024]{1,0:T(8,128)} fusion(bf16[128,1024]{1,0:T(8,128)(2,1)} %get-tuple-element.42, bf16[128,1024]{1,0:T(8,128)(2,1)} %get-tuple-element.43), kind=kOutput, calls=%fused_computation.169 | convolution fusion | flops 268435456 | bytes 4718592 | tf_op jit(solution)/shard_map/dot_general | solution.py:640
  127.8 2.2 constant_dynamic-slice_fusion.1
  130.0 1.9 constant_dynamic-slice_fusion.5
  136.4 1.7 reduce-precision_convert_fusion
  138.2 3.0 fusion.27.q_ref
  141.2 1.6 fusion.31.g_ref
  142.9 16.0 %attend_grad.1 = (f32[2048,128]{1,0:T(8,128)}, f32[2048,128]{1,0:T(8,128)}, f32[2048,128]{1,0:T(8,128)}) custom-call(s32[8]{0:T(128)} %get-tuple-element.109.last_ref, bf16[2048,128]{1,0:T(8,128)(2,1)} %fusion.27.q_ref, bf16[2048,128]{1,0:T(8,128)(2,1)} %fusion.14.k_ref, bf16[2048,128]{1,0:T(8,128)(2,1)} %get-tuple-element.91.v_ref, ...), custom_call_target="tpu_custom_call" | custom-call | tf_op jit(solution)/shard_map/attend_grad/pallas_call | solution.py:1094
  160.2 2.9 multiply_reduce_fusion.2
  163.2 1.9 fusion.3
  166.6 1.9 rev.11
  168.5 2.5 pad_maximum_fusion.1.blocks
  171.0 20.5 %swap_group.2 = bf16[16,64,384]{2,1,0:T(8,128)(2,1)} custom-call(bf16[16,64,384]{2,1,0:T(8,128)(2,1)} %pad_maximum_fusion.1.blocks), custom_call_target="tpu_custom_call" | custom-call | tf_op jit(solution)/shard_map/swap_group/pallas_call | solution.py:551
  194.4 1.9 copy.73
  196.3 1.9 copy.74
  198.2 1.9 copy.75
  200.2 47.1 %gather_group.3 = bf16[32,64,1024]{2,1,0:T(8,128)(2,1)} custom-call(bf16[2,64,1024]{2,1,0:T(8,128)(2,1)} %bitcast.137), custom_call_target="tpu_custom_call" | custom-call | tf_op jit(solution)/shard_map/gather_group/pallas_call | solution.py:523
  247.4 3.7 %fusion.47 = f32[2048,256]{1,0:T(8,128)S(1)} fusion(bf16[2048,1024]{1,0:T(8,128)(2,1)} %bitcast.153, bf16[1024,128]{1,0:T(8,128)(2,1)} %get-tuple-element.65, bf16[1024,128]{1,0:T(8,128)(2,1)S(1)} %copy-done.28), kind=kOutput, calls=%fused_computation.91 | convolution fusion | flops 1074790400 | bytes 6815744 | tf_op jit(solution)/shard_map/dot_general | solution.py:644
  253.5 2.5 multiply_reduce_fusion
  259.3 1.8 convolution_bitcast_fusion.1
  264.3 1.7 copy-done.3
  266.9 29.5 %swap_dp.1 = (bf16[512,768]{1,0:T(8,128)(2,1)}, bf16[128,1024]{1,0:T(8,128)(2,1)}) custom-call(bf16[512,768]{1,0:T(8,128)(2,1)} %dynamic-slice_convert_fusion.refs_0_, bf16[128,1024]{1,0:T(8,128)(2,1)} %dynamic-slice_convert_fusion.1.refs_1_), custom_call_target="tpu_custom_call" | custom-call | tf_op jit(solution)/shard_map/swap_dp/pallas_call | solution.py:580
  296.5 2.7 add_convert_fusion
  299.2 17.9 %swap_group.3 = bf16[16,32,768]{2,1,0:T(8,128)(2,1)} custom-call(bf16[16,32,768]{2,1,0:T(8,128)(2,1)} %bitcast.118), custom_call_target="tpu_custom_call" | custom-call | tf_op jit(solution)/shard_map/swap_group/pallas_call | solution.py:551
  317.1 1.9 convert_bitcast_fusion
  326.5 15.2 %swap_all.1 = f32[32,8,128]{2,1,0:T(8,128)} custom-call(f32[32,8,128]{2,1,0:T(8,128)} %pad.42.blocks), custom_call_target="tpu_custom_call" | custom-call | tf_op jit(solution)/shard_map/swap_all/pallas_call | solution.py:618
  346.2 2.1 convert_add_fusion
  348.3 1.9 convolution_add_fusion.2
  351.8 1.6 fusion
  (159 shorter events, 54.7 us)
Async XLA Ops:
  7.2 36.2 %copy-start = (bf16[1024,1024]{1,0:T(8,128)(2,1)S(1)}, bf16[1024,1024]{1,0:T(8,128)(2,1)}, u32[]{:S(2)}) copy-start(bf16[1024,1024]{1,0:T(8,128)(2,1)} %param.18) | copy-start | bytes 6291460
  7.2 347.8 %reduce-scatter.2.cloned.1.call-start = ((), (), s32[]{:S(2)}) async-start(), calls=%async_computation.1 | async-start | bytes 4325376 | tf_op jit(solution)/shard_map/reduce_scatter | solution.py:1192
  49.2 2.1 copy-start.1
  120.7 2.0 copy-start.17
  122.6 1.8 copy-start.6
  125.8 6.9 %copy-start.16 = (f32[2048,1]{1,0:T(8,128)S(1)}, f32[2048,1]{1,0:T(8,128)}, u32[]{:S(2)}) copy-start(f32[2048,1]{1,0:T(8,128)} %get-tuple-element.34) | copy-start | bytes 24580
  135.4 2.8 copy-start.4
  138.2 3.1 copy-start.14
  138.2 3.0 copy-start.15
  142.9 17.3 %copy-start.2 = (f32[2048,192]{1,0:T(8,128)S(1)}, f32[2048,192]{1,0:T(8,128)}, u32[]{:S(2)}) copy-start(f32[2048,192]{1,0:T(8,128)} %copy-done.1) | copy-start | bytes 4718596
  160.1 3.0 copy-start.9
  160.2 3.0 copy-start.10
  200.2 47.2 %copy-start.28 = (bf16[1024,128]{1,0:T(8,128)(2,1)S(1)}, bf16[1024,128]{1,0:T(8,128)(2,1)}, u32[]{:S(2)}) copy-start(bf16[1024,128]{1,0:T(8,128)(2,1)} %get-tuple-element.64) | copy-start | bytes 786436
  247.4 3.7 %copy-start.8 = (bf16[32,64,1024]{2,1,0:T(8,128)(2,1)S(1)}, bf16[32,64,1024]{2,1,0:T(8,128)(2,1)}, u32[]{:S(2)}) copy-start(bf16[32,64,1024]{2,1,0:T(8,128)(2,1)} %gather_group.3) | copy-start | bytes 12582916
  247.4 3.7 %copy-start.22 = (bf16[128,1024]{1,0:T(8,128)(2,1)S(1)}, bf16[128,1024]{1,0:T(8,128)(2,1)}, u32[]{:S(2)}) copy-start(bf16[128,1024]{1,0:T(8,128)(2,1)} %get-tuple-element.62) | copy-start | bytes 786436
  247.4 3.7 %copy-start.23 = (bf16[128,1024]{1,0:T(8,128)(2,1)S(1)}, bf16[128,1024]{1,0:T(8,128)(2,1)}, u32[]{:S(2)}) copy-start(bf16[128,1024]{1,0:T(8,128)(2,1)} %get-tuple-element.63) | copy-start | bytes 786436
  251.1 1.4 copy-start.26
  251.1 2.3 copy-start.33
  256.0 3.3 copy-start.7
  264.3 1.7 copy-start.3
  317.1 5.7 %copy-start.11 = (bf16[16,32,768]{2,1,0:T(8,128)(2,1)S(1)}, bf16[16,32,768]{2,1,0:T(8,128)(2,1)}, u32[]{:S(2)}) copy-start(bf16[16,32,768]{2,1,0:T(8,128)(2,1)} %swap_group.3) | copy-start | bytes 2359300
  319.2 4.6 %copy-start.32 = (f32[1,1024]{1,0:T(1,128)S(1)}, f32[1,1024]{1,0:T(1,128)}, u32[]{:S(2)}) copy-start(f32[1,1024]{1,0:T(1,128)} %get-tuple-element.45) | copy-start | bytes 12292
  320.0 4.5 %copy-start.31 = (f32[1,1024]{1,0:T(1,128)S(1)}, f32[1,1024]{1,0:T(1,128)}, u32[]{:S(2)}) copy-start(f32[1,1024]{1,0:T(1,128)} %get-tuple-element.46) | copy-start | bytes 12292
  321.9 19.9 %copy-start.29 = (f32[1024]{0:T(1024)S(1)}, f32[1024]{0:T(1024)}, u32[]{:S(2)}) copy-start(f32[1024]{0:T(1024)} %param.28) | copy-start | bytes 12292
  321.9 20.5 %copy-start.30 = (f32[1024]{0:T(1024)S(1)}, f32[1024]{0:T(1024)}, u32[]{:S(2)}) copy-start(f32[1024]{0:T(1024)} %param.29) | copy-start | bytes 12292
  322.0 24.2 %copy-start.24 = (bf16[128,1024]{1,0:T(8,128)(2,1)S(1)}, bf16[128,1024]{1,0:T(8,128)(2,1)}, u32[]{:S(2)}) copy-start(bf16[128,1024]{1,0:T(8,128)(2,1)} %get-tuple-element.44) | copy-start | bytes 786436
  322.8 25.5 %copy-start.18 = (bf16[128,16,64]{0,2,1:T(8,128)(2,1)S(1)}, bf16[128,16,64]{0,2,1:T(8,128)(2,1)}, u32[]{:S(2)}) copy-start(bf16[128,16,64]{0,2,1:T(8,128)(2,1)} %copy.73) | copy-start | bytes 786436
  346.2 4.0 %copy-start.12 = (bf16[1024,1024]{1,0:T(8,128)(2,1)S(1)}, bf16[1024,1024]{1,0:T(8,128)(2,1)}, u32[]{:S(2)}) copy-start(bf16[1024,1024]{1,0:T(8,128)(2,1)} %param.19) | copy-start | bytes 6291460
  346.2 4.0 %copy-start.19 = (bf16[128,16,64]{0,2,1:T(8,128)(2,1)S(1)}, bf16[128,16,64]{0,2,1:T(8,128)(2,1)}, u32[]{:S(2)}) copy-start(bf16[128,16,64]{0,2,1:T(8,128)(2,1)} %copy.74) | copy-start | bytes 786436
  350.2 1.6 copy-start.13
  350.2 1.6 copy-start.20
  351.8 3.3 copy-start.25
  (3 other events, 3.5 us)
Sparse Core Ops, SparseCore 0:
  120.8 143.5 reduce-scatter.1

commit v3 on v2

--- a/solution.py
+++ b/solution.py
@@ -477,11 +477,28 @@
                 def _():
                     one(self.z + distance, half)
 
-    def finish(self):
+    def from_sib(self, distance):
+        def one(z):
+            for half in (0, 1):
+                for y in (0, 1):
+                    self.to_sib(z, y, 1 - self.c, half).wait_recv()
+
+        if distance == 0:
+            one(self.z)
+        else:
+
+            @pl.when(self.z - distance >= 0)
+            def _():
+                one(self.z - distance)
+
+            @pl.when(self.z + distance <= 3)
+            def _():
+                one(self.z + distance)
+
+    def drain(self):
         for half in (0, 1):
             for z in range(4):
                 for y in (0, 1):
-                    self.to_sib(z, y, 1 - self.c, half).wait_recv()
                     self.to_sib(z, y, self.c, half).wait_send()
                 self.across(z, self.y, half).wait_send()
 
@@ -493,23 +510,14 @@
                 def _():
                     self.along(z, half, self.down, False, True).wait_send()
 
+    def finish(self):
+        for distance in range(4):
+            self.from_sib(distance)
+        self.drain()
+
 
 def gather_scratch():
     return [pltpu.SemaphoreType.DMA((Gather.SEMAPHORES,)) for _ in range(2)]
-
-
-def gather_kernel(own, out, send, recv):
-    gather = Gather(own, out, send, recv)
-    greet(gather.partners())
-    gather.start()
-    gather.line(1)
-    gather.sides(0)
-    gather.line(2)
-    gather.sides(1)
-    gather.line(3)
-    gather.sides(2)
-    gather.sides(3)
-    gather.finish()
 
 
 def comm_params(collective_id):
@@ -518,120 +526,6 @@
     )
 
 
-def all_gather_group(rows, collective_id):
-    tok_rows, width = rows.shape
-    gathered = pl.pallas_call(
-        gather_kernel,
-        out_shape=jax.ShapeDtypeStruct((2 * GROUP, tok_rows // 2, width), rows.dtype),
-        in_specs=[VMEM_SPEC],
-        out_specs=VMEM_SPEC,
-        scratch_shapes=gather_scratch(),
-        compiler_params=comm_params(collective_id),
-        name="gather_group",
-    )(rows.reshape(2, tok_rows // 2, width))
-    return gathered.reshape(GROUP * tok_rows, width)
-
-
-def swap_group_kernel(blocks, out, send, recv):
-    dp, b = here()
-    greet([(dp, (b + step) % GROUP) for step in range(1, GROUP)])
-    copies = []
-    for step in range(1, GROUP):
-        target = (b + step) % GROUP
-        copies.append(
-            remote(blocks.at[target], out.at[b], send.at[step], recv.at[step], (dp, target))
-        )
-        copies[-1].start()
-    out[b] = blocks[b]
-    for copy in copies:
-        copy.wait()
-
-
-def swap_group(blocks, collective_id):
-    return pl.pallas_call(
-        swap_group_kernel,
-        out_shape=jax.ShapeDtypeStruct(blocks.shape, blocks.dtype),
-        in_specs=[VMEM_SPEC],
-        out_specs=VMEM_SPEC,
-        scratch_shapes=[
-            pltpu.SemaphoreType.DMA((GROUP,)),
-            pltpu.SemaphoreType.DMA((GROUP,)),
-        ],
-        compiler_params=comm_params(collective_id),
-        name="swap_group",
-    )(blocks)
-
-
-def swap_dp_kernel(count, *refs):
-    blocks, outs, send, recv = refs[:count], refs[count : 2 * count], refs[-2], refs[-1]
-    dp, b = here()
-    greet([(1 - dp, b)])
-    copies = [
-        remote(blocks[i], outs[i], send.at[i], recv.at[i], (1 - dp, b)) for i in range(count)
-    ]
-    for copy in copies:
-        copy.start()
-    for copy in copies:
-        copy.wait()
-
-
-def swap_dp(blocks, collective_id):
-    count = len(blocks)
-    return pl.pallas_call(
-        functools.partial(swap_dp_kernel, count),
-        out_shape=[jax.ShapeDtypeStruct(block.shape, block.dtype) for block in blocks],
-        in_specs=[VMEM_SPEC] * count,
-        out_specs=[VMEM_SPEC] * count,
-        scratch_shapes=[
-            pltpu.SemaphoreType.DMA((count,)),
-            pltpu.SemaphoreType.DMA((count,)),
-        ],
-        compiler_params=comm_params(collective_id),
-        name="swap_dp",
-    )(*blocks)
-
-
-def swap_all_kernel(blocks, out, send, recv):
-    dp, b = here()
-    me = dp * GROUP + b
-    total = 2 * GROUP
-    targets = [(me + step) % total for step in range(1, total)]
-    greet([(target // GROUP, target % GROUP) for target in targets])
-    copies = []
-    for step, target in enumerate(targets):
-        copies.append(
-            remote(
-                blocks.at[target],
-                out.at[me],
-                send.at[step],
-                recv.at[step],
-                (target // GROUP, target % GROUP),
-            )
-        )
-        copies[-1].start()
-    out[me] = blocks[me]
-    for copy in copies:
-        copy.wait()
-
-
-def swap_all(blocks, collective_id):
-    return pl.pallas_call(
-        swap_all_kernel,
-        out_shape=jax.ShapeDtypeStruct(blocks.shape, blocks.dtype),
-        in_specs=[VMEM_SPEC],
-        out_specs=VMEM_SPEC,
-        scratch_shapes=[
-            pltpu.SemaphoreType.DMA((2 * GROUP,)),
-            pltpu.SemaphoreType.DMA((2 * GROUP,)),
-        ],
-        compiler_params=comm_params(collective_id),
-        name="swap_all",
-    )(blocks)
-
-
-ATT = 256
-
-
 def dot_nt(left, right):
     return lax.dot_general(left, right, (((1,), (1,)), ((), ())), preferred_element_type=jnp.float32)
 
@@ -644,63 +538,6 @@
     return jnp.dot(left, right, preferred_element_type=jnp.float32)
 
 
-def attend_kernel(first_ref, q_ref, k_ref, v_ref, start_ref, o_ref, l_ref):
-    length = q_ref.shape[0]
-    for query_block in range(length // ATT):
-        rows = pl.ds(query_block * ATT, ATT)
-        queries = q_ref[rows, :]
-        doc_start = start_ref[rows, :]
-        query_pos = query_block * ATT + lax.broadcasted_iota(jnp.int32, (ATT, ATT), 0)
-        key_lane = lax.broadcasted_iota(jnp.int32, (ATT, ATT), 1)
-
-        def step(key_block, total):
-            base = pl.multiple_of(key_block * ATT, ATT)
-            keys = k_ref[pl.ds(base, ATT), :]
-            values = v_ref[pl.ds(base, ATT), :]
-            key_pos = base + key_lane
-            allowed = (key_pos <= query_pos) & (key_pos >= doc_start)
-            weights = jnp.where(allowed, jnp.exp(dot_nt(queries, keys)), 0.0)
-            return total + dot_nn(weights.astype(jnp.bfloat16), values)
-
-        total = lax.fori_loop(
-            first_ref[query_block], query_block + 1, step, jnp.zeros((ATT, 128), jnp.float32)
-        )
-        row_sum = total[:, HEAD_DIM : HEAD_DIM + 1]
-        o_ref[rows, :] = total[:, :HEAD_DIM] / row_sum
-        l_ref[rows, :] = jnp.log(row_sum)
-
-
-def attend_grad_kernel(last_ref, q_ref, k_ref, v_ref, g_ref, start_ref, dq_ref, dk_ref, dv_ref):
-    length = q_ref.shape[0]
-    dq_ref[...] = jnp.zeros_like(dq_ref)
-    key_row = lax.broadcasted_iota(jnp.int32, (ATT, ATT), 0)
-    query_lane = lax.broadcasted_iota(jnp.int32, (ATT, ATT), 1)
-    for key_block in range(length // ATT):
-        rows = pl.ds(key_block * ATT, ATT)
-        keys = k_ref[rows, :]
-        values = v_ref[rows, :]
-        key_pos = key_block * ATT + key_row
-
-        def step(query_block, carried):
-            dk, dv = carried
-            base = pl.multiple_of(query_block * ATT, ATT)
-            queries = q_ref[pl.ds(base, ATT), :]
-            grads = g_ref[pl.ds(base, ATT), :]
-            doc_start = start_ref[pl.ds(query_block, 1), :]
-            allowed = (key_pos <= base + query_lane) & (key_pos >= doc_start)
-            weights = jnp.where(allowed, jnp.exp(dot_nt(keys, queries)), 0.0)
-            slopes = (weights * dot_nt(values, grads)).astype(jnp.bfloat16)
-            dv = dv + dot_nn(weights.astype(jnp.bfloat16), grads)
-            dk = dk + dot_nn(slopes, queries)
-            dq_ref[pl.ds(base, ATT), :] += dot_tn(slopes, keys)
-            return dk, dv
-
-        zero = jnp.zeros((ATT, 128), jnp.float32)
-        dk, dv = lax.fori_loop(key_block, last_ref[key_block], step, (zero, zero))
-        dk_ref[rows, :] = dk
-        dv_ref[rows, :] = dv
-
-
 FF_STEP = 512
 
 
@@ -721,21 +558,28 @@
 
 
 class Swap:
-    def __init__(self, blocks, out, send, recv):
-        self.blocks, self.out = blocks, out
+    def __init__(self, blocks, out, send, recv, own=True):
+        self.blocks, self.out, self.own = blocks, out, own
         dp, self.b = here()
         self.copies = []
         for step in range(1, GROUP):
             target = (self.b + step) % GROUP
             self.copies.append(
-                remote(blocks.at[target], out.at[self.b], send.at[step], recv.at[step], (dp, target))
+                remote(
+                    blocks.at[target] if own else blocks,
+                    out.at[self.b],
+                    send.at[step],
+                    recv.at[step],
+                    (dp, target),
+                )
             )
         self.partners = [(dp, (self.b + step) % GROUP) for step in range(1, GROUP)]
 
     def start(self):
         for copy in self.copies:
             copy.start()
-        self.out[self.b] = self.blocks[self.b]
+        if self.own:
+            self.out[self.b] = self.blocks[self.b]
 
     def wait(self):
         for copy in self.copies:
@@ -947,48 +791,599 @@
 SMEM_SPEC = pl.BlockSpec(memory_space=pltpu.SMEM)
 
 
-def split_three(column):
-    high = lax.reduce_precision(column, 8, 7)
+def own_head(pair, core):
+    shifted = jnp.where(core == 1, pltpu.roll(pair, HEAD_DIM, 1), pair)
+    return jnp.where(half_lanes(pair.shape), shifted, 0.0)
+
+
+def minus_ones(matrix):
+    lane = lax.broadcasted_iota(jnp.int32, matrix.shape, 1)
+    extra = jnp.where(lane < HEAD_DIM + 3, -1.0, 0.0)
+    return jnp.where(lane < HEAD_DIM, matrix, extra).astype(jnp.bfloat16)
+
+
+def project_kernel(
+    own,
+    w_query_hbm,
+    w_key_hbm,
+    w_value_hbm,
+    s_qk_ref,
+    out,
+    qa_ref,
+    ka_ref,
+    va_ref,
+    q_raw_ref,
+    k_raw_ref,
+    gain_ref,
+    w_head,
+    load_sem,
+    send,
+    recv,
+):
+    gather = Gather(own, out, send, recv)
+    window = pl.ds(pl.multiple_of(gather.b // 2 * 128, 128), 128)
+    loads = [
+        pltpu.make_async_copy(
+            source.at[:, window], w_head.at[:, pl.ds(128 * i, 128)], load_sem.at[i]
+        )
+        for i, source in enumerate((w_query_hbm, w_key_hbm, w_value_hbm))
+    ]
+    for load in loads:
+        load.start()
+    greet(gather.partners())
+    gather.start()
+    gain = own_head(jnp.broadcast_to(s_qk_ref[:, window], (8, 128)), gather.c)[:1]
+    gain_ref[...] = gain
+    for load in loads:
+        load.wait()
+    slots = 2 * GROUP // 8
+    half = out.shape[1]
+
+    def project(first_slot):
+        hidden = out[pl.ds(first_slot, slots)].reshape(slots * half, out.shape[2])
+        raw = dot_nn(hidden, w_head[...])
+        rows = pl.ds(pl.multiple_of(first_slot * half, half), slots * half)
+        query, key, value = (
+            own_head(raw[:, 128 * i : 128 * (i + 1)], gather.c) for i in range(3)
+        )
+        q_raw_ref[rows, :] = query
+        k_raw_ref[rows, :] = key
+        count = float(HEAD_DIM)
+        query_scale = lax.rsqrt(jnp.sum(query * query, axis=1, keepdims=True) / count + 1e-06)
+        key_scale = lax.rsqrt(jnp.sum(key * key, axis=1, keepdims=True) / count + 1e-06)
+        query = (query * query_scale * gain).astype(jnp.bfloat16).astype(jnp.float32)
+        qa_ref[rows, :] = (query * (1.0 / math.sqrt(HEAD_DIM))).astype(jnp.bfloat16)
+        ka_ref[rows, :] = minus_ones(key * key_scale * gain)
+        va_ref[rows, :] = minus_ones(value)
+
+    def project_line(distance):
+        def both(z):
+            project(slots * z)
+            project(2 * GROUP - slots - slots * z)
+
+        if distance == 0:
+            both(gather.z)
+        else:
+
+            @pl.when(gather.z - distance >= 0)
+            def _():
+                both(gather.z - distance)
+
+            @pl.when(gather.z + distance <= 3)
+            def _():
+                both(gather.z + distance)
+
+    gather.line(1)
+    gather.sides(0)
+    gather.from_sib(0)
+    project_line(0)
+    gather.line(2)
+    gather.sides(1)
+    gather.from_sib(1)
+    project_line(1)
+    gather.line(3)
+    gather.sides(2)
+    gather.from_sib(2)
+    project_line(2)
+    gather.sides(3)
+    gather.from_sib(3)
+    project_line(3)
+    gather.drain()
+
+
+def project_block(hidden, w_query, w_key, w_value, s_qk):
+    rows, width = hidden.shape
+    length = GROUP * rows
+    low, f32 = jnp.bfloat16, jnp.float32
+    shape = jax.ShapeDtypeStruct
+    return pl.pallas_call(
+        project_kernel,
+        out_shape=[
+            shape((2 * GROUP, rows // 2, width), low),
+            shape((length, 128), low),
+            shape((length, 128), low),
+            shape((length, 128), low),
+            shape((length, 128), f32),
+            shape((length, 128), f32),
+            shape((1, 128), f32),
+        ],
+        in_specs=[VMEM_SPEC] + [ANY_SPEC] * 3 + [VMEM_SPEC],
+        out_specs=[VMEM_SPEC] * 7,
+        scratch_shapes=[pltpu.VMEM((width, 384), low), pltpu.SemaphoreType.DMA((3,))]
+        + gather_scratch(),
+        compiler_params=comm_params(0),
+        name="project_block",
+    )(hidden.reshape(2, rows // 2, width), w_query, w_key, w_value, s_qk[None])
+
+
+def doc_start_of(positions, lengths_ref):
+    start = jnp.zeros_like(positions)
+    end = jnp.int32(0)
+    for doc in range(lengths_ref.shape[1]):
+        end = end + lengths_ref[0, doc]
+        start = start + jnp.where(positions >= end, lengths_ref[0, doc], 0)
+    return start
+
+
+def split_lanes(column, shape):
+    lane = lax.broadcasted_iota(jnp.int32, shape, 1)
+    high = column.astype(jnp.bfloat16).astype(jnp.float32)
     rest = column - high
-    mid = lax.reduce_precision(rest, 8, 7)
-    return [part.astype(jnp.bfloat16) for part in (high, mid, rest - mid)]
-
-
-def widened(matrix, columns):
-    joined = jnp.concatenate([matrix] + columns, axis=1)
-    return jnp.pad(joined, ((0, 0), (0, 128 - joined.shape[1])))
-
-
-def pack_stream(stream):
-    half = stream.shape[0] // 2
-    lower = stream[:half].reshape(GROUP, half // GROUP, -1)
-    upper = stream[half:].reshape(GROUP, half // GROUP, -1)[::-1]
-    return jnp.concatenate([lower, upper], axis=2)
-
-
-def unpack_rows(blocks):
-    width = blocks.shape[2] // 2
-    return jnp.concatenate(
-        [blocks[:, :, :width].transpose(1, 0, 2), blocks[:, :, width:].transpose(1, 0, 2)], axis=0
-    )
-
-
-def pack_rows(rows):
-    half = rows.shape[0] // 2
-    return jnp.concatenate(
-        [
-            rows[:half].reshape(half, GROUP, -1).transpose(1, 0, 2),
-            rows[half:].reshape(half, GROUP, -1).transpose(1, 0, 2),
+    mid = rest.astype(jnp.bfloat16).astype(jnp.float32)
+    last = rest - mid
+    return jnp.where(
+        lane == HEAD_DIM,
+        high,
+        jnp.where(lane == HEAD_DIM + 1, mid, jnp.where(lane == HEAD_DIM + 2, last, 0.0)),
+    )
+
+
+ATT = 512
+
+
+def attend_kernel(lengths_ref, qa_ref, ka_ref, va_ref, o_ref, ql_ref, packed_ref):
+    length = qa_ref.shape[0]
+    half = packed_ref.shape[1]
+    for query_block in range(length // ATT):
+        rows = pl.ds(query_block * ATT, ATT)
+        queries = qa_ref[rows, :]
+        column = query_block * ATT + lax.broadcasted_iota(jnp.int32, (ATT, 1), 0)
+        doc_start = doc_start_of(column, lengths_ref)
+        first_start = doc_start_of(jnp.int32(query_block * ATT), lengths_ref)
+        query_pos = query_block * ATT + lax.broadcasted_iota(jnp.int32, (ATT, ATT), 0)
+        key_lane = lax.broadcasted_iota(jnp.int32, (ATT, ATT), 1)
+
+        def step(key_block, total):
+            base = pl.multiple_of(key_block * ATT, ATT)
+            keys = ka_ref[pl.ds(base, ATT), :]
+            values = va_ref[pl.ds(base, ATT), :]
+            key_pos = base + key_lane
+            allowed = (key_pos <= query_pos) & (key_pos >= doc_start)
+            weights = jnp.where(allowed, jnp.exp(dot_nt(queries, keys)), 0.0)
+            return total + dot_nn(weights.astype(jnp.bfloat16), values)
+
+        total = lax.fori_loop(
+            first_start // ATT, query_block + 1, step, jnp.zeros((ATT, 128), jnp.float32)
+        )
+        row_sum = -total[:, HEAD_DIM : HEAD_DIM + 1]
+        first = half_lanes(total.shape)
+        o_ref[rows, :] = jnp.where(first, total / row_sum, 0.0)
+        extra = split_lanes(jnp.log(row_sum), total.shape)
+        ql_ref[rows, :] = jnp.where(first, queries.astype(jnp.float32), extra).astype(jnp.bfloat16)
+    first = half_lanes((half, 128))
+    for j in range(GROUP):
+        lower = o_ref[j * half : (j + 1) * half, :]
+        upper = o_ref[length - (j + 1) * half : length - j * half, :]
+        packed_ref[j] = jnp.where(first, lower, pltpu.roll(upper, HEAD_DIM, 1)).astype(
+            packed_ref.dtype
+        )
+
+
+def attend(lengths, qa, ka, va, half_rows):
+    length = qa.shape[0]
+    shape = jax.ShapeDtypeStruct
+    return pl.pallas_call(
+        attend_kernel,
+        out_shape=[
+            shape((length, 128), jnp.float32),
+            shape((length, 128), jnp.bfloat16),
+            shape((GROUP, half_rows, 128), jnp.bfloat16),
         ],
-        axis=2,
-    )
-
-
-def unpack_stream(blocks):
-    width = blocks.shape[2] // 2
-    lower = blocks[:, :, :width].reshape(-1, width)
-    upper = blocks[::-1, :, width:].reshape(-1, width)
-    return jnp.concatenate([lower, upper], axis=0)
+        in_specs=[SMEM_SPEC] + [VMEM_SPEC] * 3,
+        out_specs=[VMEM_SPEC] * 3,
+        compiler_params=pltpu.CompilerParams(vmem_limit_bytes=VMEM_LIMIT),
+        name="attend",
+    )(lengths, qa, ka, va)
+
+
+def finish_kernel(
+    lengths_ref,
+    grad_packed,
+    o_ref,
+    ql_ref,
+    ka_ref,
+    va_ref,
+    q_raw_ref,
+    k_raw_ref,
+    gain_ref,
+    hidden_all,
+    mid_all,
+    g_mlp_own,
+    g_res_ref,
+    small_in,
+    s_up_ref,
+    s_gate_ref,
+    w_query_hbm,
+    w_key_hbm,
+    w_value_hbm,
+    w_up_hbm,
+    w_gate_hbm,
+    w_down_hbm,
+    input_grad_ref,
+    g_query_ref,
+    g_key_ref,
+    g_value_ref,
+    g_up_ref,
+    g_gate_ref,
+    g_down_ref,
+    g_s_ref,
+    small_ref,
+    g_mlp_all,
+    ga_ref,
+    dq_ref,
+    dk_ref,
+    dv_ref,
+    raw_low,
+    w_qkv,
+    w_up,
+    w_gate,
+    w_down,
+    back_send,
+    back_in,
+    home,
+    g_cat,
+    inner,
+    wide_own,
+    wide_send,
+    wide_got,
+    wide_blocks,
+    wide_in,
+    qkv_part,
+    down_part,
+    down_send,
+    down_got,
+    small_own,
+    small_got,
+    small_all,
+    s_part,
+    s_send,
+    s_got,
+    load_sem,
+    x_sems,
+    back_sems,
+    wide_sems,
+    small_sems,
+    ag_send,
+    ag_recv,
+):
+    low, f32 = jnp.bfloat16, jnp.float32
+    dp, b = here()
+    length = ql_ref.shape[0]
+    half = g_mlp_own.shape[1]
+    width = hidden_all.shape[2]
+    gather = Gather(g_mlp_own, g_mlp_all, ag_send, ag_recv)
+    twin = (1 - dp, b)
+    part = w_down.shape[0] // 2
+    ff_half = w_up_hbm.shape[1] // 2
+
+    def load(index, source, target):
+        copy = pltpu.make_async_copy(source, target, load_sem.at[index])
+        copy.start()
+        return copy
+
+    loads = []
+    for p in (0, 1):
+        window = pl.ds(pl.multiple_of(p * ff_half + b * part, part), part)
+        place = pl.ds(p * part, part)
+        loads.append(load(3 * p, w_up_hbm.at[:, window], w_up.at[:, place]))
+        loads.append(load(3 * p + 1, w_gate_hbm.at[:, window], w_gate.at[:, place]))
+        loads.append(load(3 * p + 2, w_down_hbm.at[window, :], w_down.at[place, :]))
+    qkv_loads = [
+        load(6 + i, source, w_qkv.at[i])
+        for i, source in enumerate((w_query_hbm, w_key_hbm, w_value_hbm))
+    ]
+
+    def to_twin(index, source, target):
+        copy = remote(source, target, x_sems.at[0, index], x_sems.at[1, index], twin)
+        copy.start()
+        return copy
+
+    back = Swap(back_send, back_in, back_sems.at[0], back_sems.at[1])
+    wide_swap = Swap(wide_blocks, wide_in, wide_sems.at[0], wide_sems.at[1])
+    small_swap = Swap(small_own, small_all, small_sems.at[0], small_sems.at[1], own=False)
+    greet(back.partners + [twin])
+    gather.start()
+
+    first = half_lanes((half, 128))
+    for j in range(GROUP):
+        block = grad_packed[j].astype(f32)
+        for start, grads in (
+            (j * half, jnp.where(first, block, 0.0)),
+            (length - (j + 1) * half, jnp.where(first, pltpu.roll(block, HEAD_DIM, 1), 0.0)),
+        ):
+            rows = pl.ds(start, half)
+            delta = jnp.sum(grads * o_ref[rows, :], axis=1, keepdims=True)
+            ga_ref[rows, :] = (grads + split_lanes(delta, grads.shape)).astype(low)
+    dq_ref[...] = jnp.zeros_like(dq_ref)
+    key_row = lax.broadcasted_iota(jnp.int32, (ATT, ATT), 0)
+    query_lane = lax.broadcasted_iota(jnp.int32, (ATT, ATT), 1)
+    query_row = lax.broadcasted_iota(jnp.int32, (1, ATT), 1)
+    blocks = length // ATT
+    for key_block in range(blocks):
+        rows = pl.ds(key_block * ATT, ATT)
+        keys = ka_ref[rows, :]
+        values = va_ref[rows, :]
+        key_pos = key_block * ATT + key_row
+        dk_ref[rows, :] = jnp.zeros((ATT, 128), f32)
+        dv_ref[rows, :] = jnp.zeros((ATT, 128), f32)
+
+        def step(query_block, carry):
+            base = pl.multiple_of(query_block * ATT, ATT)
+            span = pl.ds(base, ATT)
+            queries = ql_ref[span, :]
+            grads = ga_ref[span, :]
+            doc_start = doc_start_of(base + query_row, lengths_ref)
+            allowed = (key_pos <= base + query_lane) & (key_pos >= doc_start)
+            weights = jnp.where(allowed, jnp.exp(dot_nt(keys, queries)), 0.0)
+            slopes = (weights * dot_nt(values, grads)).astype(low)
+            dv_ref[rows, :] += dot_nn(weights.astype(low), grads)
+            dk_ref[rows, :] += dot_nn(slopes, queries)
+            dq_ref[span, :] += dot_tn(slopes, keys)
+            return carry
+
+        lax.fori_loop(key_block, blocks, step, 0)
+        if key_block == 0:
+            gather.line(1)
+            gather.sides(0)
+        if key_block == 2:
+            gather.line(2)
+            gather.sides(1)
+
+    gain = gain_ref[...]
+    count = float(HEAD_DIM)
+    score_scale = 1.0 / math.sqrt(HEAD_DIM)
+
+    def norm_pull(raw, grad):
+        scale = lax.rsqrt(jnp.sum(raw * raw, axis=1, keepdims=True) / count + 1e-06)
+        normed = raw * scale
+        g_gain = jnp.sum(grad * normed, axis=0, keepdims=True)
+        inside = grad * gain
+        mean = jnp.sum(inside * normed, axis=1, keepdims=True) / count
+        return scale * (inside - normed * mean), g_gain
+
+    g_gain = jnp.zeros((1, 128), f32)
+    wide_first = half_lanes((ATT, 128))
+    for block in range(blocks):
+        rows = pl.ds(block * ATT, ATT)
+        dq = jnp.where(wide_first, dq_ref[rows, :] * score_scale, 0.0)
+        dk = jnp.where(wide_first, dk_ref[rows, :], 0.0)
+        dv = jnp.where(wide_first, dv_ref[rows, :], 0.0)
+        g_query, gain_first = norm_pull(q_raw_ref[rows, :], dq)
+        g_key, gain_second = norm_pull(k_raw_ref[rows, :], dk)
+        g_gain = g_gain + gain_first + gain_second
+        for i, grads in enumerate((g_query, g_key, dv)):
+            raw_low[rows, 128 * i : 128 * (i + 1)] = grads.astype(low)
+    for j in range(GROUP):
+        for i in range(3):
+            lanes = slice(128 * i, 128 * (i + 1))
+            lower = raw_low[j * half : (j + 1) * half, lanes].astype(f32)
+            upper = raw_low[length - (j + 1) * half : length - j * half, lanes].astype(f32)
+            back_send[j, :, lanes] = jnp.where(
+                first, lower, pltpu.roll(upper, HEAD_DIM, 1)
+            ).astype(low)
+    back.start()
+    small_own[...] = small_in[...]
+    small_own[16:17, :] = g_gain
+    small_copy = to_twin(0, small_own, small_got)
+    gather.line(3)
+    gather.sides(2)
+
+    quarter = width // 4
+    for chunk in range(4):
+        lanes = pl.ds(chunk * quarter, quarter)
+        tokens = hidden_all[:, :, lanes].reshape(length, quarter)
+        grads = dot_tn(tokens, raw_low[...])
+        query_key = jnp.where(
+            half_lanes((quarter, 128)), grads[:, :128], pltpu.roll(grads[:, 128:256], HEAD_DIM, 1)
+        )
+        qkv_part[chunk, :, :128] = query_key
+        qkv_part[chunk, :, 128:] = grads[:, 256:]
+    gather.sides(3)
+    gather.finish()
+
+    small_copy.wait()
+    small_own[...] += small_got[...]
+    small_swap.start()
+
+    for copy in loads:
+        copy.wait()
+    windows = [pl.ds(pl.multiple_of(p * ff_half + b * part, part), part) for p in (0, 1)]
+    s_up = jnp.concatenate([s_up_ref[:, window] for window in windows], axis=1)
+    s_gate = jnp.concatenate([s_gate_ref[:, window] for window in windows], axis=1)
+    slots = ATT // half
+
+    def tokens_of(array, step):
+        return array[pl.ds(step * slots, slots)].reshape(ATT, width)
+
+    def recompute(step, sums):
+        rows = pl.ds(pl.multiple_of(step * ATT, ATT), ATT)
+        middle = tokens_of(mid_all, step)
+        up = dot_nn(middle, w_up[...])
+        gate = dot_nn(middle, w_gate[...])
+        g_inner = dot_nt(tokens_of(g_mlp_all, step), w_down[...])
+        scaled = gate * s_gate
+        sigmoid = 1.0 / (1.0 + jnp.exp(-scaled))
+        silu = scaled / (1.0 + jnp.exp(-scaled))
+        up_scaled = up * s_up
+        inner[rows, :] = (up_scaled * silu).astype(low)
+        g_up_scaled = g_inner * silu
+        g_scaled = g_inner * up_scaled * (sigmoid * (1.0 + scaled * (1.0 - sigmoid)))
+        g_cat[rows, : 2 * part] = (g_up_scaled * s_up).astype(low)
+        g_cat[rows, 2 * part :] = (g_scaled * s_gate).astype(low)
+        return (
+            sums[0] + jnp.sum(g_up_scaled * up, axis=0, keepdims=True),
+            sums[1] + jnp.sum(g_scaled * gate, axis=0, keepdims=True),
+        )
+
+    zero_row = jnp.zeros((1, 2 * part), f32)
+    g_s_up, g_s_gate = lax.fori_loop(0, blocks, recompute, (zero_row, zero_row))
+    for p in (0, 1):
+        s_part[p] = jnp.zeros(s_part.shape[1:], f32)
+        s_part[p, 0:1, :] = g_s_up[:, p * part : (p + 1) * part]
+        s_part[p, 1:2, :] = g_s_gate[:, p * part : (p + 1) * part]
+    s_send[...] = s_part[1 - dp]
+    s_copy = to_twin(1, s_send, s_got)
+    for chunk in range(4):
+        lanes = pl.ds(chunk * quarter, quarter)
+        down_part[:, lanes] = dot_tn(inner[...], g_mlp_all[:, :, lanes].reshape(length, quarter))
+    down_send[...] = down_part[pl.ds(pl.multiple_of((1 - dp) * part, part), part), :].astype(low)
+    down_copy = to_twin(2, down_send, down_got)
+
+    def wide_chunk(chunk):
+        lanes = pl.ds(pl.multiple_of(chunk * quarter, quarter), quarter)
+        return dot_tn(mid_all[:, :, lanes].reshape(length, quarter), g_cat[...])
+
+    wide_copies = []
+    for i in (0, 1):
+        chunk = 2 * (1 - dp) + i
+        wide_send[i, :, : 4 * part] = wide_chunk(chunk).astype(low)
+        wide_send[i, :, 4 * part :] = qkv_part[chunk].astype(low)
+        wide_copies.append(to_twin(3 + i, wide_send.at[i], wide_got.at[i]))
+    for i in (0, 1):
+        chunk = 2 * dp + i
+        wide_own[i, :, : 4 * part] = wide_chunk(chunk)
+        wide_own[i, :, 4 * part :] = qkv_part[chunk]
+
+    back.wait()
+    for pair in range(GROUP // 2):
+        for i in range(3):
+            lanes = slice(128 * i, 128 * (i + 1))
+            even = back_in[2 * pair, :, lanes].astype(f32)
+            odd = back_in[2 * pair + 1, :, lanes].astype(f32)
+            place = slice(128 * pair, 128 * (pair + 1))
+            home[i, :half, place] = jnp.where(first, even, pltpu.roll(odd, HEAD_DIM, 1)).astype(low)
+            home[i, half:, place] = jnp.where(first, pltpu.roll(even, HEAD_DIM, 1), odd).astype(low)
+    for copy in qkv_loads:
+        copy.wait()
+    input_grad_ref[...] = (
+        g_res_ref[...]
+        + dot_nt(home[0], w_qkv[0])
+        + dot_nt(home[1], w_qkv[1])
+        + dot_nt(home[2], w_qkv[2])
+    )
+
+    rows_out = width // (2 * GROUP)
+    per_chunk = quarter // rows_out
+    for i in (0, 1):
+        wide_copies[i].wait()
+        total = (wide_own[i] + wide_got[i].astype(f32)).astype(low)
+        for k in range(per_chunk):
+            wide_blocks[i * per_chunk + k] = total[k * rows_out : (k + 1) * rows_out]
+    wide_swap.start()
+    s_copy.wait()
+    g_s_ref[...] = s_part[dp] + s_got[...]
+    down_copy.wait()
+    g_down_ref[...] = down_part[pl.ds(pl.multiple_of(dp * part, part), part), :] + down_got[
+        ...
+    ].astype(f32)
+    small_swap.wait()
+    small_all[b] = small_own[...]
+    small_ref[...] = jnp.sum(small_all[...], axis=0)
+    jsrc = 8 * dp + b // 2
+    small_ref[17:18, :] = small_all[jsrc, 16:17, :]
+    wide_swap.wait()
+    row_first = half_lanes((rows_out, 128))
+    for j in range(GROUP):
+        for p in (0, 1):
+            place = slice(p * ff_half + j * part, p * ff_half + (j + 1) * part)
+            g_up_ref[:, place] = wide_in[j, :, p * part : (p + 1) * part].astype(f32)
+            g_gate_ref[:, place] = wide_in[j, :, (2 + p) * part : (3 + p) * part].astype(f32)
+    for pair in range(GROUP // 2):
+        place = slice(128 * pair, 128 * (pair + 1))
+        even = wide_in[2 * pair, :, 4 * part : 4 * part + 128].astype(f32)
+        odd = wide_in[2 * pair + 1, :, 4 * part : 4 * part + 128].astype(f32)
+        g_query_ref[:, place] = jnp.where(row_first, even, pltpu.roll(odd, HEAD_DIM, 1))
+        g_key_ref[:, place] = jnp.where(row_first, pltpu.roll(even, HEAD_DIM, 1), odd)
+        even = wide_in[2 * pair, :, 4 * part + 128 :].astype(f32)
+        odd = wide_in[2 * pair + 1, :, 4 * part + 128 :].astype(f32)
+        g_value_ref[:, place] = jnp.where(row_first, even, pltpu.roll(odd, HEAD_DIM, 1))
+
+
+def finish_block(inputs, rows, width, ff):
+    low, f32 = jnp.bfloat16, jnp.float32
+    shape, vmem, sems = jax.ShapeDtypeStruct, pltpu.VMEM, pltpu.SemaphoreType.DMA
+    length = GROUP * rows
+    half = rows // 2
+    rows_out = width // (2 * GROUP)
+    part = ff // (2 * GROUP)
+    wide = 4 * part + 256
+    quarter = width // 4
+    return pl.pallas_call(
+        finish_kernel,
+        out_shape=[
+            shape((rows, width), f32),
+            shape((rows_out, width), f32),
+            shape((rows_out, width), f32),
+            shape((rows_out, width), f32),
+            shape((rows_out, ff), f32),
+            shape((rows_out, ff), f32),
+            shape((part, width), f32),
+            shape((8, 128), f32),
+            shape((24, 128), f32),
+        ],
+        in_specs=[SMEM_SPEC] + [VMEM_SPEC] * 15 + [ANY_SPEC] * 6,
+        out_specs=[VMEM_SPEC] * 9,
+        scratch_shapes=[
+            vmem((2 * GROUP, half, width), low),
+            vmem((length, 128), low),
+            vmem((length, 128), f32),
+            vmem((length, 128), f32),
+            vmem((length, 128), f32),
+            vmem((length, 384), low),
+            vmem((3, width, width), low),
+            vmem((width, 2 * part), low),
+            vmem((width, 2 * part), low),
+            vmem((2 * part, width), low),
+            vmem((GROUP, half, 384), low),
+            vmem((GROUP, half, 384), low),
+            vmem((3, rows, width), low),
+            vmem((length, 4 * part), low),
+            vmem((length, 2 * part), low),
+            vmem((2, quarter, wide), f32),
+            vmem((2, quarter, wide), low),
+            vmem((2, quarter, wide), low),
+            vmem((GROUP, rows_out, wide), low),
+            vmem((GROUP, rows_out, wide), low),
+            vmem((4, quarter, 256), f32),
+            vmem((2 * part, width), f32),
+            vmem((part, width), low),
+            vmem((part, width), low),
+            vmem((24, 128), f32),
+            vmem((24, 128), f32),
+            vmem((GROUP, 24, 128), f32),
+            vmem((2, 8, 128), f32),
+            vmem((8, 128), f32),
+            vmem((8, 128), f32),
+            sems((9,)),
+            sems((2, 8)),
+            sems((2, GROUP)),
+            sems((2, GROUP)),
+            sems((2, GROUP)),
+        ]
+        + gather_scratch(),
+        compiler_params=comm_params(2),
+        name="finish_block",
+    )(*inputs)
 
 
 def on_device_heads(
@@ -1008,73 +1403,26 @@
     alpha_attn,
     alpha_mlp,
 ):
-    low = jnp.bfloat16
     model_width = w_query.shape[0]
     tok_rows = tokens.shape[2]
-    length = GROUP * tok_rows
-    dp, b = here()
-    score_scale = 1.0 / math.sqrt(HEAD_DIM)
+    half_rows = tok_rows // 2
     hidden = tokens[0, 0]
-    hidden_f = hidden.astype(jnp.float32)
-    positions = jnp.arange(length, dtype=jnp.int32)
-    doc_ends = jnp.cumsum(lengths[0], dtype=jnp.int32)
-    doc_starts = doc_ends - lengths[0]
-    document = doc_index(positions, doc_ends)
-    member = document[:, None] == jnp.arange(lengths.shape[1], dtype=jnp.int32)[None]
-    start_of = jnp.sum(jnp.where(member, doc_starts[None], 0), axis=1, dtype=jnp.int32)
-    end_of = jnp.sum(jnp.where(member, doc_ends[None], 0), axis=1, dtype=jnp.int32)
-    blocks = length // ATT
-    first_block = start_of[::ATT] // ATT
-    last_block = (end_of[ATT - 1 :: ATT] + ATT - 1) // ATT
-
-    hidden_all = all_gather_group(hidden, 0)
-    head_col = b * HEAD_DIM
-
-    def head_slice(weight):
-        return lax.dynamic_slice_in_dim(weight, head_col, HEAD_DIM, 1)
-
-    gain = lax.dynamic_slice_in_dim(s_qk, head_col, HEAD_DIM, 0)
-    w_head = jnp.concatenate([head_slice(w_query), head_slice(w_key), head_slice(w_value)], axis=1)
-    raw = dot_nn(hidden_all, w_head)
-    query_raw, key_raw, value_raw = (
-        raw[:, :HEAD_DIM],
-        raw[:, HEAD_DIM : 2 * HEAD_DIM],
-        raw[:, 2 * HEAD_DIM :],
-    )
-
-    def scaled_norm(raw_rows, gain_vector):
-        return rms_norm(raw_rows) * gain_vector
-
-    queries = scaled_norm(query_raw, gain).astype(low)
-    keys = scaled_norm(key_raw, gain).astype(low)
-    values = value_raw.astype(low)
-    scaled_queries = queries * jnp.asarray(score_scale, low)
-    ones = jnp.ones((length, 1), low)
-    attended_head, log_total = pl.pallas_call(
-        attend_kernel,
-        out_shape=[
-            jax.ShapeDtypeStruct((length, HEAD_DIM), jnp.float32),
-            jax.ShapeDtypeStruct((length, 1), jnp.float32),
-        ],
-        in_specs=[SMEM_SPEC] + [VMEM_SPEC] * 4,
-        out_specs=[VMEM_SPEC] * 2,
-        compiler_params=pltpu.CompilerParams(vmem_limit_bytes=VMEM_LIMIT),
-        name="attend",
-    )(first_block, scaled_queries, keys, widened(values, [ones]), start_of[:, None])
-    attended_head_low = attended_head.astype(low)
-
+    hidden_all, qa, ka, va, query_raw, key_raw, gain = project_block(
+        hidden, w_query, w_key, w_value, s_qk
+    )
+    attended, ql, packed = attend(lengths, qa, ka, va, half_rows)
     (
         result,
         grad_hidden,
         grad_packed,
         middle_all,
-        grad_mlp_low,
+        grad_mlp,
         attended_low,
         branch_low,
         grad_alpha_attn,
         grad_alpha_mlp,
     ) = middle_block(
-        pack_stream(attended_head_low),
+        packed,
         hidden,
         cotangent[0, 0],
         w_out,
@@ -1086,135 +1434,63 @@
         alpha_attn,
         alpha_mlp,
     )
-    middle_all = middle_all.reshape(length, model_width)
-
-    grad_head = unpack_stream(grad_packed)
-    delta = jnp.sum(grad_head.astype(jnp.float32) * attended_head, axis=1, keepdims=True)
-    minus = [-ones] * 3
-    dq, dk, dv = pl.pallas_call(
-        attend_grad_kernel,
-        out_shape=[jax.ShapeDtypeStruct((length, 128), jnp.float32)] * 3,
-        in_specs=[SMEM_SPEC] + [VMEM_SPEC] * 5,
-        out_specs=[VMEM_SPEC] * 3,
-        compiler_params=pltpu.CompilerParams(vmem_limit_bytes=VMEM_LIMIT),
-        name="attend_grad",
-    )(
-        last_block,
-        widened(scaled_queries, split_three(log_total)),
-        widened(keys, minus),
-        widened(values, minus),
-        widened(grad_head, split_three(delta)),
-        start_of.reshape(blocks, ATT),
-    )
-    grad_queries = dq[:, :HEAD_DIM] * score_scale
-    grad_keys = dk[:, :HEAD_DIM]
-    grad_values = dv[:, :HEAD_DIM]
-    _, pull_query = jax.vjp(scaled_norm, query_raw, gain)
-    grad_query_raw, grad_qk_first = pull_query(grad_queries)
-    _, pull_key = jax.vjp(scaled_norm, key_raw, gain)
-    grad_key_raw, grad_qk_second = pull_key(grad_keys)
-    grad_s_qk = grad_qk_first + grad_qk_second
-    raw_low = jnp.concatenate([grad_query_raw, grad_key_raw, grad_values], axis=1).astype(low)
-    home = swap_group(pack_stream(raw_low), 3)
-    home = unpack_rows(home)
-
-    def home_part(index):
-        return home[:, :, index * HEAD_DIM : (index + 1) * HEAD_DIM].reshape(tok_rows, model_width)
-
-    input_grad = (
-        grad_hidden
-        + dot_nt(home_part(0), w_query)
-        + dot_nt(home_part(1), w_key)
-        + dot_nt(home_part(2), w_value)
-    )
-
-    mlp_all = all_gather_group(grad_mlp_low, 5)
-    ff_part = w_up.shape[1] // (2 * GROUP)
-    ff_half = w_up.shape[1] // 2
-
-    def ff_slice(array, axis):
-        return jnp.concatenate(
-            [
-                lax.dynamic_slice_in_dim(array, b * ff_part, ff_part, axis),
-                lax.dynamic_slice_in_dim(array, ff_half + b * ff_part, ff_part, axis),
-            ],
-            axis=axis,
-        )
-
-    up_part = dot_nn(middle_all, ff_slice(w_up, 1))
-    gate_part = dot_nn(middle_all, ff_slice(w_gate, 1))
-    inner_grad_part = dot_nt(mlp_all, ff_slice(w_down, 0))
-    inner_part, pull_part = jax.vjp(
-        gated_inner, up_part, gate_part, ff_slice(s_up, 0), ff_slice(s_gate, 0)
-    )
-    g_up, g_gate, g_s_up, g_s_gate = pull_part(inner_grad_part)
-    part_down = dot_tn(inner_part.astype(low), mlp_all)
-    part_up = dot_tn(middle_all, g_up.astype(low))
-    part_gate = dot_tn(middle_all, g_gate.astype(low))
-    part_qkv = dot_tn(hidden_all, raw_low)
     part_out = dot_tn(attended_low, branch_low)
-
-    part_wide = jnp.concatenate(
-        [part_up, part_gate, part_qkv, jnp.zeros((model_width, 64), jnp.float32)], axis=1
-    )
-    half_width = model_width // 2
-
-    def mine(array, size, axis=0):
-        return lax.dynamic_slice_in_dim(array, dp * size, size, axis)
-
-    def other(array, size, axis=0):
-        return lax.dynamic_slice_in_dim(array, (1 - dp) * size, size, axis)
-
-    got_wide, got_down = swap_dp(
-        [other(part_wide, half_width).astype(low), other(part_down, ff_part).astype(low)], 7
-    )
-    grad_down = mine(part_down, ff_part) + got_down
-    wide = (mine(part_wide, half_width) + got_wide).astype(low)
-    wide = wide.reshape(GROUP, half_width // GROUP, -1)
-    got = swap_group(wide, 8)
-    grad_up = jnp.concatenate(
-        [got[:, :, i * ff_part : (i + 1) * ff_part].transpose(1, 0, 2).reshape(-1, ff_half) for i in (0, 1)],
-        axis=1,
-    ).astype(jnp.float32)
-    grad_gate = jnp.concatenate(
-        [got[:, :, i * ff_part : (i + 1) * ff_part].transpose(1, 0, 2).reshape(-1, ff_half) for i in (2, 3)],
-        axis=1,
-    ).astype(jnp.float32)
-    base = 4 * ff_part
-    grad_query, grad_key, grad_value = (
-        got[:, :, base + i * HEAD_DIM : base + (i + 1) * HEAD_DIM]
-        .transpose(1, 0, 2)
-        .reshape(-1, model_width)
-        .astype(jnp.float32)
-        for i in range(3)
-    )
+    grad_out = lax.psum_scatter(part_out, ("dp", "blk"), scatter_dimension=0, tiled=True)
+    small = jnp.concatenate(
+        [
+            grad_alpha_attn.reshape(-1, 128),
+            grad_alpha_mlp.reshape(-1, 128),
+            jnp.zeros((8, 128), jnp.float32),
+        ],
+        axis=0,
+    )
+    (
+        input_grad,
+        grad_query,
+        grad_key,
+        grad_value,
+        grad_up,
+        grad_gate,
+        grad_down,
+        grad_scales,
+        small,
+    ) = finish_block(
+        (
+            lengths,
+            grad_packed,
+            attended,
+            ql,
+            ka,
+            va,
+            query_raw,
+            key_raw,
+            gain,
+            hidden_all,
+            middle_all,
+            grad_mlp.reshape(2, half_rows, model_width),
+            grad_hidden,
+            small,
+            s_up[None],
+            s_gate[None],
+            w_query,
+            w_key,
+            w_value,
+            w_up,
+            w_gate,
+            w_down,
+        ),
+        tok_rows,
+        model_width,
+        w_up.shape[1],
+    )
+    dp, b = here()
     rows_out = model_width // (2 * GROUP)
-    grad_out = lax.psum_scatter(part_out, ("dp", "blk"), scatter_dimension=0, tiled=True)
-
-    def vector_rows(vector):
-        rows = vector.reshape(2 * GROUP, -1)
-        return jnp.pad(rows, ((0, 0), (0, 128 - rows.shape[1])))
-
-    s_full = jnp.zeros((model_width,), jnp.float32)
-    s_full = lax.dynamic_update_slice_in_dim(s_full, grad_s_qk, head_col, 0)
-
-    def ff_full(part):
-        full = jnp.zeros((w_up.shape[1],), jnp.float32)
-        full = lax.dynamic_update_slice_in_dim(full, part[:ff_part], b * ff_part, 0)
-        return lax.dynamic_update_slice_in_dim(full, part[ff_part:], ff_half + b * ff_part, 0)
-
-    small = jnp.stack(
-        [
-            vector_rows(s_full),
-            vector_rows(ff_full(g_s_up)),
-            vector_rows(ff_full(g_s_gate)),
-            vector_rows(grad_alpha_attn[0]),
-            vector_rows(grad_alpha_mlp[0]),
-        ],
-        axis=1,
-    )
-    small = jnp.pad(small, ((0, 0), (0, 3), (0, 0)))
-    small = jnp.sum(swap_all(small, 9), axis=0)
+    first_row = (dp * GROUP + b) * rows_out
+    grad_attn, grad_mlp_alpha = (
+        lax.dynamic_slice_in_dim(small[8 * i : 8 * (i + 1)].reshape(-1), first_row, rows_out, 0)
+        for i in (0, 1)
+    )
+    grad_gain = lax.dynamic_slice_in_dim(small[17], (b % 2) * rows_out, rows_out, 0)
     mean_alpha = 0.5 * (jnp.mean(alpha_attn) + jnp.mean(alpha_mlp))
     return (
         result[None, None],
@@ -1226,11 +1502,11 @@
         grad_up,
         grad_gate,
         grad_down,
-        small[0, :rows_out],
-        small[1],
-        small[2],
-        small[3, :rows_out],
-        small[4, :rows_out],
+        grad_gain,
+        grad_scales[0],
+        grad_scales[1],
+        grad_attn,
+        grad_mlp_alpha,
         mean_alpha,
     )
 

time: 370 us -> 268 us (0.72); the launches traced: 364 us -> 268 us
  Pallas kernels: 239 us -> 195 us
  other arithmetic: 41.3 us -> 1.87 us
  waiting for transfers between devices: 0.02 us -> 33.7 us
  local copies, waits for them, and re-layouts: 40.5 us -> 16.4 us
  matrix products: 25.4 us -> 3.73 us
    pallas_call x8 -> x3, Pallas kernels: 193 us -> 148 us  [the longest x1 105 us: finish_block(): pl.pallas_call(finish_kernel, out_shape=[shape((rows, width), f32), shape...]
    reduce_scatter x1, waiting for transfers between devices: 0.01 us -> 33.7 us  [on_device_heads(): lax.psum_scatter(part_out, ('dp', 'blk'), scatter_dimension=0, tiled=True)]
    dot_general x7 -> x0, matrix products: 15.5 us -> none  [the longest x3 9.82 us: dot_nn(): return jnp.dot(left, right, preferred_element_type=jnp.float32)]
    convert_element_type x9 -> x0, other arithmetic: 12.1 us -> none  [the longest x3 3.12 us: split_three(): return [part.astype(jnp.bfloat16) for part in (high, mid, rest - mid)]]
    concatenate x9 -> x1, other arithmetic: 10.1 us -> 0.67 us  [on_device_heads(): jnp.concatenate([grad_alpha_attn.reshape(-1, 128), grad_alpha_mlp.reshape...]
    slice x9 -> x1, local copies, waits for them, and re-layouts: 9.22 us -> 0.73 us  [on_device_heads(): small[17]]
    convert_element_type x9 -> x0, local copies, waits for them, and re-layouts: 6.5 us -> none  [the longest x6 3.76 us: on_device_heads(): grad_query, grad_key, grad_value = (got[:, :, base + i * HEAD_DIM:base +...]
    reduce_sum x6 -> x0, other arithmetic: 6.26 us -> none  [the longest x1 2.92 us: scaled_norm(): return rms_norm(raw_rows) * gain_vector]
  transfers between devices with their start and end apart: 1 -> 1, of which waited for: 0 -> 1; matrix products, arithmetic and copies ran while one was open for 22% -> 2% of each run, Pallas kernels for 40% -> 39%
where the time goes in v3:
time: 268 us
  Pallas kernels  195 us (73%)
  waiting for transfers between devices  33.7 us (13%)
  between operations  16.6 us (6%)
  local copies, waits for them, and re-layouts  16.4 us (6%)
  matrix products  3.73 us (1%)
    pallas_call x1, Pallas kernels, finish_block(): pl.pallas_call(finish_kernel, out_shape=[shape((rows, width), f32), shape...  105 us
    pallas_call x1, Pallas kernels, middle_block(): pl.pallas_call(middle_kernel, out_shape=[shape((rows, width), low), shape...  47.3 us
    pallas_call x1, Pallas kernels, project_block(): pl.pallas_call(project_kernel, out_shape=[shape((2 * GROUP, rows // 2, wi...  35.4 us
    reduce_scatter x1, waiting for transfers between devices, on_device_heads(): lax.psum_scatter(part_out, ('dp', 'blk'), scatter_dimension=0, tiled=True)  33.7 us
    unnamed x20, local copies, waits for them, and re-layouts  11.8 us
    pallas_call x1, Pallas kernels, attend(): pl.pallas_call(attend_kernel, out_shape=[shape((length, 128), jnp.float32...  7.72 us
  transfers between devices with their start and end apart: 1, of which 1 were waited for; matrix products, arithmetic and copies ran while one was open for 2% of the time, Pallas kernels for 39%

profile of v3, /device:TPU:0, one launch (start us, length us, event | category | flops | bytes accessed | tf_op | source)
XLA Modules:
  0.0 267.6 jit_solution(16793465522431456952)
XLA Ops:
  7.2 0.0 reduce-scatter.2.cloned.1.call-start
  7.2 35.4 %project_block.1 = (bf16[32,64,1024]{2,1,0:T(8,128)(2,1)}, bf16[2048,128]{1,0:T(8,128)(2,1)}, bf16[2048,128]{1,0:T(8,128)(2,1)}, bf16[2048,128]{1,0:T(8,128)(2,1...) custom-call(bf16[2,64,1024]{2,1,0:T(8,128)(2,1)} %bitcast.25, bf16[1024,1024]{1,0:T(8,128)(2,1)} %w_query_hbm.3, ...), custom_call_target="tpu_custom_call" | custom-call | tf_op jit(solution)/shard_map/project_block/pallas_call | solution.py:899
  42.7 7.7 %attend.1 = (f32[2048,128]{1,0:T(8,128)}, bf16[2048,128]{1,0:T(8,128)(2,1)}, bf16[16,64,128]{2,1,0:T(8,128)(2,1)}) custom-call(s32[1,2]{1,0:T(1,128)} %lengths_ref.3, bf16[2048,128]{1,0:T(8,128)(2,1)} %get-tuple-element.43.qa_ref, bf16[2048,128]{1,0:T(8,128)(2,1)} %get-tuple-element.44.ka_ref, bf16[2048,128]{1,0:T(8,128)(2,1)} %get-tuple-element.45.va_ref), custom_call_target="tpu_custom_call" | custom-call | tf_op jit(solution)/shard_map/attend/pallas_call | solution.py:985
  50.4 47.3 %middle_block.1 = (bf16[128,1024]{1,0:T(8,128)(2,1)}, f32[128,1024]{1,0:T(8,128)}, bf16[16,64,128]{2,1,0:T(8,128)(2,1)}, bf16[32,64,1024]{2,1,0:T(8,128)(2,1)}, ...) custom-call(bf16[16,64,128]{2,1,0:T(8,128)(2,1)} %get-tuple-element., ...), custom_call_target="tpu_custom_call" | custom-call | tf_op jit(solution)/shard_map/middle_block/pallas_call | solution.py:743
  97.7 0.0 copy-start.2
  97.7 0.0 copy-start.3
  97.7 0.0 copy-start.4
  97.7 0.0 copy-start.5
  97.7 3.7 %fusion = f32[1024,1024]{1,0:T(8,128)} fusion(bf16[128,1024]{1,0:T(8,128)(2,1)} %get-tuple-element.64, bf16[128,1024]{1,0:T(8,128)(2,1)} %get-tuple-element.65), kind=kOutput, calls=%fused_computation.6 | convolution fusion | flops 268435456 | bytes 4718592 | tf_op jit(solution)/shard_map/dot_general | solution.py:534
  101.5 0.0 reduce-scatter.2.cloned.1.call-update
  101.5 0.6 reduce_sum.18
  102.1 0.0 copy-done.3
  102.1 0.6 reduce_sum.19
  102.7 0.1 pad.2.clone
  102.8 0.7 maximum_maximum_fusion.small_in
  103.5 104.9 %finish_block.1 = (f32[128,1024]{1,0:T(8,128)}, f32[32,1024]{1,0:T(8,128)}, f32[32,1024]{1,0:T(8,128)}, f32[32,1024]{1,0:T(8,128)}, f32[32,4096]{1,0:T(8,128)}, ...) custom-call(s32[1,2]{1,0:T(1,128)} %lengths_ref.3, ...), custom_call_target="tpu_custom_call" | custom-call | tf_op jit(solution)/shard_map/finish_block/pallas_call | solution.py:1331
  208.4 0.7 slice.15
  209.1 0.7 slice_bitcast_fusion
  209.8 0.6 dynamic_slice.13
  210.4 0.6 dynamic_slice.14
  212.3 0.6 dynamic-slice_bitcast_fusion
  212.8 1.3 slice_bitcast_fusion.2
  214.1 33.7 %reduce-scatter.2.cloned.1.call-done = f32[32,1024]{1,0:T(8,128)} async-done(((f32[1024,1024]{1,0:T(8,128)}), f32[32,1024]{1,0:T(8,128)}) %reduce-scatter.2.cloned.1.call-update) | async-done | bytes 131088 | tf_op jit(solution)/shard_map/reduce_scatter | solution.py:1438
  247.8 0.7 copy.38
  248.5 1.9 copy.39
  250.4 1.6 copy.40
  251.9 1.6 copy.41
  253.5 1.6 copy.42
  255.1 1.9 copy.43
  256.9 1.9 copy.44
  258.8 0.0 copy-done
  258.8 0.8 copy.45
  (7 shorter events, 0.0 us)
Async XLA Ops:
  7.2 240.6 %reduce-scatter.2.cloned.1.call-start = ((), (), s32[]{:S(2)}) async-start(), calls=%async_computation.1 | async-start | bytes 4325376 | tf_op jit(solution)/shard_map/reduce_scatter | solution.py:1438
  97.7 3.8 %copy-start.2 = (f32[1024]{0:T(1024)S(1)}, f32[1024]{0:T(1024)}, u32[]{:S(2)}) copy-start(f32[1024]{0:T(1024)} %param.28) | copy-start | bytes 12292
  97.7 4.4 %copy-start.3 = (f32[1024]{0:T(1024)S(1)}, f32[1024]{0:T(1024)}, u32[]{:S(2)}) copy-start(f32[1024]{0:T(1024)} %param.29) | copy-start | bytes 12292
  97.7 5.1 %copy-start.4 = (f32[1,1024]{1,0:T(1,128)S(1)}, f32[1,1024]{1,0:T(1,128)}, u32[]{:S(2)}) copy-start(f32[1,1024]{1,0:T(1,128)} %get-tuple-element.58) | copy-start | bytes 12292
  97.7 5.1 %copy-start.5 = (f32[1,1024]{1,0:T(1,128)S(1)}, f32[1,1024]{1,0:T(1,128)}, u32[]{:S(2)}) copy-start(f32[1,1024]{1,0:T(1,128)} %get-tuple-element.59) | copy-start | bytes 12292
  103.5 144.3 %copy-start.1 = (bf16[128,1024]{1,0:T(8,128)(2,1)S(1)}, bf16[128,1024]{1,0:T(8,128)(2,1)}, u32[]{:S(2)}) copy-start(bf16[128,1024]{1,0:T(8,128)(2,1)} %get-tuple-element.47) | copy-start | bytes 786436
  208.4 50.4 %copy-start = (f32[128,1024]{1,0:T(8,128)S(1)}, f32[128,1024]{1,0:T(8,128)}, u32[]{:S(2)}) copy-start(f32[128,1024]{1,0:T(8,128)} %get-tuple-element.98) | copy-start | bytes 1572868
Sparse Core Ops, SparseCore 0:
  101.6 146.1 reduce-scatter.1

commit v4 on v0

--- a/solution.py
+++ b/solution.py
@@ -1,8 +1,11 @@
+import functools
 import math
 
 import jax
 import jax.numpy as jnp
 from jax import lax
+from jax.experimental import pallas as pl
+from jax.experimental.pallas import tpu as pltpu
 from jax.sharding import PartitionSpec as P
 
 HEAD_DIM = 64
@@ -113,7 +116,7 @@
     return (grad_keys, grad_values)
 
 
-def on_device(
+def on_device_general(
     tokens,
     cotangent,
     lengths,
@@ -351,6 +354,1359 @@
     )
 
 
+MESH = pl.DeviceIdType.MESH
+VMEM_SPEC = pl.BlockSpec(memory_space=pltpu.VMEM)
+VMEM_LIMIT = 62 << 20
+GROUP = 16
+
+
+def here():
+    return lax.axis_index("dp"), lax.axis_index("blk")
+
+
+def greet(partners):
+    barrier = pltpu.get_barrier_semaphore()
+    for partner in partners:
+        pl.semaphore_signal(barrier, inc=1, device_id=partner, device_id_type=MESH)
+    pl.semaphore_wait(barrier, len(partners))
+
+
+def remote(src, dst, send_sem, recv_sem, device):
+    return pltpu.make_async_remote_copy(
+        src_ref=src,
+        dst_ref=dst,
+        send_sem=send_sem,
+        recv_sem=recv_sem,
+        device_id=device,
+        device_id_type=MESH,
+    )
+
+
+class Gather:
+    KINDS = 22
+
+    def __init__(self, own, out, send, recv, pieces):
+        self.own, self.out, self.send, self.recv = own, out, send, recv
+        self.pieces = pieces
+        dp, b = here()
+        self.dp, self.b = dp, b
+        self.z, self.y, self.c = b // 4, (b // 2) % 2, b % 2
+        self.up = (dp, (b + 4) % GROUP)
+        self.down = (dp, (b + 12) % GROUP)
+        self.side = (dp, b + 2 - 4 * self.y)
+        self.sib = (dp, b + 1 - 2 * self.c)
+        self.half = self.pieces // 2
+
+    def partners(self):
+        return [self.up, self.down, self.side, self.sib]
+
+    def copy(self, z, y, c, kind, piece, device, own=False):
+        block = z * 4 + y * 2 + c
+        upper = piece // self.half
+        place = 2 * GROUP - 1 - block if upper else block
+        rows = self.out.shape[1] // self.half
+        span = pl.ds(piece % self.half * rows, rows)
+        target = self.out.at[place, span]
+        source = self.own.at[upper, span] if own else target
+        index = self.pieces * kind + piece
+        return remote(source, target, self.send.at[index], self.recv.at[index], device)
+
+    def along(self, z, piece, device, own=False, back=False):
+        return self.copy(z, self.y, self.c, z + (4 if back else 0), piece, device, own)
+
+    def across(self, z, y, piece, own=False):
+        return self.copy(z, y, self.c, 8 + z, piece, self.side, own)
+
+    def over(self, z, piece, device, back=False):
+        return self.copy(z, 1 - self.y, self.c, 21 if back else 20, piece, device)
+
+    def to_sib(self, z, y, c, piece, own=False):
+        return self.copy(z, y, c, 12 + 2 * z + y, piece, self.sib, own)
+
+    def each_side(self, distance, action):
+        if distance == 0:
+            action(self.z, None)
+            return
+        low, high = self.z - distance, self.z + distance
+
+        @pl.when(low >= 0)
+        def _():
+            action(low, False)
+
+        @pl.when(high <= 3)
+        def _():
+            action(high, True)
+
+    def start(self):
+        for piece in range(self.pieces):
+
+            @pl.when(self.z < 3)
+            def _():
+                self.along(self.z, piece, self.up, True).start()
+
+            @pl.when(self.z > 0)
+            def _():
+                self.along(self.z, piece, self.down, True, True).start()
+
+            self.across(self.z, self.y, piece, True).start()
+        for piece in range(self.pieces):
+            self.to_sib(self.z, self.y, self.c, piece, True).start()
+        for upper in (0, 1):
+            place = 2 * GROUP - 1 - self.b if upper else self.b
+            self.out[place] = self.own[upper]
+
+    def line(self, distance):
+        def action(z, above):
+            for piece in range(self.pieces):
+                self.along(z, piece, self.sib, False, above).wait_recv()
+                if above:
+
+                    @pl.when(self.z > 0)
+                    def _():
+                        self.along(z, piece, self.down, False, True).start()
+                else:
+
+                    @pl.when(self.z < 3)
+                    def _():
+                        self.along(z, piece, self.up).start()
+
+                if distance > 1 or piece < self.half:
+                    self.across(z, self.y, piece).start()
+                self.to_sib(z, self.y, self.c, piece).start()
+
+        self.each_side(distance, action)
+
+    def sides(self, distance):
+        def action(z, above):
+            for piece in range(self.pieces):
+                if distance == 1 and piece >= self.half:
+                    continue
+                self.across(z, 1 - self.y, piece).wait_recv()
+                self.to_sib(z, 1 - self.y, self.c, piece).start()
+
+        self.each_side(distance, action)
+
+    def hand_over(self):
+        for piece in range(self.half, self.pieces):
+
+            @pl.when(self.z < 3)
+            def _():
+                self.over(self.z, piece, self.up).start()
+
+            @pl.when(self.z > 0)
+            def _():
+                self.over(self.z, piece, self.down, True).start()
+
+    def handed(self):
+        def action(z, above):
+            for piece in range(self.half, self.pieces):
+                self.over(z, piece, self.sib, above).wait_recv()
+                self.to_sib(z, 1 - self.y, self.c, piece).start()
+
+        self.each_side(1, action)
+
+    def from_sib(self, distance):
+        def action(z, above):
+            for piece in range(self.pieces):
+                for y in (0, 1):
+                    self.to_sib(z, y, 1 - self.c, piece).wait_recv()
+
+        self.each_side(distance, action)
+
+    def drain(self):
+        for piece in range(self.pieces):
+            for z in range(4):
+                for y in (0, 1):
+                    self.to_sib(z, y, self.c, piece).wait_send()
+                if piece < self.half:
+                    self.across(z, self.y, piece).wait_send()
+                else:
+
+                    @pl.when((z > self.z + 1) | (z < self.z - 1) | (z == self.z))
+                    def _():
+                        self.across(z, self.y, piece).wait_send()
+
+                @pl.when((self.z >= z) & (self.z < 3))
+                def _():
+                    self.along(z, piece, self.up).wait_send()
+
+                @pl.when((self.z <= z) & (self.z > 0))
+                def _():
+                    self.along(z, piece, self.down, False, True).wait_send()
+
+            if piece >= self.half:
+
+                @pl.when(self.z < 3)
+                def _():
+                    self.over(self.z, piece, self.up).wait_send()
+
+                @pl.when(self.z > 0)
+                def _():
+                    self.over(self.z, piece, self.down, True).wait_send()
+
+    def finish(self):
+        for distance in range(4):
+            self.from_sib(distance)
+        self.drain()
+
+
+def gather_scratch(pieces):
+    return [pltpu.SemaphoreType.DMA((pieces * Gather.KINDS,)) for _ in range(2)]
+
+
+def comm_params(collective_id):
+    return pltpu.CompilerParams(
+        collective_id=collective_id, has_side_effects=True, vmem_limit_bytes=VMEM_LIMIT
+    )
+
+
+def dot_nt(left, right):
+    return lax.dot_general(left, right, (((1,), (1,)), ((), ())), preferred_element_type=jnp.float32)
+
+
+def dot_tn(left, right):
+    return lax.dot_general(left, right, (((0,), (0,)), ((), ())), preferred_element_type=jnp.float32)
+
+
+def dot_nn(left, right):
+    return jnp.dot(left, right, preferred_element_type=jnp.float32)
+
+
+FF_STEP = 512
+
+
+def mean_last(array):
+    return jnp.mean(array, axis=-1, keepdims=True)
+
+
+def rms_scale(array):
+    return lax.rsqrt(mean_last(array * array) + 1e-06)
+
+
+def rms_pull(grad, normed, scale):
+    return scale * (grad - normed * mean_last(grad * normed))
+
+
+def half_lanes(shape):
+    return lax.broadcasted_iota(jnp.int32, shape, 1) < HEAD_DIM
+
+
+class Swap:
+    def __init__(self, blocks, out, send, recv, own=True):
+        self.blocks, self.out, self.own = blocks, out, own
+        dp, self.b = here()
+        self.copies = []
+        for step in range(1, GROUP):
+            target = (self.b + step) % GROUP
+            self.copies.append(
+                remote(
+                    (blocks.block(target) if isinstance(blocks, SendBlocks) else blocks.at[target])
+                    if own
+                    else blocks,
+                    out.at[self.b],
+                    send.at[step],
+                    recv.at[step],
+                    (dp, target),
+                )
+            )
+        self.partners = [(dp, (self.b + step) % GROUP) for step in range(1, GROUP)]
+
+    def start(self):
+        for copy in self.copies:
+            copy.start()
+        if self.own:
+            mine = self.blocks
+            mine = mine.block(self.b) if isinstance(mine, SendBlocks) else mine.at[self.b]
+            self.out[self.b] = mine[...]
+
+    def wait(self):
+        for copy in self.copies:
+            copy.wait()
+
+
+ANY_SPEC = pl.BlockSpec(memory_space=pl.ANY)
+
+
+SMEM_SPEC = pl.BlockSpec(memory_space=pltpu.SMEM)
+
+
+def own_head(pair, core):
+    shifted = jnp.where(core == 1, pltpu.roll(pair, HEAD_DIM, 1), pair)
+    return jnp.where(half_lanes(pair.shape), shifted, 0.0)
+
+
+def minus_ones(matrix):
+    lane = lax.broadcasted_iota(jnp.int32, matrix.shape, 1)
+    extra = jnp.where(lane < HEAD_DIM + 3, -1.0, 0.0)
+    return jnp.where(lane < HEAD_DIM, matrix, extra).astype(jnp.bfloat16)
+
+
+PROJECT_PIECES = 4
+
+
+def project_kernel(
+    own,
+    w_query_hbm,
+    w_key_hbm,
+    w_value_hbm,
+    s_qk_ref,
+    out,
+    qa_ref,
+    ka_ref,
+    va_ref,
+    q_raw_ref,
+    k_raw_ref,
+    gain_ref,
+    w_head,
+    load_sem,
+    send,
+    recv,
+):
+    gather = Gather(own, out, send, recv, PROJECT_PIECES)
+    window = pl.ds(pl.multiple_of(gather.b // 2 * 128, 128), 128)
+    loads = [
+        pltpu.make_async_copy(
+            source.at[:, window], w_head.at[:, pl.ds(128 * i, 128)], load_sem.at[i]
+        )
+        for i, source in enumerate((w_query_hbm, w_key_hbm, w_value_hbm))
+    ]
+    for load in loads:
+        load.start()
+    greet(gather.partners())
+    gather.start()
+    gain = own_head(jnp.broadcast_to(s_qk_ref[:, window], (8, 128)), gather.c)[:1]
+    gain_ref[...] = gain
+    for load in loads:
+        load.wait()
+    slots = 2 * GROUP // 8
+    half = out.shape[1]
+
+    def project(first_slot):
+        hidden = out[pl.ds(first_slot, slots)].reshape(slots * half, out.shape[2])
+        raw = dot_nn(hidden, w_head[...])
+        rows = pl.ds(pl.multiple_of(first_slot * half, half), slots * half)
+        query, key, value = (
+            own_head(raw[:, 128 * i : 128 * (i + 1)], gather.c) for i in range(3)
+        )
+        q_raw_ref[rows, :] = query.astype(jnp.bfloat16)
+        k_raw_ref[rows, :] = key.astype(jnp.bfloat16)
+        count = float(HEAD_DIM)
+        query_scale = lax.rsqrt(jnp.sum(query * query, axis=1, keepdims=True) / count + 1e-06)
+        key_scale = lax.rsqrt(jnp.sum(key * key, axis=1, keepdims=True) / count + 1e-06)
+        query = (query * query_scale * gain).astype(jnp.bfloat16).astype(jnp.float32)
+        qa_ref[rows, :] = (query * (1.0 / math.sqrt(HEAD_DIM))).astype(jnp.bfloat16)
+        ka_ref[rows, :] = minus_ones(key * key_scale * gain)
+        va_ref[rows, :] = minus_ones(value)
+
+    def project_line(distance):
+        def both(z):
+            project(slots * z)
+            project(2 * GROUP - slots - slots * z)
+
+        if distance == 0:
+            both(gather.z)
+        else:
+
+            @pl.when(gather.z - distance >= 0)
+            def _():
+                both(gather.z - distance)
+
+            @pl.when(gather.z + distance <= 3)
+            def _():
+                both(gather.z + distance)
+
+    gather.line(1)
+    gather.sides(0)
+    gather.from_sib(0)
+    project_line(0)
+    gather.line(2)
+    gather.hand_over()
+    gather.sides(1)
+    gather.line(3)
+    gather.sides(2)
+    gather.from_sib(2)
+    project_line(2)
+    gather.handed()
+    gather.from_sib(1)
+    project_line(1)
+    gather.sides(3)
+    gather.from_sib(3)
+    project_line(3)
+    gather.drain()
+
+
+def project_block(hidden, w_query, w_key, w_value, s_qk):
+    rows, width = hidden.shape
+    length = GROUP * rows
+    low, f32 = jnp.bfloat16, jnp.float32
+    shape = jax.ShapeDtypeStruct
+    return pl.pallas_call(
+        project_kernel,
+        out_shape=[
+            shape((2 * GROUP, rows // 2, width), low),
+            shape((length, 128), low),
+            shape((length, 128), low),
+            shape((length, 128), low),
+            shape((length, 128), low),
+            shape((length, 128), low),
+            shape((1, 128), f32),
+        ],
+        in_specs=[VMEM_SPEC] + [ANY_SPEC] * 3 + [VMEM_SPEC],
+        out_specs=[VMEM_SPEC] * 7,
+        scratch_shapes=[pltpu.VMEM((width, 384), low), pltpu.SemaphoreType.DMA((3,))]
+        + gather_scratch(PROJECT_PIECES),
+        compiler_params=comm_params(0),
+        name="project_block",
+    )(hidden.reshape(2, rows // 2, width), w_query, w_key, w_value, s_qk[None])
+
+
+def doc_start_of(positions, lengths_ref):
+    start = jnp.zeros_like(positions)
+    end = jnp.int32(0)
+    for doc in range(lengths_ref.shape[1]):
+        end = end + lengths_ref[0, doc]
+        start = start + jnp.where(positions >= end, lengths_ref[0, doc], 0)
+    return start
+
+
+def split_lanes(column, shape):
+    lane = lax.broadcasted_iota(jnp.int32, shape, 1)
+    high = column.astype(jnp.bfloat16).astype(jnp.float32)
+    rest = column - high
+    mid = rest.astype(jnp.bfloat16).astype(jnp.float32)
+    last = rest - mid
+    return jnp.where(
+        lane == HEAD_DIM,
+        high,
+        jnp.where(lane == HEAD_DIM + 1, mid, jnp.where(lane == HEAD_DIM + 2, last, 0.0)),
+    )
+
+
+ATT = 512
+
+
+def attend_kernel(lengths_ref, qa_ref, ka_ref, va_ref, o_ref, ql_ref, packed_ref):
+    length = qa_ref.shape[0]
+    half = packed_ref.shape[1]
+    for query_block in range(length // ATT):
+        rows = pl.ds(query_block * ATT, ATT)
+        queries = qa_ref[rows, :]
+        column = query_block * ATT + lax.broadcasted_iota(jnp.int32, (ATT, 1), 0)
+        doc_start = doc_start_of(column, lengths_ref)
+        first_start = doc_start_of(jnp.int32(query_block * ATT), lengths_ref)
+        query_pos = query_block * ATT + lax.broadcasted_iota(jnp.int32, (ATT, ATT), 0)
+        key_lane = lax.broadcasted_iota(jnp.int32, (ATT, ATT), 1)
+
+        def step(key_block, total):
+            base = pl.multiple_of(key_block * ATT, ATT)
+            keys = ka_ref[pl.ds(base, ATT), :]
+            values = va_ref[pl.ds(base, ATT), :]
+            key_pos = base + key_lane
+            allowed = (key_pos <= query_pos) & (key_pos >= doc_start)
+            weights = jnp.where(allowed, jnp.exp(dot_nt(queries, keys)), 0.0)
+            return total + dot_nn(weights.astype(jnp.bfloat16), values)
+
+        total = lax.fori_loop(
+            first_start // ATT, query_block + 1, step, jnp.zeros((ATT, 128), jnp.float32)
+        )
+        row_sum = -total[:, HEAD_DIM : HEAD_DIM + 1]
+        first = half_lanes(total.shape)
+        o_ref[rows, :] = jnp.where(first, total / row_sum, 0.0).astype(o_ref.dtype)
+        extra = split_lanes(jnp.log(row_sum), total.shape)
+        ql_ref[rows, :] = jnp.where(first, queries.astype(jnp.float32), extra).astype(jnp.bfloat16)
+    first = half_lanes((half, 128))
+    for j in range(GROUP):
+        lower = o_ref[j * half : (j + 1) * half, :].astype(jnp.float32)
+        upper = o_ref[length - (j + 1) * half : length - j * half, :].astype(jnp.float32)
+        packed_ref[j] = jnp.where(first, lower, pltpu.roll(upper, HEAD_DIM, 1)).astype(
+            packed_ref.dtype
+        )
+
+
+def attend(lengths, qa, ka, va, half_rows):
+    length = qa.shape[0]
+    shape = jax.ShapeDtypeStruct
+    return pl.pallas_call(
+        attend_kernel,
+        out_shape=[
+            shape((length, 128), jnp.bfloat16),
+            shape((length, 128), jnp.bfloat16),
+            shape((GROUP, half_rows, 128), jnp.bfloat16),
+        ],
+        in_specs=[SMEM_SPEC] + [VMEM_SPEC] * 3,
+        out_specs=[VMEM_SPEC] * 3,
+        compiler_params=pltpu.CompilerParams(vmem_limit_bytes=VMEM_LIMIT),
+        name="attend",
+    )(lengths, qa, ka, va)
+
+
+TAIL_PIECES = 2
+KEYS = 256
+
+
+class SendBlocks:
+    def __init__(self, ref, first_row, rows, first_lane, lanes):
+        self.ref, self.first_row, self.rows = ref, first_row, rows
+        self.lanes = pl.ds(first_lane, lanes)
+
+    def block(self, index):
+        start = pl.multiple_of(self.first_row + index * self.rows, self.rows)
+        return self.ref.at[pl.ds(start, self.rows), self.lanes]
+
+
+def tail_kernel(
+    lengths_ref,
+    o_ref,
+    hidden_ref,
+    cot_ref,
+    gain_ref,
+    s_up_ref,
+    s_gate_ref,
+    alpha_attn_ref,
+    alpha_mlp_ref,
+    w_out_hbm,
+    w_up_hbm,
+    w_gate_hbm,
+    w_down_hbm,
+    w_query_hbm,
+    w_key_hbm,
+    w_value_hbm,
+    ql_hbm,
+    ka_hbm,
+    va_hbm,
+    att_hbm,
+    q_raw_hbm,
+    k_raw_hbm,
+    hidden_hbm,
+    result_ref,
+    input_grad_ref,
+    wide_in,
+    qkv_in,
+    g_down_ref,
+    out_in,
+    g_s_ref,
+    small_ref,
+    mid_all,
+    g_mlp_all,
+    w_out,
+    w_up,
+    w_gate,
+    w_down,
+    up_slice,
+    gate_slice,
+    down_slice,
+    up_raw,
+    gate_raw,
+    mid_own,
+    g_mlp_own,
+    o_in,
+    g_send,
+    g_in,
+    acc,
+    g_res,
+    att_pair,
+    branch_pair,
+    out_got,
+    out_side_got,
+    ql_ref,
+    ka_ref,
+    va_ref,
+    ga_ref,
+    dq_acc,
+    dk_acc,
+    dv_acc,
+    back_in,
+    qkv_part,
+    qkv_got,
+    wide_own,
+    wide_got,
+    down_got,
+    small_own,
+    small_got,
+    small_all,
+    s_part,
+    s_send,
+    s_got,
+    load_sems,
+    x_sems,
+    pair_sems,
+    out_sems,
+    swap_sems,
+    grad_sems,
+    back_sems,
+    qkv_sems,
+    wide_sems,
+    small_sems,
+    mid_send,
+    mid_recv,
+    mlp_send,
+    mlp_recv,
+):
+    low, f32 = jnp.bfloat16, jnp.float32
+    dp, b = here()
+    z, y, c = b // 4, (b // 2) % 2, b % 2
+    twin, sib, side = (1 - dp, b), (dp, b + 1 - 2 * c), (dp, b + 2 - 4 * y)
+    rows, width = hidden_ref.shape
+    half = rows // 2
+    length = GROUP * rows
+    ff = w_up.shape[1]
+    ff_half = ff // 2
+    part = ff // (2 * GROUP)
+    quarter = width // 4
+    rows_out = width // (2 * GROUP)
+    blocks = length // ATT
+    loaded = []
+
+    def load(source, target):
+        copy = pltpu.make_async_copy(source, target, load_sems.at[len(loaded)])
+        copy.start()
+        loaded.append(copy)
+        return copy
+
+    def to(device, sems, index, source, target):
+        copy = remote(source, target, sems.at[0, index], sems.at[1, index], device)
+        copy.start()
+        return copy
+
+    load_out = load(w_out_hbm, w_out)
+    load_mlp = [load(w_up_hbm, w_up), load(w_gate_hbm, w_gate), load(w_down_hbm, w_down)]
+    load_slices = []
+    windows = [pl.ds(pl.multiple_of(p * ff_half + b * part, part), part) for p in (0, 1)]
+    for p in (0, 1):
+        place = pl.ds(p * part, part)
+        load_slices.append(load(w_up_hbm.at[:, windows[p]], up_slice.at[:, place]))
+        load_slices.append(load(w_gate_hbm.at[:, windows[p]], gate_slice.at[:, place]))
+        load_slices.append(load(w_down_hbm.at[windows[p], :], down_slice.at[place, :]))
+
+    swap = Swap(o_ref, o_in, swap_sems.at[0], swap_sems.at[1])
+    grad_swap = Swap(g_send, g_in, grad_sems.at[0], grad_sems.at[1])
+    small_swap = Swap(small_own, small_all, small_sems.at[0], small_sems.at[1], own=False)
+    gather_mid = Gather(mid_own, mid_all, mid_send, mid_recv, TAIL_PIECES)
+    gather_mlp = Gather(g_mlp_own, g_mlp_all, mlp_send, mlp_recv, TAIL_PIECES)
+    greet(swap.partners + [twin])
+    swap.start()
+    swap.wait()
+
+    first = half_lanes((half, 128))
+    for pair in range(GROUP // 2):
+        even = o_in[2 * pair].astype(f32)
+        odd = o_in[2 * pair + 1].astype(f32)
+        lanes = slice(pair * 128, (pair + 1) * 128)
+        att_pair[c, :half, lanes] = jnp.where(first, even, pltpu.roll(odd, HEAD_DIM, 1)).astype(low)
+        att_pair[c, half:, lanes] = jnp.where(first, pltpu.roll(even, HEAD_DIM, 1), odd).astype(low)
+    att_copy = to(sib, pair_sems, 0, att_pair.at[c], att_pair.at[c])
+    hidden = hidden_ref[...].astype(f32)
+    alpha_attn = alpha_attn_ref[...]
+    alpha_mlp = alpha_mlp_ref[...]
+    load_out.wait()
+    branch = dot_nn(att_pair[c], w_out[...])
+    branch_scale = rms_scale(branch)
+    branch_normed = branch * branch_scale
+    mixed = hidden + alpha_attn * (branch_normed - hidden)
+    middle_scale = rms_scale(mixed)
+    middle = mixed * middle_scale
+    middle_low = middle.astype(low)
+    mid_own[0] = middle_low[:half]
+    mid_own[1] = middle_low[half:]
+    gather_mid.start()
+    for copy in load_mlp:
+        copy.wait()
+    steps = ff // FF_STEP
+    acc[...] = jnp.zeros_like(acc)
+
+    def forward(step, carry):
+        cols = pl.ds(pl.multiple_of(step * FF_STEP, FF_STEP), FF_STEP)
+        up = dot_nn(middle_low, w_up[:, cols])
+        gate = dot_nn(middle_low, w_gate[:, cols])
+        up_raw[:, cols] = up
+        gate_raw[:, cols] = gate
+        scaled = gate * s_gate_ref[:, cols]
+        inner = up * s_up_ref[:, cols] * (scaled / (1.0 + jnp.exp(-scaled)))
+        acc[...] += dot_nn(inner.astype(low), w_down[cols, :])
+        return carry
+
+    lax.fori_loop(0, steps, forward, 0)
+    gather_mid.line(1)
+    gather_mid.sides(0)
+    mlp = acc[...]
+    mlp_scale = rms_scale(mlp)
+    mlp_normed = mlp * mlp_scale
+    mixed_out = middle + alpha_mlp * (mlp_normed - middle)
+    out_scale = rms_scale(mixed_out)
+    result = mixed_out * out_scale
+    result_ref[...] = result.astype(low)
+
+    g_mixed = rms_pull(cot_ref[...].astype(f32), result, out_scale)
+    g_alpha_mlp = jnp.sum(g_mixed * (mlp_normed - middle), axis=0, keepdims=True)
+    small_own[...] = jnp.zeros_like(small_own)
+    for i in range(width // 128):
+        small_own[8 + i : 9 + i, :] = g_alpha_mlp[:, 128 * i : 128 * (i + 1)]
+    g_mlp = rms_pull(g_mixed * alpha_mlp, mlp_normed, mlp_scale).astype(low)
+    g_mlp_own[0] = g_mlp[:half]
+    g_mlp_own[1] = g_mlp[half:]
+    gather_mlp.start()
+    acc[...] = g_mixed * (1.0 - alpha_mlp)
+
+    def backward(step, carry):
+        cols = pl.ds(pl.multiple_of(step * FF_STEP, FF_STEP), FF_STEP)
+        g_inner = dot_nt(g_mlp, w_down[cols, :])
+        s_up = s_up_ref[:, cols]
+        s_gate = s_gate_ref[:, cols]
+        scaled = gate_raw[:, cols] * s_gate
+        sigmoid = 1.0 / (1.0 + jnp.exp(-scaled))
+        g_up = g_inner * (scaled / (1.0 + jnp.exp(-scaled))) * s_up
+        slope = sigmoid * (1.0 + scaled * (1.0 - sigmoid))
+        g_gate = g_inner * (up_raw[:, cols] * s_up) * slope * s_gate
+        acc[...] += dot_nt(g_up.astype(low), w_up[:, cols]) + dot_nt(
+            g_gate.astype(low), w_gate[:, cols]
+        )
+        return carry
+
+    lax.fori_loop(0, steps // 2, backward, 0)
+    gather_mid.line(2)
+    gather_mid.hand_over()
+    gather_mid.sides(1)
+    lax.fori_loop(steps // 2, steps, backward, 0)
+    g_pre = rms_pull(acc[...], middle, middle_scale)
+    g_res[...] = g_pre * (1.0 - alpha_attn)
+    g_alpha_attn = jnp.sum(g_pre * (branch_normed - hidden), axis=0, keepdims=True)
+    for i in range(width // 128):
+        small_own[i : i + 1, :] = g_alpha_attn[:, 128 * i : 128 * (i + 1)]
+    branch_pair[c] = rms_pull(g_pre * alpha_attn, branch_normed, branch_scale).astype(low)
+    g_att = dot_nt(branch_pair[c], w_out[...]).astype(low).astype(f32)
+    for pair in range(GROUP // 2):
+        lower = g_att[:half, pair * 128 : (pair + 1) * 128]
+        upper = g_att[half:, pair * 128 : (pair + 1) * 128]
+        g_send[2 * pair] = jnp.where(first, lower, pltpu.roll(upper, HEAD_DIM, 1)).astype(low)
+        g_send[2 * pair + 1] = jnp.where(first, pltpu.roll(lower, HEAD_DIM, 1), upper).astype(low)
+    grad_swap.start()
+    branch_copy = to(sib, pair_sems, 1, branch_pair.at[c], branch_pair.at[c])
+
+    g_cat = w_down.at[pl.ds(0, length), pl.ds(0, 4 * part)]
+    inner_all = w_down.at[pl.ds(0, length), pl.ds(512, 2 * part)]
+    raw_low = w_down.at[pl.ds(length, length), pl.ds(0, 384)]
+    att_ref = w_down.at[pl.ds(length, length), pl.ds(640, 128)]
+    q_raw_ref = w_down.at[pl.ds(length, length), pl.ds(768, 128)]
+    k_raw_ref = w_down.at[pl.ds(length, length), pl.ds(896, 128)]
+    w_qkv = [w_up.at[:, pl.ds(i * width, width)] for i in range(3)]
+    home = [w_up.at[pl.ds(i * rows, rows), pl.ds(3 * width, width)] for i in range(3)]
+    out_send = w_out.at[pl.ds(0, quarter), :]
+    out_side_send = [w_out.at[pl.ds(quarter + half * k, half), :] for k in (0, 1)]
+    out_line = w_out.at[pl.ds(2 * quarter, 4 * rows_out), :]
+    down_send = w_out.at[pl.ds(3 * quarter, part), :]
+    out_own = [up_raw.at[:, pl.ds((2 + k) * width, width)] for k in (0, 1)]
+    wide_send = [w_gate.at[pl.ds(quarter * i, quarter), pl.ds(2048, 512)] for i in (0, 1)]
+    qkv_send = w_gate.at[pl.ds(0, 2 * quarter), pl.ds(2560, 256)]
+    back_send = SendBlocks(w_gate, 0, half, 2816, 384)
+    qkv_blocks = SendBlocks(w_gate, 2 * quarter, rows_out, 2560, 256)
+    wide_blocks = SendBlocks(w_gate, 2 * quarter, rows_out, 2048, 512)
+    back_swap = Swap(back_send, back_in, back_sems.at[0], back_sems.at[1])
+    qkv_swap = Swap(qkv_blocks, qkv_in, qkv_sems.at[0], qkv_sems.at[1])
+    tokens_of_half = [w_gate.at[:, pl.ds(i * width, width)] for i in (0, 1)]
+    load_heads = [
+        load(source, target)
+        for source, target in (
+            (att_hbm, att_ref),
+            (ql_hbm, ql_ref),
+            (ka_hbm, ka_ref),
+            (va_hbm, va_ref),
+            (q_raw_hbm, q_raw_ref),
+            (k_raw_hbm, k_raw_ref),
+        )
+    ]
+    load_hidden = [
+        load(hidden_hbm.at[pl.ds(i * width, width), :], tokens_of_half[i]) for i in (0, 1)
+    ]
+    load_qkv = [
+        load(source, w_qkv[i]) for i, source in enumerate((w_query_hbm, w_key_hbm, w_value_hbm))
+    ]
+    gather_mid.line(3)
+    gather_mid.sides(2)
+    gather_mlp.line(1)
+    gather_mlp.sides(0)
+
+    att_copy.wait()
+    branch_copy.wait()
+    both_branch = branch_pair[...].reshape(2 * rows, width)
+
+    def out_rows(owner):
+        lanes = pl.ds(pl.multiple_of(owner * 2 * quarter + c * quarter, quarter), quarter)
+        return dot_tn(att_pair[:, :, lanes].reshape(2 * rows, quarter), both_branch)
+
+    out_send[...] = out_rows(1 - dp).astype(low)
+    out_copy = to(twin, x_sems, 0, out_send, out_got)
+    out_mine = out_rows(dp)
+    for k in (0, 1):
+        out_own[k][...] = out_mine[2 * half * k : 2 * half * (k + 1)]
+    gather_mid.handed()
+    gather_mid.sides(3)
+
+    for copy in load_heads:
+        copy.wait()
+    grad_swap.wait()
+    for j in range(GROUP):
+        block = g_in[j].astype(f32)
+        for start, grads in (
+            (j * half, jnp.where(first, block, 0.0)),
+            (length - (j + 1) * half, jnp.where(first, pltpu.roll(block, HEAD_DIM, 1), 0.0)),
+        ):
+            span = pl.ds(start, half)
+            delta = jnp.sum(grads * att_ref[span, :].astype(f32), axis=1, keepdims=True)
+            ga_ref[span, :] = (grads + split_lanes(delta, grads.shape)).astype(low)
+    dq_acc[...] = jnp.zeros_like(dq_acc)
+    key_row = lax.broadcasted_iota(jnp.int32, (KEYS, ATT), 0)
+    query_lane = lax.broadcasted_iota(jnp.int32, (KEYS, ATT), 1)
+    query_row = lax.broadcasted_iota(jnp.int32, (1, ATT), 1)
+    gain = gain_ref[...]
+    count = float(HEAD_DIM)
+    score_scale = 1.0 / math.sqrt(HEAD_DIM)
+    wide_first = half_lanes((ATT, 128))
+
+    def norm_pull(raw, grad):
+        raw = raw.astype(f32)
+        scale = lax.rsqrt(jnp.sum(raw * raw, axis=1, keepdims=True) / count + 1e-06)
+        normed = raw * scale
+        g_gain = jnp.sum(grad * normed, axis=0, keepdims=True)
+        inside = grad * gain
+        mean = jnp.sum(inside * normed, axis=1, keepdims=True) / count
+        return scale * (inside - normed * mean), g_gain
+
+    key_first = half_lanes((KEYS, 128))
+
+    def key_step(key_block, g_gain):
+        span = pl.ds(pl.multiple_of(key_block * KEYS, KEYS), KEYS)
+        keys = ka_ref[span, :]
+        values = va_ref[span, :]
+        key_pos = key_block * KEYS + key_row
+        dk_acc[...] = jnp.zeros_like(dk_acc)
+        dv_acc[...] = jnp.zeros_like(dv_acc)
+
+        def step(query_block, carry):
+            base = pl.multiple_of(query_block * ATT, ATT)
+            queries = ql_ref[pl.ds(base, ATT), :]
+            grads = ga_ref[pl.ds(base, ATT), :]
+            doc_start = doc_start_of(base + query_row, lengths_ref)
+            allowed = (key_pos <= base + query_lane) & (key_pos >= doc_start)
+            weights = jnp.where(allowed, jnp.exp(dot_nt(keys, queries)), 0.0)
+            slopes = (weights * dot_nt(values, grads)).astype(low)
+            dv_acc[...] += dot_nn(weights.astype(low), grads)
+            dk_acc[...] += dot_nn(slopes, queries)
+            dq_acc[pl.ds(base, ATT), :] += dot_tn(slopes, keys)
+            return carry
+
+        lax.fori_loop(key_block * KEYS // ATT, blocks, step, 0)
+        dk = jnp.where(key_first, dk_acc[...], 0.0)
+        g_key, key_gain = norm_pull(k_raw_ref[span, :], dk)
+        raw_low[span, 128:256] = g_key.astype(low)
+        raw_low[span, 256:384] = jnp.where(key_first, dv_acc[...], 0.0).astype(low)
+        return g_gain + key_gain
+
+    g_gain = lax.fori_loop(0, 2, key_step, jnp.zeros((1, 128), f32))
+    gather_mlp.line(2)
+    gather_mlp.hand_over()
+    gather_mlp.sides(1)
+    g_gain = lax.fori_loop(2, length // KEYS, key_step, g_gain)
+    for block in range(blocks):
+        span = pl.ds(block * ATT, ATT)
+        dq = jnp.where(wide_first, dq_acc[span, :] * score_scale, 0.0)
+        g_query, query_gain = norm_pull(q_raw_ref[span, :], dq)
+        g_gain = g_gain + query_gain
+        raw_low[span, 0:128] = g_query.astype(low)
+    for j in range(GROUP):
+        for i in range(3):
+            lanes = slice(128 * i, 128 * (i + 1))
+            lower = raw_low[j * half : (j + 1) * half, lanes].astype(f32)
+            upper = raw_low[length - (j + 1) * half : length - j * half, lanes].astype(f32)
+            back_send.block(j)[:, lanes] = jnp.where(
+                first, lower, pltpu.roll(upper, HEAD_DIM, 1)
+            ).astype(low)
+    gather_mlp.line(3)
+    gather_mlp.sides(2)
+    back_swap.start()
+
+    small_own[16:17, :] = g_gain
+    small_copy = to(twin, x_sems, 1, small_own, small_got)
+
+    for copy in load_hidden:
+        copy.wait()
+
+    def qkv_chunk(chunk):
+        lanes = pl.ds(pl.multiple_of(chunk * quarter, quarter), quarter)
+        grads = sum(
+            dot_tn(tokens_of_half[i][:, lanes], raw_low[pl.ds(i * width, width), :]) for i in (0, 1)
+        )
+        query_key = jnp.where(
+            half_lanes((quarter, 128)), grads[:, :128], pltpu.roll(grads[:, 128:256], HEAD_DIM, 1)
+        )
+        return query_key, grads[:, 256:]
+
+    for i in (0, 1):
+        query_key, value = qkv_chunk(2 * (1 - dp) + i)
+        span = slice(quarter * i, quarter * (i + 1))
+        qkv_send[span, :128] = query_key.astype(low)
+        qkv_send[span, 128:] = value.astype(low)
+    qkv_copy = to(twin, x_sems, 2, qkv_send, qkv_got)
+    for i in (0, 1):
+        query_key, value = qkv_chunk(2 * dp + i)
+        span = slice(quarter * i, quarter * (i + 1))
+        qkv_part[span, :128] = query_key
+        qkv_part[span, 128:] = value
+
+    out_copy.wait()
+    side_copies = []
+    for k in (0, 1):
+        out_own[k][...] += out_got[2 * half * k : 2 * half * (k + 1)].astype(f32)
+        other = pl.ds(pl.multiple_of((1 - y) * half, half), half)
+        out_side_send[k][...] = out_own[k][other, :].astype(low)
+        side_copies.append(to(side, pair_sems, 2 + k, out_side_send[k], out_side_got.at[k]))
+    small_copy.wait()
+    small_own[...] += small_got[...]
+    small_swap.start()
+    gather_mlp.sides(3)
+    gather_mlp.handed()
+    gather_mid.finish()
+    gather_mlp.finish()
+
+    for copy in load_slices:
+        copy.wait()
+    s_up = jnp.concatenate([s_up_ref[:, window] for window in windows], axis=1)
+    s_gate = jnp.concatenate([s_gate_ref[:, window] for window in windows], axis=1)
+    slots = KEYS // half
+
+    def tokens_of(array, step):
+        return array[pl.ds(step * slots, slots)].reshape(KEYS, width)
+
+    def recompute(step, sums):
+        span = pl.ds(pl.multiple_of(step * KEYS, KEYS), KEYS)
+        some = tokens_of(mid_all, step)
+        up = dot_nn(some, up_slice[...])
+        gate = dot_nn(some, gate_slice[...])
+        g_inner = dot_nt(tokens_of(g_mlp_all, step), down_slice[...])
+        scaled = gate * s_gate
+        sigmoid = 1.0 / (1.0 + jnp.exp(-scaled))
+        silu = scaled / (1.0 + jnp.exp(-scaled))
+        up_scaled = up * s_up
+        inner_all[span, :] = (up_scaled * silu).astype(low)
+        g_up_scaled = g_inner * silu
+        g_scaled = g_inner * up_scaled * (sigmoid * (1.0 + scaled * (1.0 - sigmoid)))
+        g_cat[span, : 2 * part] = (g_up_scaled * s_up).astype(low)
+        g_cat[span, 2 * part :] = (g_scaled * s_gate).astype(low)
+        return (
+            sums[0] + jnp.sum(g_up_scaled * up, axis=0, keepdims=True),
+            sums[1] + jnp.sum(g_scaled * gate, axis=0, keepdims=True),
+        )
+
+    zero_row = jnp.zeros((1, 2 * part), f32)
+    g_s_up, g_s_gate = lax.fori_loop(0, length // KEYS, recompute, (zero_row, zero_row))
+
+    def wide_chunk(chunk):
+        lanes = pl.ds(pl.multiple_of(chunk * quarter, quarter), quarter)
+        return dot_tn(mid_all[:, :, lanes].reshape(length, quarter), g_cat[...])
+
+    wide_copies = []
+    for i in (0, 1):
+        wide_send[i][...] = wide_chunk(2 * (1 - dp) + i).astype(low)
+        wide_copies.append(to(twin, x_sems, 3 + i, wide_send[i], wide_got.at[i]))
+    for p in (0, 1):
+        s_part[p] = jnp.zeros(s_part.shape[1:], f32)
+        s_part[p, 0:1, :] = g_s_up[:, p * part : (p + 1) * part]
+        s_part[p, 1:2, :] = g_s_gate[:, p * part : (p + 1) * part]
+    s_send[...] = s_part[1 - dp]
+    s_copy = to(twin, x_sems, 5, s_send, s_got)
+    for chunk in range(4):
+        lanes = pl.ds(chunk * quarter, quarter)
+        grads = dot_tn(inner_all[...], g_mlp_all[:, :, lanes].reshape(length, quarter))
+        for p in (0, 1):
+            place = slice(p * width + chunk * quarter, p * width + (chunk + 1) * quarter)
+            up_raw[:, place] = grads[p * part : (p + 1) * part]
+    down_other = pl.ds(pl.multiple_of((1 - dp) * width, width), width)
+    down_mine = pl.ds(pl.multiple_of(dp * width, width), width)
+    down_send[...] = up_raw[:, down_other].astype(low)
+    down_copy = to(twin, x_sems, 6, down_send, down_got)
+
+    qkv_copy.wait()
+    per_chunk = quarter // rows_out
+    total = (qkv_part[...] + qkv_got[...].astype(f32)).astype(low)
+    for k in range(GROUP):
+        qkv_blocks.block(k)[...] = total[k * rows_out : (k + 1) * rows_out]
+    qkv_swap.start()
+    for copy in side_copies:
+        copy.wait()
+    out_copies = []
+    for k in (0, 1):
+        mine = pl.ds(pl.multiple_of(y * half, half), half)
+        total = (out_own[k][mine, :] + out_side_got[k].astype(f32)).astype(low)
+        out_line[2 * rows_out * k : 2 * rows_out * (k + 1), :] = total
+        for core in (0, 1):
+            line_rows = pl.ds((2 * k + core) * rows_out, rows_out)
+            target = (2 * c + k) * 4 + 2 * y + core
+            index = 2 * k + core
+            copy = remote(
+                out_line.at[line_rows],
+                out_in.at[z],
+                out_sems.at[0, index],
+                out_sems.at[1, z],
+                (dp, target),
+            )
+            out_copies.append((target, copy))
+
+            @pl.when(target != b)
+            def _():
+                copy.start()
+
+            @pl.when(target == b)
+            def _():
+                out_in[z] = out_line[line_rows, :]
+
+    def wide_copy(target):
+        return remote(
+            wide_blocks.block(target),
+            wide_in.at[b],
+            wide_sems.at[0, target],
+            wide_sems.at[1, b],
+            (dp, target),
+        )
+
+    for i in (0, 1):
+        wide_own[...] = wide_chunk(2 * dp + i)
+        wide_copies[i].wait()
+        total = (wide_own[...] + wide_got[i].astype(f32)).astype(low)
+        for k in range(per_chunk):
+            target = i * per_chunk + k
+            wide_blocks.block(target)[...] = total[k * rows_out : (k + 1) * rows_out]
+
+            @pl.when(target != b)
+            def _():
+                wide_copy(target).start()
+
+            @pl.when(target == b)
+            def _():
+                wide_in[b] = wide_blocks.block(target)[...]
+
+    for copy in load_qkv:
+        copy.wait()
+    back_swap.wait()
+    for pair in range(GROUP // 2):
+        for i in range(3):
+            lanes = slice(128 * i, 128 * (i + 1))
+            even = back_in[2 * pair, :, lanes].astype(f32)
+            odd = back_in[2 * pair + 1, :, lanes].astype(f32)
+            place = slice(128 * pair, 128 * (pair + 1))
+            home[i][:half, place] = jnp.where(first, even, pltpu.roll(odd, HEAD_DIM, 1)).astype(low)
+            home[i][half:, place] = jnp.where(first, pltpu.roll(even, HEAD_DIM, 1), odd).astype(low)
+    input_grad_ref[...] = (
+        g_res[...]
+        + dot_nt(home[0][...], w_qkv[0][...])
+        + dot_nt(home[1][...], w_qkv[1][...])
+        + dot_nt(home[2][...], w_qkv[2][...])
+    )
+    s_copy.wait()
+    g_s_ref[...] = s_part[dp] + s_got[...]
+    down_copy.wait()
+    g_down_ref[...] = up_raw[:, down_mine] + down_got[...].astype(f32)
+    small_swap.wait()
+    small_all[b] = small_own[...]
+    small_ref[...] = jnp.sum(small_all[...], axis=0)
+    small_ref[17:18, :] = small_all[8 * dp + b // 2, 16:17, :]
+    qkv_swap.wait()
+    for target, copy in out_copies:
+
+        @pl.when(target != b)
+        def _():
+            copy.wait_send()
+
+    for source_z in range(4):
+        source = source_z * 4 + 2 * y + z // 2
+
+        @pl.when(source != b)
+        def _():
+            remote(
+                out_line.at[pl.ds(0, rows_out)],
+                out_in.at[source_z],
+                out_sems.at[0, 0],
+                out_sems.at[1, source_z],
+                sib,
+            ).wait_recv()
+
+    for other in range(GROUP):
+
+        @pl.when(other != b)
+        def _():
+            copy = remote(
+                wide_blocks.block(other),
+                wide_in.at[other],
+                wide_sems.at[0, other],
+                wide_sems.at[1, other],
+                sib,
+            )
+            copy.wait_send()
+            copy.wait_recv()
+
+
+def tail_block(vmem_inputs, hbm_inputs):
+    low, f32 = jnp.bfloat16, jnp.float32
+    shape, vmem, sems = jax.ShapeDtypeStruct, pltpu.VMEM, pltpu.SemaphoreType.DMA
+    packed, hidden = vmem_inputs[1], vmem_inputs[2]
+    w_out, w_up, w_gate, w_down = hbm_inputs[:4]
+    rows, width = hidden.shape
+    half = rows // 2
+    ff = w_up.shape[1]
+    length = GROUP * rows
+    rows_out = width // (2 * GROUP)
+    part = ff // (2 * GROUP)
+    quarter = width // 4
+    return pl.pallas_call(
+        tail_kernel,
+        out_shape=[
+            shape((rows, width), low),
+            shape((rows, width), f32),
+            shape((GROUP, rows_out, 4 * part), low),
+            shape((GROUP, rows_out, 256), low),
+            shape((part, width), f32),
+            shape((4, rows_out, width), low),
+            shape((8, 128), f32),
+            shape((24, 128), f32),
+        ],
+        in_specs=[SMEM_SPEC]
+        + [VMEM_SPEC] * (len(vmem_inputs) - 1)
+        + [ANY_SPEC] * len(hbm_inputs),
+        out_specs=[VMEM_SPEC] * 8,
+        scratch_shapes=[
+            vmem((2 * GROUP, half, width), low),
+            vmem((2 * GROUP, half, width), low),
+            vmem(w_out.shape, low),
+            vmem(w_up.shape, low),
+            vmem(w_gate.shape, low),
+            vmem(w_down.shape, low),
+            vmem((width, 2 * part), low),
+            vmem((width, 2 * part), low),
+            vmem((2 * part, width), low),
+            vmem((rows, ff), f32),
+            vmem((rows, ff), f32),
+            vmem((2, half, width), low),
+            vmem((2, half, width), low),
+            vmem(packed.shape, low),
+            vmem(packed.shape, low),
+            vmem(packed.shape, low),
+            vmem((rows, width), f32),
+            vmem((rows, width), f32),
+            vmem((2, rows, width), low),
+            vmem((2, rows, width), low),
+            vmem((quarter, width), low),
+            vmem((2, half, width), low),
+            vmem((length, 128), low),
+            vmem((length, 128), low),
+            vmem((length, 128), low),
+            vmem((length, 128), low),
+            vmem((length, 128), f32),
+            vmem((KEYS, 128), f32),
+            vmem((KEYS, 128), f32),
+            vmem((GROUP, half, 384), low),
+            vmem((2 * quarter, 256), f32),
+            vmem((2 * quarter, 256), low),
+            vmem((quarter, 4 * part), f32),
+            vmem((2, quarter, 4 * part), low),
+            vmem((part, width), low),
+            vmem((24, 128), f32),
+            vmem((24, 128), f32),
+            vmem((GROUP, 24, 128), f32),
+            vmem((2, 8, 128), f32),
+            vmem((8, 128), f32),
+            vmem((8, 128), f32),
+            sems((24,)),
+            sems((2, 8)),
+            sems((2, 4)),
+            sems((2, 4)),
+            sems((2, GROUP)),
+            sems((2, GROUP)),
+            sems((2, GROUP)),
+            sems((2, GROUP)),
+            sems((2, GROUP)),
+            sems((2, GROUP)),
+        ]
+        + gather_scratch(TAIL_PIECES)
+        + gather_scratch(TAIL_PIECES),
+        compiler_params=comm_params(1),
+        name="tail_block",
+    )(*vmem_inputs, *hbm_inputs)
+
+
+def assemble_kernel(
+    result,
+    input_grad,
+    wide_in,
+    qkv_in,
+    down,
+    out_in,
+    small,
+    output_ref,
+    input_grad_ref,
+    g_query_ref,
+    g_key_ref,
+    g_value_ref,
+    g_out_ref,
+    g_up_ref,
+    g_gate_ref,
+    g_down_ref,
+    small_ref,
+):
+    f32 = jnp.float32
+    output_ref[...] = result[...]
+    input_grad_ref[...] = input_grad[...]
+    g_down_ref[...] = down[...]
+    small_ref[...] = small[...]
+    g_out_ref[...] = sum(out_in[i].astype(f32) for i in range(4))
+    part = wide_in.shape[2] // 4
+    ff_half = g_up_ref.shape[1] // 2
+    for j in range(GROUP):
+        for p in (0, 1):
+            place = slice(p * ff_half + j * part, p * ff_half + (j + 1) * part)
+            g_up_ref[:, place] = wide_in[j, :, p * part : (p + 1) * part].astype(f32)
+            g_gate_ref[:, place] = wide_in[j, :, (2 + p) * part : (3 + p) * part].astype(f32)
+    first = half_lanes((g_query_ref.shape[0], 128))
+    for pair in range(GROUP // 2):
+        place = slice(128 * pair, 128 * (pair + 1))
+        even, odd = qkv_in[2 * pair].astype(f32), qkv_in[2 * pair + 1].astype(f32)
+        even_qk, odd_qk = even[:, :128], odd[:, :128]
+        g_query_ref[:, place] = jnp.where(first, even_qk, pltpu.roll(odd_qk, HEAD_DIM, 1))
+        g_key_ref[:, place] = jnp.where(first, pltpu.roll(even_qk, HEAD_DIM, 1), odd_qk)
+        g_value_ref[:, place] = jnp.where(
+            first, even[:, 128:], pltpu.roll(odd[:, 128:], HEAD_DIM, 1)
+        )
+
+
+def assemble_block(inputs, ff):
+    result, input_grad, wide_in, qkv_in, down, out_in, small = inputs
+    f32 = jnp.float32
+    shape = jax.ShapeDtypeStruct
+    width = result.shape[1]
+    rows_out = wide_in.shape[1]
+    return pl.pallas_call(
+        assemble_kernel,
+        out_shape=[
+            shape(result.shape, result.dtype),
+            shape(input_grad.shape, f32),
+            shape((rows_out, width), f32),
+            shape((rows_out, width), f32),
+            shape((rows_out, width), f32),
+            shape((rows_out, width), f32),
+            shape((rows_out, ff), f32),
+            shape((rows_out, ff), f32),
+            shape(down.shape, f32),
+            shape(small.shape, f32),
+        ],
+        in_specs=[VMEM_SPEC] * 7,
+        out_specs=[VMEM_SPEC] * 10,
+        compiler_params=pltpu.CompilerParams(vmem_limit_bytes=VMEM_LIMIT),
+        name="assemble_block",
+    )(*inputs)
+
+
+def on_device_heads(
+    tokens,
+    cotangent,
+    lengths,
+    w_query,
+    w_key,
+    w_value,
+    w_out,
+    w_up,
+    w_gate,
+    w_down,
+    s_qk,
+    s_up,
+    s_gate,
+    alpha_attn,
+    alpha_mlp,
+):
+    model_width = w_query.shape[0]
+    tok_rows = tokens.shape[2]
+    half_rows = tok_rows // 2
+    hidden = tokens[0, 0]
+    hidden_all, qa, ka, va, query_raw, key_raw, gain = project_block(
+        hidden, w_query, w_key, w_value, s_qk
+    )
+    attended, ql, packed = attend(lengths, qa, ka, va, half_rows)
+    (result, input_grad, wide_in, qkv_in, grad_down, out_in, grad_scales, small) = tail_block(
+        (
+            lengths,
+            packed,
+            hidden,
+            cotangent[0, 0],
+            gain,
+            s_up[None],
+            s_gate[None],
+            alpha_attn[None],
+            alpha_mlp[None],
+        ),
+        (
+            w_out,
+            w_up,
+            w_gate,
+            w_down,
+            w_query,
+            w_key,
+            w_value,
+            ql,
+            ka,
+            va,
+            attended,
+            query_raw,
+            key_raw,
+            hidden_all.reshape(GROUP * tok_rows, model_width),
+        ),
+    )
+    (
+        output,
+        input_grad,
+        grad_query,
+        grad_key,
+        grad_value,
+        grad_out,
+        grad_up,
+        grad_gate,
+        grad_down,
+        small,
+    ) = assemble_block(
+        (result, input_grad, wide_in, qkv_in, grad_down, out_in, small), w_up.shape[1]
+    )
+    dp, b = here()
+    rows_out = model_width // (2 * GROUP)
+    first_row = (dp * GROUP + b) * rows_out
+    grad_attn, grad_mlp_alpha = (
+        lax.dynamic_slice_in_dim(small[8 * i : 8 * (i + 1)].reshape(-1), first_row, rows_out, 0)
+        for i in (0, 1)
+    )
+    grad_gain = lax.dynamic_slice_in_dim(small[17], (b % 2) * rows_out, rows_out, 0)
+    mean_alpha = 0.5 * (jnp.mean(alpha_attn) + jnp.mean(alpha_mlp))
+    return (
+        output[None, None],
+        input_grad[None, None],
+        grad_query,
+        grad_key,
+        grad_value,
+        grad_out,
+        grad_up,
+        grad_gate,
+        grad_down,
+        grad_gain,
+        grad_scales[0],
+        grad_scales[1],
+        grad_attn,
+        grad_mlp_alpha,
+        mean_alpha,
+    )
+
+
+def on_device(*arrays):
+    head_count = arrays[3].shape[0] // HEAD_DIM
+    tok_rows = arrays[0].shape[2]
+    fits = lax.axis_size("blk") == head_count == 16 and lax.axis_size("dp") == 2
+    if fits and tok_rows == 128:
+        return on_device_heads(*arrays)
+    return on_device_general(*arrays)
+
+
 def solution(mesh):
     in_specs = (
         P("dp", "blk", None, None),

time: 1580 us -> 167 us (0.11)
  waiting for transfers between devices: 1180 us -> 0 us
  matrix products: 171 us -> 0 us
  Pallas kernels: 0 us -> 157 us
  local copies, waits for them, and re-layouts: 81.9 us -> 4.39 us
  other arithmetic: 48.9 us -> 1.26 us
  blocking collectives: 40.1 us -> 0 us
  loops' own time: 33.6 us -> 0 us
  between operations: 19.1 us -> 3.08 us
    reduce_scatter x5 -> x0, waiting for transfers between devices: 671 us -> none  [the longest x1 187 us: on_device(): lax.psum_scatter(grad_w_down, ('dp', 'blk'), scatter_dimension=0, tiled=T...]
    unnamed x13 -> x0, waiting for transfers between devices: 425 us -> none
    dot_general x49 -> x0, matrix products: 171 us -> none  [the longest x11 24.5 us: pair_terms(): jnp.einsum('qhd,khd->hqk', query_heads, key_heads, preferred_element_type...]
    pallas_call x0 -> x4, Pallas kernels: none -> 157 us  [the longest x1 109 us: tail_block(): pl.pallas_call(tail_kernel, out_shape=[shape((rows, width), low), shape((...]
    all_gather x2 -> x0, waiting for transfers between devices: 80.7 us -> none  [the longest x1 47.9 us: on_device(): key_part = lax.all_gather(key_rows, 'blk', axis=0, tiled=True)]
    unnamed x1 -> x0, blocking collectives: 40.1 us -> none
    unnamed x162 -> x4, local copies, waits for them, and re-layouts: 35 us -> 0.01 us
    another operation x37 -> x0, loops' own time: 33.6 us -> none  [the longest x1 32 us: on_device(): lax.scan(query_step, (zero_part, zero_part), jnp.arange(members, dtype=jn...]
  transfers between devices with their start and end apart: 10 -> 0, of which waited for: 10 -> 0; matrix products, arithmetic and copies ran while one was open for 10% -> 0% of each run, Pallas kernels for 0% -> 0%
where the time goes in v4:
time: 167 us; the launch traced here: 165 us
  Pallas kernels  157 us (94%)
  local copies, waits for them, and re-layouts  4.39 us (3%)
  between operations  3.08 us (2%)
    pallas_call x1, Pallas kernels, tail_block(): pl.pallas_call(tail_kernel, out_shape=[shape((rows, width), low), shape((...  109 us
    pallas_call x1, Pallas kernels, project_block(): pl.pallas_call(project_kernel, out_shape=[shape((2 * GROUP, rows // 2, wi...  36.6 us
    pallas_call x1, Pallas kernels, attend(): pl.pallas_call(attend_kernel, out_shape=[shape((length, 128), jnp.bfloat1...  7.39 us

profile of v4, /device:TPU:0, one launch (start us, length us, event | category | flops | bytes accessed | tf_op | source)
XLA Modules:
  0.0 165.3 jit_solution(11010008373762545354)
XLA Ops:
  0.6 36.6 %project_block.1 = (bf16[32,64,1024]{2,1,0:T(8,128)(2,1)}, bf16[2048,128]{1,0:T(8,128)(2,1)}, bf16[2048,128]{1,0:T(8,128)(2,1)}, bf16[2048,128]{1,0:T(8,128)(2,1...) custom-call(bf16[2,64,1024]{2,1,0:T(8,128)(2,1)} %bitcast.22, ...), custom_call_target="tpu_custom_call" | custom-call | tf_op jit(solution)/shard_map/project_block/pallas_call | solution.py:743
  37.2 7.4 %attend.1 = (bf16[2048,128]{1,0:T(8,128)(2,1)}, bf16[2048,128]{1,0:T(8,128)(2,1)}, bf16[16,64,128]{2,1,0:T(8,128)(2,1)}) custom-call(s32[1,2]{1,0:T(1,128)} %lengths_ref.3, bf16[2048,128]{1,0:T(8,128)(2,1)} %get-tuple-element.43.qa_ref, bf16[2048,128]{1,0:T(8,128)(2,1)} %get-tuple-element.44.ka_ref.ka_hbm, bf16[2048,128]{1,0:T(8,128)(2,1)} %get-tuple-element.45.va_ref.va_hbm), custom_call_target="tpu_custom_call" | custom-call | tf_op jit(solution)/shard_map/attend/pallas_call | solution.py:829
  44.6 0.0 copy-start
  44.6 0.0 copy-start.1
  44.6 109.4 %tail_block.1 = (bf16[128,1024]{1,0:T(8,128)(2,1)}, f32[128,1024]{1,0:T(8,128)}, bf16[16,32,512]{2,1,0:T(8,128)(2,1)}, bf16[16,32,256]{2,1,0:T(8,128)(2,1)}, f32...) custom-call(s32[1,2]{1,0:T(1,128)} %lengths_ref.3, ...), custom_call_target="tpu_custom_call" | custom-call | tf_op jit(solution)/shard_map/tail_block/pallas_call | solution.py:1458
  154.0 3.3 %assemble_block.1 = (bf16[128,1024]{1,0:T(8,128)(2,1)}, f32[128,1024]{1,0:T(8,128)}, f32[32,1024]{1,0:T(8,128)}, f32[32,1024]{1,0:T(8,128)}, f32[32,1024]{1,0:T(...) custom-call(bf16[128,1024]{1,0:T(8,128)(2,1)} %get-tuple-element.53., ...), custom_call_target="tpu_custom_call" | custom-call | tf_op jit(solution)/shard_map/assemble_block/pallas_call | solution.py:1584
  157.3 0.7 slice_bitcast_fusion
  158.0 0.6 dynamic_slice.14
  158.5 0.6 dynamic_slice.13
  159.1 0.7 slice.15
  159.8 0.6 dynamic-slice_bitcast_fusion
  160.4 1.3 slice_bitcast_fusion.2
  161.7 0.0 copy-done
  161.7 0.6 reduce_sum.18
  162.3 0.0 copy-done.1
  162.3 0.7 reduce_sum.19
Async XLA Ops:
  44.6 117.1 %copy-start = (f32[1024]{0:T(1024)S(1)}, f32[1024]{0:T(1024)}, u32[]{:S(2)}) copy-start(f32[1024]{0:T(1024)} %param.28) | copy-start | bytes 12292
  44.6 117.7 %copy-start.1 = (f32[1024]{0:T(1024)S(1)}, f32[1024]{0:T(1024)}, u32[]{:S(2)}) copy-start(f32[1024]{0:T(1024)} %param.29) | copy-start | bytes 12292
